TPU v7x, 32 devices: a whole 2x2x4 slice. The times are simulated.
32 devices in a mesh: dp: 4 (over y, x), context: 8 (over z, core).
Axes of the slice: x: 2, y: 2, z: 4, core: 2. Of those that a mesh axis runs over, the one named last changes fastest.
Arguments:
- query_rows: bfloat16 [4, 1536, 1024], P('dp', 'context'), may hold values from -40 to 40
- key_rows: bfloat16 [4, 1536, 128], P('dp', 'context'), may hold values from -12 to 12
- value_rows: bfloat16 [4, 1536, 128], P('dp', 'context'), may hold values from -6 to 6
- out_grads: bfloat16 [4, 1536, 1024], P('dp', 'context'), may hold values from -16 to 16
- layer_input: bfloat16 [4, 1536, 8192], P('dp', 'context'), may hold values from -6 to 6
- doc_ids: int32 [4, 1536], P('dp'), may hold values from 0 to 7, never falling along the last dimension, each value on 1 to 768 neighbouring positions
- pair_span: int32 [8], replicated, may hold values from 0 to 7, each once
Outputs:
- grad_qkv: bfloat16 [4, 1536, 1280], P('dp', 'context')
- grad_weight: float32 [8192, 1280], P(('dp', 'context'))
- amax_record: float32 [4, 8, 2], P('dp', 'context')
Inputs may be any that keep to these rules, and one draw needn't show every extreme that they name: doc_ids[b] never falls along positions; each document holds 1 to 768 positions, one exactly 768. `pair_span`: each of 0 to 7 once.
All inputs are finite; a program needn't handle non-finite values.
Results may differ from a plain program's by a relative error of at most 0.0056.
Values may be sent and summed in bfloat16 or wider, within the bound.
No kernel may reach another device: no remote copies, remote signals or barrier semaphores. Data moves between devices by JAX's collectives and lax.ppermute only.
A program may use at most 64 MiB of HBM per device.

v0:
```python
import math

import jax
import jax.numpy as jnp
import numpy as np
from jax import lax
from jax.sharding import PartitionSpec as P

THETA_BASE = 500000.0
NEG_LARGE = -1e30


def rope_table(seq_len, head_dim):
    inverse_freq = THETA_BASE ** (-2.0 * np.arange(head_dim // 2) / head_dim)
    angles = np.arange(seq_len)[:, None] * inverse_freq[None, :]
    angles = np.concatenate([angles, angles], axis=1)
    return (np.cos(angles).astype(np.float32), np.sin(angles).astype(np.float32))


def stored_positions(pair_span, pairs, span_len):
    block_index = jnp.arange(2 * pairs, dtype=jnp.int32)
    owner_pair = pair_span[block_index // 2]
    span_index = jnp.where(block_index % 2 == 0, owner_pair, 2 * pairs - 1 - owner_pair)
    row_index = jnp.arange(2 * pairs * span_len, dtype=jnp.int32)
    return (span_index[row_index // span_len] * span_len + row_index % span_len, span_index)


def unrotate(grad_rows, cosine, sine_rows):
    half_dim = grad_rows.shape[-1] // 2
    turned = jnp.concatenate([-grad_rows[..., half_dim:], grad_rows[..., :half_dim]], axis=-1)
    return grad_rows * cosine - turned * sine_rows


def fold_rows(columns, weight_term, shard_rows):
    input_part = lax.slice_in_dim(columns, 0, shard_rows.shape[0], axis=0)
    return weight_term + lax.dot_general(
        input_part, shard_rows, (((0,), (0,)), ((), ())), preferred_element_type=jnp.float32
    )


def local(query_rows, key_rows, value_rows, out_grads, layer_input, doc_ids, pair_span):
    shards = lax.axis_size("context")
    replicas = lax.axis_size("dp")
    this_shard = lax.axis_index("context")
    tok_dev = query_rows.shape[1]
    head_dim = key_rows.shape[2]
    head_count = query_rows.shape[2] // head_dim
    model_width = layer_input.shape[2]
    span_len = tok_dev // 2
    seq_len = tok_dev * shards
    key_block = min(512, seq_len)
    block_count = seq_len // key_block
    score_scale = 1.0 / math.sqrt(head_dim)
    qkv_width = (head_count + 2) * head_dim
    positions, span_index = stored_positions(pair_span, shards, span_len)
    own_pos = lax.dynamic_slice_in_dim(positions, this_shard * tok_dev, tok_dev)
    seq_docs = doc_ids[0]
    own_docs = seq_docs[own_pos]
    span_ids = jnp.arange(2 * shards, dtype=jnp.int32)
    holder = (span_index[None, :] == span_ids[:, None]).astype(jnp.int32)
    inverse = jnp.sum(holder * span_ids[None, :], axis=1)
    out_local = jnp.max(jnp.abs(out_grads)).astype(jnp.float32)
    keys_all, values_all = (
        lax.all_gather(key_rows[0], "context", axis=0, tiled=True),
        lax.all_gather(value_rows[0], "context", axis=0, tiled=True),
    )
    keys_seq = keys_all.reshape(2 * shards, span_len, head_dim)[inverse].reshape(seq_len, head_dim)
    values_seq = values_all.reshape(2 * shards, span_len, head_dim)[inverse].reshape(
        seq_len, head_dim
    )
    queries = query_rows[0].reshape(tok_dev * head_count, head_dim)
    out_rows = out_grads[0].reshape(tok_dev * head_count, head_dim)

    def block_mask(block_start):
        key_pos = block_start + jnp.arange(key_block, dtype=jnp.int32)
        key_docs = lax.dynamic_slice_in_dim(seq_docs, block_start, key_block)
        return (key_pos[None, :] <= own_pos[:, None]) & (key_docs[None, :] == own_docs[:, None])

    def block_scores(block_start):
        key_part = lax.dynamic_slice_in_dim(keys_seq, block_start, key_block)
        value_part = lax.dynamic_slice_in_dim(values_seq, block_start, key_block)
        scores = jnp.dot(queries, key_part.T, preferred_element_type=jnp.float32) * score_scale
        dprobs = jnp.dot(out_rows, value_part.T, preferred_element_type=jnp.float32)
        return (
            key_part,
            scores.reshape(tok_dev, head_count, key_block),
            dprobs.reshape(tok_dev, head_count, key_block),
        )

    def stats_step(state_now, block_start):
        allowed = block_mask(block_start)[:, None, :]
        row_top, row_total, weighted = state_now
        key_part, scores, dprobs = block_scores(block_start)
        new_top = jnp.maximum(row_top, jnp.max(jnp.where(allowed, scores, NEG_LARGE), axis=2))
        factor = jnp.exp(row_top - new_top)
        expd = jnp.where(allowed, jnp.exp(scores - new_top[:, :, None]), 0.0)
        state_next = (
            new_top,
            row_total * factor + jnp.sum(expd, axis=2),
            weighted * factor + jnp.sum(expd * dprobs, axis=2),
        )
        return (state_next, None)

    block_starts = jnp.arange(block_count, dtype=jnp.int32) * key_block
    start_state = (
        jnp.full((tok_dev, head_count), NEG_LARGE, jnp.float32),
        jnp.zeros((tok_dev, head_count), jnp.float32),
        jnp.zeros((tok_dev, head_count), jnp.float32),
    )
    (row_top, row_total, weighted), unused = lax.scan(stats_step, start_state, block_starts)
    row_delta = weighted / row_total

    def grad_step(state_now, block_start):
        allowed = block_mask(block_start)[:, None, :]
        grad_q, ds_max = state_now
        key_part, scores, dprobs = block_scores(block_start)
        prob_rows = (
            jnp.where(allowed, jnp.exp(scores - row_top[:, :, None]), 0.0) / row_total[:, :, None]
        )
        dscores = prob_rows * (dprobs - row_delta[:, :, None])
        probs_low = prob_rows.astype(jnp.bfloat16).reshape(tok_dev * head_count, key_block)
        dscores_low = dscores.astype(jnp.bfloat16).reshape(tok_dev * head_count, key_block)
        grad_v = lax.dot_general(
            probs_low, out_rows, (((0,), (0,)), ((), ())), preferred_element_type=jnp.float32
        )
        grad_k = lax.dot_general(
            dscores_low, queries, (((0,), (0,)), ((), ())), preferred_element_type=jnp.float32
        )
        grad_q = grad_q + jnp.dot(dscores_low, key_part, preferred_element_type=jnp.float32)
        return ((grad_q, jnp.maximum(ds_max, jnp.max(jnp.abs(dscores)))), (grad_k, grad_v))

    grad_start = (
        jnp.zeros((tok_dev * head_count, head_dim), jnp.float32),
        jnp.zeros((), jnp.float32),
    )
    (grad_q, ds_max), (key_terms, value_terms) = lax.scan(grad_step, grad_start, block_starts)
    key_terms = key_terms.reshape(2 * shards, span_len, head_dim)[span_index].reshape(
        seq_len, head_dim
    )
    value_terms = value_terms.reshape(2 * shards, span_len, head_dim)[span_index].reshape(
        seq_len, head_dim
    )
    own_k, own_v = (
        lax.psum_scatter(key_terms, "context", scatter_dimension=0, tiled=True),
        lax.psum_scatter(value_terms, "context", scatter_dimension=0, tiled=True),
    )
    cos_tab, sin_tab = rope_table(seq_len, head_dim)
    cosine = jnp.asarray(cos_tab)[own_pos]
    sine_rows = jnp.asarray(sin_tab)[own_pos]
    query_grads = unrotate(
        grad_q.reshape(tok_dev, head_count, head_dim) * score_scale,
        cosine[:, None, :],
        sine_rows[:, None, :],
    )
    key_grads = unrotate(own_k * score_scale, cosine, sine_rows)
    grad_rows = jnp.concatenate(
        [query_grads.reshape(tok_dev, head_count * head_dim), key_grads, own_v], axis=1
    ).astype(jnp.bfloat16)
    out_max, ds_global = lax.pmax((out_local, ds_max), ("dp", "context"))
    amax_record = jnp.stack([out_max, ds_global]).reshape(1, 1, 2)
    slice_rows = model_width // (replicas * shards)
    inputs = layer_input[0].reshape(tok_dev, replicas, shards, slice_rows)
    columns = lax.all_to_all(inputs, "context", split_axis=2, concat_axis=0, tiled=True).reshape(
        shards * tok_dev, replicas * slice_rows
    )
    zero_term = jnp.zeros((replicas * slice_rows, qkv_width), jnp.float32)
    weight_term = fold_rows(
        columns, zero_term, lax.all_gather(grad_rows, "context", axis=0, tiled=True)
    )
    grad_weight = lax.psum_scatter(weight_term, "dp", scatter_dimension=0, tiled=True)
    return (grad_rows.reshape(1, tok_dev, qkv_width), grad_weight, amax_record)


def solution(mesh):
    in_specs = (
        P("dp", "context", None),
        P("dp", "context", None),
        P("dp", "context", None),
        P("dp", "context", None),
        P("dp", "context", None),
        P("dp", None),
        P(),
    )
    out_specs = (P("dp", "context", None), P(("dp", "context"), None), P("dp", "context", None))
    return jax.shard_map(local, mesh=mesh, in_specs=in_specs, out_specs=out_specs, check_vma=False)
```

profile of v0, /device:TPU:0, one launch (start us, length us, event | category | flops | bytes accessed | tf_op | source)
XLA Modules:
  0.0 437.2 jit_solution(713180459632359643)
XLA Ops:
  11.3 4.3 fusion.37
  15.6 3.2 select_select_fusion
  18.8 2.5 compare_select_fusion.7
  24.5 16.4 %all-gather = bf16[1,1536,128]{2,1,0:T(8,128)(2,1)S(1)} all-gather(bf16[1,192,128]{2,1,0:T(8,128)(2,1)} %param.14), channel_id=2, replica_groups=mesh['dp'=4,'context'=8] {'context'}, dimensions={1}, use_global_device_ids=true | all-gather | bytes 442368 | tf_op jit(solution)/shard_map/all_gather | solution.py:64
  40.9 14.6 %all-gather.1 = bf16[1,1536,128]{2,1,0:T(8,128)(2,1)S(1)} all-gather(bf16[1,192,128]{2,1,0:T(8,128)(2,1)} %param.15), channel_id=3, replica_groups=mesh['dp'=4,'context'=8] {'context'}, dimensions={1}, use_global_device_ids=true | all-gather | bytes 442368 | tf_op jit(solution)/shard_map/all_gather | solution.py:65
  60.2 69.7 %while.33 = (s32[]{:T(128)}, f32[192,8]{1,0:T(8,128)}, f32[192,8]{1,0:T(8,128)}, f32[192,8]{1,0:T(8,128)}, s32[3]{0:T(128)}, /*index=5*/s32[192]{0:T(256)S(1)}, ...) while((s32[]{:T(128)}, f32[192,8]{1,0:T(8,128)}, ...), condition=%wide.region_5.6_spmd.clone, body=%wide.region_1.5_spmd.clone.sunk | while | flops 410823680 | bytes 21890864 | solution.py:110
  67.4 2.3 select_reduce_fusion.3
  74.2 3.0 fusion.87
  90.5 2.3 select_reduce_fusion.3
  97.4 3.0 fusion.87
  120.6 3.0 fusion.87
  132.9 46.3 %while.34 = (s32[]{:T(128)}, f32[1536,128]{1,0:T(8,128)}, f32[]{:T(128)}, f32[3,512,128]{2,1,0:T(8,128)}, f32[3,512,128]{2,1,0:T(8,128)}, /*index=5*/s32[3]{0:T(...) while((s32[]{:T(128)}, f32[1536,128]{1,0:T(8,128)}, ...), condition=%wide.wide.region_8.9_spmd.clone, body=%wide.wide.region_6.8_spmd.clone.sunk | while | flops 1015185920 | bytes 29456260 | solution.py:136
  142.3 2.3 abs_reduce_fusion.4
  157.7 2.3 abs_reduce_fusion.4
  173.2 2.3 abs_reduce_fusion.4
  179.3 2.8 gather_fusion.6
  182.2 2.8 gather_fusion.7
  189.6 25.3 %reduce-scatter.4.cloned.1.call-done = f32[192,128]{1,0:T(8,128)} async-done(((f32[1536,128]{1,0:T(8,128)}), f32[192,128]{1,0:T(8,128)}) %reduce-scatter.4.cloned.1.call-update) | async-done | bytes 98320 | tf_op jit(solution)/shard_map/reduce_scatter | solution.py:144
  219.5 27.7 %reduce-scatter.6.cloned.1.call-done = f32[192,128]{1,0:T(8,128)} async-done(((f32[1536,128]{1,0:T(8,128)}), f32[192,128]{1,0:T(8,128)}) %reduce-scatter.6.cloned.1.call-update) | async-done | bytes 98320 | tf_op jit(solution)/shard_map/reduce_scatter | solution.py:145
  252.1 105.6 %all_to_all.15 = bf16[192,4,8,256]{3,1,0,2:T(4,128)(2,1)S(1)} all-to-all(bf16[192,4,8,256]{3,1,0,2:T(4,128)(2,1)S(1)} %copy.21), channel_id=1, replica_groups=mesh['dp'=4,'context'=8] {'context'}, dimensions={2} | all-to-all | bytes 6291456 | tf_op jit(solution)/shard_map/all_to_all | solution.py:163
  358.6 8.2 %convolution_bitcast_fusion.2 = f32[1024,1280]{0,1:T(8,128)} fusion(bf16[1536,1280]{1,0:T(8,128)(2,1)} %all-gather.4.cloned.1.call-done, bf16[1536,1024]{1,0:T(8,128)(2,1)S(1)} %bitcast.158), kind=kOutput, calls=%fused_computation.57 | convolution fusion | flops 4026531840 | bytes 12320768 | tf_op jit(solution)/shard_map/dot_general | solution.py:36
  368.4 39.6 %all-reduce = (f32[1]{0:T(128)}, f32[1]{0:T(128)}) all-reduce(f32[1]{0:T(128)} %bitcast.37, bf16[1]{0:T(256)(128)(2,1)} %bitcast.50), channel_id=1, replica_groups=mesh['dp'=4,'context'=8] {'dp','context'}, use_global_device_ids=true, to_apply=%region_14.15 | all-reduce | flops 2 | bytes 14 | tf_op jit(solution)/shard_map/pmax | solution.py:159
  410.7 17.2 %reduce-scatter.8.cloned.1.call-done = f32[256,1280]{0,1:T(8,128)} async-done(((f32[1024,1280]{0,1:T(8,128)}), f32[256,1280]{0,1:T(8,128)}) %reduce-scatter.8.cloned.1.call-update) | async-done | bytes 1310736 | tf_op jit(solution)/shard_map/reduce_scatter | solution.py:170
  427.9 2.8 copy.22
  (197 shorter events, 115.3 us)
Async XLA Ops:
  7.2 207.8 %reduce-scatter.4.cloned.1.call-start = ((), (), s32[]{:S(2)}) async-start(), calls=%async_computation.4 | async-start | bytes 884736 | tf_op jit(solution)/shard_map/reduce_scatter | solution.py:144
  21.4 38.8 %copy-start.15 = (s32[1024]{0:T(1024)}, s32[1024]{0:T(1024)S(1)}, u32[]{:S(2)}) copy-start(s32[1024]{0:T(1024)S(1)} %pad_clamp_fusion.2) | copy-start | bytes 12292
  74.2 3.0 copy-start.2
  74.2 3.0 copy-start.9
  97.3 3.0 copy-start.2
  97.4 3.0 copy-start.9
  120.6 3.0 copy-start.2
  120.6 3.0 copy-start.9
  139.0 2.0 copy-start.3
  142.3 2.9 copy-start.4
  154.4 2.0 copy-start.3
  157.7 2.9 copy-start.4
  169.8 2.0 copy-start.3
  173.2 2.9 copy-start.4
  179.3 5.8 %copy-start.6 = (f32[1536,128]{1,0:T(8,128)S(1)}, f32[1536,128]{1,0:T(8,128)}, u32[]{:S(2)}) copy-start(f32[1536,128]{1,0:T(8,128)} %get-tuple-element.155) | copy-start | bytes 2359300
  182.1 4.1 copy-start.11
  182.1 4.1 copy-start.16
  182.1 65.1 %reduce-scatter.6.cloned.1.call-start = ((), (), s32[]{:S(2)}) async-start(), calls=%async_computation.5 | async-start | bytes 884736 | tf_op jit(solution)/shard_map/reduce_scatter | solution.py:145
  182.2 4.7 %copy-start.10 = (f32[1536,128]{1,0:T(8,128)S(1)}, f32[1536,128]{1,0:T(8,128)}, u32[]{:S(2)}) copy-start(f32[1536,128]{1,0:T(8,128)} %constant.125.clone) | copy-start | bytes 2359300
  185.0 173.5 %all-gather.4.cloned.1.call-start = ((), (), s32[]{:S(2)}) async-start(), calls=%async_computation.6 | async-start | bytes 4423680 | tf_op jit(solution)/shard_map/all_gather | solution.py:168
  215.9 34.1 %copy-start.7 = (bf16[1,192,8192]{2,1,0:T(8,128)(2,1)S(1)}, bf16[1,192,8192]{2,1,0:T(8,128)(2,1)}, u32[]{:S(2)}) copy-start(bf16[1,192,8192]{2,1,0:T(8,128)(2,1)} %param.17) | copy-start | bytes 9437188
  249.7 178.1 %reduce-scatter.8.cloned.1.call-start = ((), (), s32[]{:S(2)}) async-start(), calls=%async_computation.7 | async-start | bytes 6553600 | tf_op jit(solution)/shard_map/reduce_scatter | solution.py:170
  366.8 43.1 %copy-start.13 = (f32[192,128]{1,0:T(8,128)S(1)}, f32[192,128]{1,0:T(8,128)}, u32[]{:S(2)}) copy-start(f32[192,128]{1,0:T(8,128)} %reduce-scatter.6.cloned.1.call-done) | copy-start | bytes 294916
  366.8 43.1 %copy-start.12 = (bf16[192,128]{1,0:T(8,128)(2,1)S(1)}, bf16[192,128]{1,0:T(8,128)(2,1)}, u32[]{:S(2)}) copy-start(bf16[192,128]{1,0:T(8,128)(2,1)} %get-tuple-element.327) | copy-start | bytes 147460
  (9 other events, 9.9 us)
Sparse Core Ops, SparseCore 0:
  182.2 32.6 reduce-scatter.3
  217.4 29.7 reduce-scatter.5
  249.8 90.0 all-gather.3
  366.9 60.9 reduce-scatter.7
where the time goes:
time: 440 us; the launch traced here: 437 us
  blocking collectives  176 us (40%)
  waiting for transfers between devices  70.3 us (16%)
  local copies, waits for them, and re-layouts  63.8 us (14%)
  matrix products  50.2 us (11%)
  other arithmetic  48.1 us (11%)
  loops' own time  14.3 us (3%)
  between operations  14.1 us (3%)
    all_to_all x1, blocking collectives, local(): lax.all_to_all(inputs, 'context', split_axis=2, concat_axis=0, tiled=True)  106 us
    pmax x1, blocking collectives, local(): out_max, ds_global = lax.pmax((out_local, ds_max), ('dp', 'context'))  39.6 us
    reduce_scatter x1, waiting for transfers between devices, local(): lax.psum_scatter(value_terms, 'context', scatter_dimension=0, tiled=True)  27.7 us
    reduce_scatter x1, waiting for transfers between devices, local(): lax.psum_scatter(key_terms, 'context', scatter_dimension=0, tiled=True)  25.3 us
    reduce_scatter x1, waiting for transfers between devices, local(): lax.psum_scatter(weight_term, 'dp', scatter_dimension=0, tiled=True)  17.2 us
    all_gather x1, blocking collectives, local(): lax.all_gather(key_rows[0], 'context', axis=0, tiled=True)  16.4 us
    dot_general x6, matrix products, block_scores(): dprobs = jnp.dot(out_rows, value_part.T, preferred_element_type=jnp.float32)  15.9 us
    all_gather x1, blocking collectives, local(): lax.all_gather(value_rows[0], 'context', axis=0, tiled=True)  14.6 us
  transfers between devices with their start and end apart: 4, of which 3 were waited for; matrix products, arithmetic and copies ran while one was open for 4% of the time, Pallas kernels for 0%

commit v1 on v0

v1 whole, which is shorter than its diff:
```python
import functools
import math

import jax
import jax.numpy as jnp
import numpy as np
from jax import lax
from jax.experimental import pallas as pl
from jax.experimental.pallas import tpu as pltpu
from jax.sharding import PartitionSpec as P

THETA_BASE = 500000.0
NEG_LARGE = -1e30
DOC_VALUES = 8
EXTRA = 16
F32 = jnp.float32
BF16 = jnp.bfloat16
VMEM = pl.BlockSpec(memory_space=pltpu.VMEM)
SMEM = pl.BlockSpec(memory_space=pltpu.SMEM)
ANY = pl.BlockSpec(memory_space=pl.ANY)


def rope_tables(seq_len, head_dim):
    inverse_freq = THETA_BASE ** (-2.0 * np.arange(head_dim // 2) / head_dim)
    angles = np.arange(seq_len)[:, None] * inverse_freq[None, :]
    angles = np.concatenate([angles, angles], axis=1)
    sign = np.where(np.arange(head_dim) < head_dim // 2, 1.0, -1.0)
    return np.concatenate(
        [np.cos(angles).astype(np.float32), (np.sin(angles) * sign).astype(np.float32)], axis=1
    )


def unrotate(rows, cosine, signed_sine):
    return rows * cosine + pltpu.roll(rows, rows.shape[-1] // 2, 1) * signed_sine


def span_of(pair, half, shards):
    return pair if half == 0 else 2 * shards - 1 - pair


def spread_max(out_max, ds_max, width):
    high = ds_max.astype(BF16).astype(F32)
    middle = (ds_max - high).astype(BF16).astype(F32)
    low = ds_max - high - middle
    row = lax.broadcasted_iota(jnp.int32, (EXTRA, width), 0)
    return jnp.where(
        row == 0,
        out_max,
        jnp.where(row == 1, high, jnp.where(row == 2, middle, jnp.where(row == 3, low, 0.0))),
    )


def read_max(rows):
    wide = rows.astype(F32)
    return wide[0:1], wide[1:2] + wide[2:3] + wide[3:4]


def attend_kernel(shards, heads, pair_ref, docs_ref, rope, q_cats, g_cats, *refs):
    pieces = refs[:shards]
    (gq_ref, keep_ref, send_ref, keys, values, score_buf, dprob_buf, dq_acc, dk_acc, dv_acc, order) = refs[shards:]
    lanes, head_dim = q_cats.shape[1:]
    span_len = lanes // heads
    tok_dev = 2 * span_len
    scale = 1.0 / math.sqrt(head_dim)
    me = lax.axis_index("context")
    pair = pair_ref[me]
    for index in range(shards):
        rows = pl.ds(index * tok_dev, tok_dev)
        keys[rows] = pieces[index][:, :head_dim]
        values[rows] = pieces[index][:, head_dim:]
    dk_acc[...] = jnp.zeros_like(dk_acc)
    dv_acc[...] = jnp.zeros_like(dv_acc)
    docs = docs_ref[...]
    starts = [jnp.sum(jnp.where(docs < value, 1.0, 0.0)) for value in range(1, DOC_VALUES)]
    out_max = jnp.max(jnp.abs(g_cats[...].astype(F32)))
    ds_top = jnp.zeros((1, lanes), F32)
    lane = lax.broadcasted_iota(jnp.int32, (1, lanes), 1)
    lane_row = lane % span_len
    sub = lax.broadcasted_iota(jnp.int32, (span_len, 1), 0)

    for half in range(2):
        span = span_of(pair, half, shards)
        base = span * span_len
        base_f = base.astype(F32)
        first_start = jnp.float32(0.0)
        for start in starts:
            first_start = jnp.maximum(first_start, jnp.where(start <= base_f, start, 0.0))
        first_key = first_start.astype(jnp.int32)

        def listing(block, count):
            other = pair_ref[me ^ (block // 2)]
            key_span = jnp.where(block % 2 == 0, other, 2 * shards - 1 - other)
            order[0, count] = block
            order[1, count] = key_span
            needed = (key_span <= span) & (key_span * span_len + span_len > first_key)
            return count + needed.astype(jnp.int32)

        count = lax.fori_loop(0, 2 * shards, listing, jnp.int32(0))
        query_pos = base + lane_row
        query_f = query_pos.astype(F32)
        doc_start = jnp.zeros((1, lanes), F32)
        for start in starts:
            doc_start = jnp.maximum(doc_start, jnp.where(start <= query_f, start, 0.0))
        doc_first = doc_start.astype(jnp.int32)
        own = pl.ds(half * span_len, span_len)
        q_cat, g_cat = q_cats.at[half], g_cats.at[half]

        def score_step(index, top):
            block = order[0, index]
            key_pos = order[1, index] * span_len + sub
            rows = pl.ds(pl.multiple_of(block * span_len, span_len), span_len)
            scores = lax.dot_general(
                keys[rows], q_cat[...], (((1,), (1,)), ((), ())), preferred_element_type=F32
            )
            allowed = (key_pos <= query_pos) & (key_pos >= doc_first)
            scores = jnp.where(allowed, scores, NEG_LARGE)
            score_buf[index] = scores
            dprob_buf[index] = lax.dot_general(
                values[rows], g_cat[...], (((1,), (1,)), ((), ())), preferred_element_type=F32
            )
            return jnp.maximum(top, jnp.max(scores, axis=0, keepdims=True))

        top = lax.fori_loop(0, count, score_step, jnp.full((1, lanes), NEG_LARGE, F32))

        def exp_step(index, sums):
            total, weighted = sums
            expd = jnp.exp((score_buf[index] - top) * scale)
            score_buf[index] = expd
            return (
                total + jnp.sum(expd, axis=0, keepdims=True),
                weighted + jnp.sum(expd * dprob_buf[index], axis=0, keepdims=True),
            )

        zero_row = jnp.zeros((1, lanes), F32)
        total, weighted = lax.fori_loop(0, count, exp_step, (zero_row, zero_row))
        inverse = 1.0 / total
        delta = weighted * inverse
        dq_acc[...] = jnp.zeros_like(dq_acc)

        def grad_step(index, ds_now):
            block = order[0, index]
            rows = pl.ds(pl.multiple_of(block * span_len, span_len), span_len)
            probs = score_buf[index] * inverse
            dscores = probs * (dprob_buf[index] - delta)
            probs_low = probs.astype(BF16)
            ds_low = dscores.astype(BF16)
            dv_acc[rows] += jnp.dot(probs_low, g_cat[...], preferred_element_type=F32)
            dk_acc[rows] += jnp.dot(ds_low, q_cat[...], preferred_element_type=F32)
            dq_acc[...] += lax.dot_general(
                keys[rows], ds_low, (((0,), (0,)), ((), ())), preferred_element_type=F32
            )
            return jnp.maximum(ds_now, jnp.max(jnp.abs(dscores), axis=0, keepdims=True))

        ds_top = lax.fori_loop(0, count, grad_step, ds_top)
        cosine = rope[half, :, :head_dim]
        signed_sine = rope[half, :, head_dim:]
        grad_q = dq_acc[...].T * scale
        for head in range(heads):
            part = grad_q[head * span_len : (head + 1) * span_len]
            gq_ref[own, pl.ds(head * head_dim, head_dim)] = unrotate(part, cosine, signed_sine).astype(BF16)

    ds_max = jnp.max(ds_top)
    extra = spread_max(out_max, ds_max, 2 * head_dim)
    row = lax.broadcasted_iota(jnp.int32, (EXTRA, 2 * head_dim), 0)
    plain = jnp.where(row == 0, out_max, jnp.where(row == 1, ds_max, 0.0))
    for index in range(shards):
        rows = pl.ds(index * tok_dev, tok_dev)
        target = (keep_ref, send_ref)[index % 2]
        kind = target.dtype
        target[index // 2, :tok_dev, :head_dim] = dk_acc[rows].astype(kind)
        target[index // 2, :tok_dev, head_dim:] = dv_acc[rows].astype(kind)
        target[index // 2, tok_dev:] = (extra if index % 2 else plain).astype(kind)


def merge_kernel(keep_ref, got_ref, own_ref, *send_refs):
    tok_dev = keep_ref.shape[1] - EXTRA
    width = keep_ref.shape[2]
    out_max, ds_max = read_max(got_ref[0, tok_dev:])
    out_max = jnp.maximum(out_max, keep_ref[0, tok_dev : tok_dev + 1])
    ds_max = jnp.maximum(ds_max, keep_ref[0, tok_dev + 1 : tok_dev + 2])
    extra = spread_max(out_max, ds_max, width)
    for index in range(keep_ref.shape[0]):
        both = keep_ref[index, :tok_dev] + got_ref[index, :tok_dev].astype(F32)
        target = own_ref if index == 0 else send_refs[index - 1]
        target[:tok_dev] = both.astype(target.dtype)
        target[tok_dev:] = extra.astype(target.dtype)


def finish_kernel(rope, gq_ref, own_ref, *refs):
    got_refs, (rows_ref, gkv_ref) = refs[:-2], refs[-2:]
    tok_dev = gq_ref.shape[0]
    head_dim = own_ref.shape[1] // 2
    total = own_ref[:tok_dev]
    out_max, ds_max = read_max(own_ref[tok_dev:])
    for got_ref in got_refs:
        total = total + got_ref[:tok_dev].astype(F32)
        other_out, other_ds = read_max(got_ref[tok_dev:])
        out_max = jnp.maximum(out_max, other_out)
        ds_max = jnp.maximum(ds_max, other_ds)
    wide = rope[...].reshape(tok_dev, 2 * head_dim)
    grad_k = unrotate(
        total[:, :head_dim] * (1.0 / math.sqrt(head_dim)), wide[:, :head_dim], wide[:, head_dim:]
    ).astype(BF16)
    grad_v = total[:, head_dim:].astype(BF16)
    gkv_ref[:tok_dev, :head_dim] = grad_k
    gkv_ref[:tok_dev, head_dim:] = grad_v
    gkv_ref[tok_dev:] = spread_max(out_max, ds_max, 2 * head_dim).astype(BF16)
    width = gq_ref.shape[1]
    rows_ref[:, :width] = gq_ref[...]
    rows_ref[:, width : width + head_dim] = grad_k
    rows_ref[:, width + head_dim :] = grad_v


def partial_kernel(count, first, tile, adds, *refs):
    xs, gs = refs[:count], refs[count : 2 * count]
    rest = refs[2 * count :]
    got_ref, outs = (rest[0], rest[1:]) if adds else (None, rest)
    blocks = len(outs) if adds else outs[0].shape[0] // tile
    tok_dev = xs[0].shape[0]
    for block in range(blocks):
        cols = slice(first + block * tile, first + (block + 1) * tile)
        total = None
        for x_ref, g_ref in zip(xs, gs):
            term = lax.dot_general(
                x_ref[:, cols], g_ref[:tok_dev], (((0,), (0,)), ((), ())), preferred_element_type=F32
            )
            total = term if total is None else total + term
        rows = slice(block * tile, (block + 1) * tile)
        if adds:
            total = total + got_ref[rows].astype(F32)
            outs[block][...] = total.astype(outs[block].dtype)
        else:
            outs[0][rows] = total.astype(outs[0].dtype)


def total_kernel(groups, places, *refs):
    out_ref, amax_ref = refs[-2:]
    used = 0
    for group, (rows, cols) in zip(groups, places):
        total = refs[used][...]
        for ref in refs[used + 1 : used + group]:
            total = total + ref[...].astype(F32)
        used += group
        out_ref[rows, cols] = total
    out_max, ds_max = None, None
    for ref in refs[used:-2]:
        tok_dev = ref.shape[0] - EXTRA
        other_out, other_ds = read_max(ref[tok_dev:])
        out_max = other_out if out_max is None else jnp.maximum(out_max, other_out)
        ds_max = other_ds if ds_max is None else jnp.maximum(ds_max, other_ds)
    lane = lax.broadcasted_iota(jnp.int32, (1, 2), 1)
    amax_ref[0] = jnp.where(lane == 0, out_max[:, :2], ds_max[:, :2])


def prepare_kernel(replicas, shards, order, tile, pair_ref, table_ref, q_ref, g_ref, *refs):
    rope_sems = refs[-1]
    rope_ref, q_cat, g_cat = refs[-4:-1]
    tok_dev = q_ref.shape[0]
    span_len = tok_dev // 2
    head_dim = q_cat.shape[2]
    rep, me = lax.axis_index("dp"), lax.axis_index("context")
    copies = []
    for half in range(2):
        start = pl.multiple_of(span_of(pair_ref[me], half, shards) * span_len, 8)
        copy = pltpu.make_async_copy(table_ref.at[pl.ds(start, span_len)], rope_ref.at[half], rope_sems.at[half])
        copy.start()
        copies.append(copy)
    if len(refs) > 4:
        x_ref, outs = refs[0], refs[1:-4]
        for half in range(2):
            for step in range(replicas):
                for place, relative in enumerate(order):
                    source = (((rep ^ step) * shards + (me ^ relative)) * 2 + half) * tile
                    outs[half * replicas + step][:, place * tile : (place + 1) * tile] = x_ref[
                        :, pl.ds(pl.multiple_of(source, tile), tile)
                    ]
    for half in range(2):
        own = slice(half * span_len, (half + 1) * span_len)
        for head in range(q_ref.shape[1] // head_dim):
            rows = slice(head * span_len, (head + 1) * span_len)
            cols = slice(head * head_dim, (head + 1) * head_dim)
            q_cat[half, rows] = q_ref[own, cols]
            g_cat[half, rows] = g_ref[own, cols]
    for copy in copies:
        copy.wait()


def params(mebibytes):
    return pltpu.CompilerParams(vmem_limit_bytes=mebibytes << 20)


def cost(microseconds):
    return pl.CostEstimate(flops=int(microseconds * 1.0e9), bytes_accessed=0, transcendentals=0)


def local(query_rows, key_rows, value_rows, out_grads, layer_input, doc_ids, pair_span):
    shards = lax.axis_size("context")
    replicas = lax.axis_size("dp")
    tok_dev = query_rows.shape[1]
    head_dim = key_rows.shape[2]
    width = query_rows.shape[2]
    heads = width // head_dim
    model_width = layer_input.shape[2]
    span_len = tok_dev // 2
    seq_len = tok_dev * shards
    qkv_width = width + 2 * head_dim
    lanes = heads * span_len
    slice_rows = model_width // (replicas * shards)
    tile = slice_rows // 2
    table = jnp.asarray(rope_tables(seq_len, head_dim))
    order = list(range(1, shards, 2)) + list(range(0, shards, 2))

    def context_move(x, step):
        return lax.ppermute(x, "context", [(i, i ^ step) for i in range(shards)])

    def dp_move(x, step):
        return lax.ppermute(x, "dp", [(i, i ^ step) for i in range(replicas)])

    def struct(shape, kind=BF16):
        return jax.ShapeDtypeStruct(shape, kind)

    own_kv = jnp.concatenate([key_rows[0], value_rows[0]], axis=1)
    pieces = [None] * shards
    pieces[0] = own_kv
    for step in range(2, shards, 2):
        pieces[step] = context_move(own_kv, step)
    for step in range(0, shards, 2):
        pieces[step + 1] = context_move(pieces[step], 1)

    x_local = layer_input[0]
    rope_shape = (2, span_len, 2 * head_dim)
    cat_shape = (2, lanes, head_dim)
    prepared = pl.pallas_call(
        functools.partial(prepare_kernel, replicas, shards, order, tile),
        out_shape=[struct((tok_dev, shards * tile))] * (2 * replicas if tile % 128 == 0 else 0)
        + [struct(rope_shape, F32), struct(cat_shape), struct(cat_shape)],
        in_specs=[SMEM, ANY, VMEM, VMEM] + [VMEM] * (tile % 128 == 0),
        out_specs=[VMEM] * (3 + (2 * replicas if tile % 128 == 0 else 0)),
        scratch_shapes=[pltpu.SemaphoreType.DMA((2,))],
        compiler_params=params(40),
        cost_estimate=cost(4),
        name="prepare",
    )(pair_span, table, query_rows[0], out_grads[0], *([x_local] if tile % 128 == 0 else []))
    packed = prepared[:-3]
    rope, q_cats, g_cats = prepared[-3:]
    if tile % 128:
        me, rep = lax.axis_index("context"), lax.axis_index("dp")
        parts = []
        for step in range(replicas):
            part = lax.dynamic_slice_in_dim(x_local, (rep ^ step) * shards * slice_rows, shards * slice_rows, 1)
            part = part.reshape(tok_dev, shards, 2, tile)
            parts.append(jnp.take(part, jnp.asarray(order, jnp.int32) ^ me, axis=1))
        packed = [part[:, :, half].reshape(tok_dev, shards * tile) for half in range(2) for part in parts]
    x_halves = [list(packed[:replicas]), list(packed[replicas:])]
    x_halves[0][1:] = [dp_move(x_halves[0][step], step) for step in range(1, replicas)]

    buf = (2 * shards, span_len, lanes)
    grad_q, keep, send = pl.pallas_call(
        functools.partial(attend_kernel, shards, heads),
        out_shape=[
            struct((tok_dev, width)),
            struct((shards // 2, tok_dev + EXTRA, 2 * head_dim), F32),
            struct((shards // 2, tok_dev + EXTRA, 2 * head_dim)),
        ],
        in_specs=[SMEM, VMEM, VMEM, VMEM, VMEM] + [VMEM] * shards,
        out_specs=[VMEM] * 3,
        scratch_shapes=[
            pltpu.VMEM((seq_len, head_dim), BF16),
            pltpu.VMEM((seq_len, head_dim), BF16),
            pltpu.VMEM(buf, F32),
            pltpu.VMEM(buf, F32),
            pltpu.VMEM((head_dim, lanes), F32),
            pltpu.VMEM((seq_len, head_dim), F32),
            pltpu.VMEM((seq_len, head_dim), F32),
            pltpu.SMEM((2, 2 * shards + 1), jnp.int32),
        ],
        compiler_params=params(48),
        cost_estimate=cost(12),
        name="attend",
    )(pair_span, doc_ids, rope, q_cats, g_cats, *pieces)

    gq = [grad_q] + [dp_move(grad_q, step) for step in range(1, replicas)]

    got = context_move(send, 1)
    block = (tok_dev + EXTRA, 2 * head_dim)
    merged = pl.pallas_call(
        merge_kernel,
        out_shape=[struct(block, F32)] + [struct(block)] * (shards // 2 - 1),
        in_specs=[VMEM] * 2,
        out_specs=[VMEM] * (shards // 2),
        cost_estimate=cost(2),
        name="merge_cores",
    )(keep, got)
    others = [context_move(merged[step // 2], step) for step in range(2, shards, 2)]
    grad_rows, grad_kv = pl.pallas_call(
        finish_kernel,
        out_shape=[struct((tok_dev, qkv_width)), struct(block)],
        in_specs=[VMEM] * (3 + len(others)),
        out_specs=[VMEM] * 2,
        cost_estimate=cost(2),
        name="finish_rows",
    )(rope, grad_q, merged[0], *others)
    gkv = [grad_kv] + [dp_move(grad_kv, step) for step in range(1, replicas)]

    second = lax.optimization_barrier((x_halves[1][1:], gq[1:]))
    x_halves[1][1:] = [dp_move(x, step) for step, x in enumerate(second[0], 1)]

    def reduce_context(xs, gs, cols):
        rows = xs[0].shape[1] // shards
        half_rows = shards // 2 * rows
        specs = [VMEM] * (2 * replicas)
        away = pl.pallas_call(
            functools.partial(partial_kernel, replicas, 0, rows, False),
            out_shape=[struct((half_rows, cols))],
            in_specs=specs,
            out_specs=[VMEM],
            compiler_params=params(40),
            cost_estimate=cost(2 * cols / width),
            name="weights_other_core",
        )(*xs, *gs)[0]
        arrived = context_move(away, 1)
        blocks = pl.pallas_call(
            functools.partial(partial_kernel, replicas, half_rows, rows, True),
            out_shape=[struct((rows, cols), F32)] + [struct((rows, cols))] * (shards // 2 - 1),
            in_specs=specs + [VMEM],
            out_specs=[VMEM] * (shards // 2),
            compiler_params=params(40),
            cost_estimate=cost(2 * cols / width),
            name="weights_own_core",
        )(*xs, *gs, arrived)
        return [blocks[0]] + [context_move(blocks[step // 2], step) for step in range(2, shards, 2)]

    sums = [reduce_context(x_halves[half], gq, width) for half in range(2)]
    sums += [reduce_context(x_halves[half], gkv, 2 * head_dim) for half in range(2)]
    places = []
    for cols in (slice(0, width), slice(width, qkv_width)):
        for half in range(2):
            places.append((slice(half * tile, (half + 1) * tile), cols))
    grad_weight, amax = pl.pallas_call(
        functools.partial(total_kernel, [len(part) for part in sums], places),
        out_shape=[struct((slice_rows, qkv_width), F32), struct((1, 1, 2), F32)],
        in_specs=[VMEM] * (len(sums) * len(sums[0]) + replicas),
        out_specs=[VMEM] * 2,
        compiler_params=params(40),
        name="total_weights",
    )(*[x for part in sums for x in part], *gkv)
    return (grad_rows[None], grad_weight, amax)


def solution(mesh):
    in_specs = (
        P("dp", "context", None),
        P("dp", "context", None),
        P("dp", "context", None),
        P("dp", "context", None),
        P("dp", "context", None),
        P("dp", None),
        P(),
    )
    out_specs = (P("dp", "context", None), P(("dp", "context"), None), P("dp", "context", None))
    return jax.shard_map(local, mesh=mesh, in_specs=in_specs, out_specs=out_specs, check_vma=False)
```

time: 440 us -> 186 us (0.42)
  blocking collectives: 176 us -> 0 us
  local copies, waits for them, and re-layouts: 63.8 us -> 8.44 us
  starting transfers between devices: 0.34 us -> 51.9 us
  matrix products: 50.2 us -> 0 us
  other arithmetic: 48.1 us -> 0.84 us
  Pallas kernels: 0 us -> 26.5 us
  waiting for transfers between devices: 70.3 us -> 94 us
  loops' own time: 14.3 us -> 0 us
  between operations: 14.1 us -> 0.94 us
    all_to_all x1 -> x0, blocking collectives: 106 us -> none  [local(): lax.all_to_all(inputs, 'context', split_axis=2, concat_axis=0, tiled=True)]
    ppermute x0 -> x39, waiting for transfers between devices: none -> 94 us  [the longest x27 51.4 us: context_move(): return lax.ppermute(x, 'context', [(i, i ^ step) for i in range(shards)])]
    reduce_scatter x3 -> x0, waiting for transfers between devices: 70.2 us -> none  [the longest x1 27.7 us: local(): lax.psum_scatter(value_terms, 'context', scatter_dimension=0, tiled=True)]
    ppermute x0 -> x39, starting transfers between devices: none -> 51.9 us  [the longest x27 33.7 us: context_move(): return lax.ppermute(x, 'context', [(i, i ^ step) for i in range(shards)])]
    dot_general x22 -> x0, matrix products: 50.2 us -> none  [the longest x6 15.9 us: block_scores(): dprobs = jnp.dot(out_rows, value_part.T, preferred_element_type=jnp.float32)]
    pmax x1 -> x0, blocking collectives: 39.6 us -> none  [local(): out_max, ds_global = lax.pmax((out_local, ds_max), ('dp', 'context'))]
    all_gather x2 -> x0, blocking collectives: 31 us -> none  [the longest x1 16.4 us: local(): lax.all_gather(key_rows[0], 'context', axis=0, tiled=True)]
    pallas_call x0 -> x13, Pallas kernels: none -> 26.5 us  [the longest x1 7.46 us: local(): pl.pallas_call(functools.partial(attend_kernel, shards, heads), out_shape...]
  transfers between devices with their start and end apart: 4 -> 39, of which waited for: 3 -> 18; matrix products, arithmetic and copies ran while one was open for 4% -> 0% of each run, Pallas kernels for 0% -> 10%
where the time goes in v1:
time: 186 us; the launch traced here: 183 us
  waiting for transfers between devices  94 us (51%)
  starting transfers between devices  51.9 us (28%)
  Pallas kernels  26.5 us (14%)
  local copies, waits for them, and re-layouts  8.44 us (5%)
    ppermute x27, waiting for transfers between devices, context_move(): return lax.ppermute(x, 'context', [(i, i ^ step) for i in range(shards)])  51.4 us
    ppermute x12, waiting for transfers between devices, dp_move(): return lax.ppermute(x, 'dp', [(i, i ^ step) for i in range(replicas)])  42.6 us
    ppermute x27, starting transfers between devices, context_move(): return lax.ppermute(x, 'context', [(i, i ^ step) for i in range(shards)])  33.7 us
    ppermute x12, starting transfers between devices, dp_move(): return lax.ppermute(x, 'dp', [(i, i ^ step) for i in range(replicas)])  18.2 us
    unnamed x46, local copies, waits for them, and re-layouts  8.44 us
    pallas_call x1, Pallas kernels, local(): pl.pallas_call(functools.partial(attend_kernel, shards, heads), out_shape...  7.46 us
    pallas_call x4, Pallas kernels, reduce_context(): pl.pallas_call(functools.partial(partial_kernel, replicas, half_rows, row...  6.02 us
    pallas_call x4, Pallas kernels, reduce_context(): pl.pallas_call(functools.partial(partial_kernel, replicas, 0, rows, False...  5.59 us
  transfers between devices with their start and end apart: 39, of which 18 were waited for; matrix products, arithmetic and copies ran while one was open for 0% of the time, Pallas kernels for 10%

profile of v1, /device:TPU:0, one launch (start us, length us, event | category | flops | bytes accessed | tf_op | source)
XLA Modules:
  0.0 182.6 jit_solution(5850463158338024250)
XLA Ops:
  1.5 3.1 %collective-permute-start.1 = (bf16[192,256]{1,0:T(8,128)(2,1)S(1)}, bf16[192,256]{1,0:T(8,128)(2,1)S(1)}, u32[]{:S(2)}, u32[]{:S(2)}) collective-permute-start(bf16[192,256]{1,0:T(8,128)(2,1)S(1)} %pad_maximum_fusion.refs_0_), channel_id=1, source_target_pairs={{0,2},{1,3},{2,0},{3,1},{4,6},{5,7},{6,4},{7,5},{8,10},{9,11},{10,... | collective-permute-start | bytes 294920 | tf_op jit(solution)/shard_map/ppermute | solution.py:314
  4.6 2.6 %collective-permute-start.3 = (bf16[192,256]{1,0:T(8,128)(2,1)S(1)}, bf16[192,256]{1,0:T(8,128)(2,1)S(1)}, u32[]{:S(2)}, u32[]{:S(2)}) collective-permute-start(bf16[192,256]{1,0:T(8,128)(2,1)S(1)} %pad_maximum_fusion.refs_0_), channel_id=1, source_target_pairs={{0,4},{1,5},{2,6},{3,7},{4,0},{5,1},{6,2},{7,3},{8,12},{9,13},{10,... | collective-permute-start | bytes 294920 | tf_op jit(solution)/shard_map/ppermute | solution.py:314
  7.7 7.3 %collective-permute-done.3.refs_4_ = bf16[192,256]{1,0:T(8,128)(2,1)S(1)} collective-permute-done((bf16[192,256]{1,0:T(8,128)(2,1)S(1)}, bf16[192,256]{1,0:T(8,128)(2,1)S(1)}, u32[]{:S(2)}, u32[]{:S(2)}) %collective-permute-start.3) | collective-permute-done | bytes 98336 | tf_op jit(solution)/shard_map/ppermute | solution.py:314
  23.3 7.5 %attend.1 = (bf16[192,1024]{1,0:T(8,128)(2,1)S(1)}, f32[4,208,256]{2,1,0:T(8,128)S(1)}, bf16[4,208,256]{2,1,0:T(8,128)(2,1)S(1)}) custom-call(s32[8]{0:T(128)S(1)} %copy-done.15, s32[1,1536]{1,0:T(1,128)S(1)} %copy-done.13, f32[2,96,256]{2,1,0:T(8,128)S(1)} %get-tuple-element.44.rope, bf16[2,768,128]{2,1,0:T(8,128)(2,1)S(1)} %get-tuple-element.45.q_cats, ...), custom_call_target="tpu_custom_call" | custom-call | flops 12000000000 | tf_op jit(solution)/shard_map/attend/pallas_call | solution.py:358
  38.0 5.0 %collective-permute-done.14.refs_5_ = bf16[192,1024]{1,0:T(8,128)(2,1)S(1)} collective-permute-done((bf16[192,1024]{1,0:T(8,128)(2,1)S(1)}, bf16[192,1024]{1,0:T(8,128)(2,1)S(1)}, u32[]{:S(2)}, u32[]{:S(2)}) %collective-permute-start.14) | collective-permute-done | bytes 393248 | tf_op jit(solution)/shard_map/ppermute | solution.py:317
  43.1 2.9 %collective-permute-start.13 = (bf16[192,1024]{1,0:T(8,128)(2,1)S(1)}, bf16[192,1024]{1,0:T(8,128)(2,1)S(1)}, u32[]{:S(2)}, u32[]{:S(2)}) collective-permute-start(bf16[192,1024]{1,0:T(8,128)(2,1)S(1)} %get-tuple-element.58), channel_id=1, source_target_pairs={{0,24},{8,16},{16,8},{24,0},{1,25},{9,17},{17,9},{25,1},{2,26},{10... | collective-permute-start | bytes 1179656 | tf_op jit(solution)/shard_map/ppermute | solution.py:317
  45.9 7.5 %collective-permute-done.15.refs_6_ = bf16[192,1024]{1,0:T(8,128)(2,1)S(1)} collective-permute-done((bf16[192,1024]{1,0:T(8,128)(2,1)S(1)}, bf16[192,1024]{1,0:T(8,128)(2,1)S(1)}, u32[]{:S(2)}, u32[]{:S(2)}) %collective-permute-start.15) | collective-permute-done | bytes 393248 | tf_op jit(solution)/shard_map/ppermute | solution.py:317
  55.1 4.8 %collective-permute-done.11.refs_1_ = bf16[192,1024]{1,0:T(8,128)(2,1)S(1)} collective-permute-done((bf16[192,1024]{1,0:T(8,128)(2,1)S(1)}, bf16[192,1024]{1,0:T(8,128)(2,1)S(1)}, u32[]{:S(2)}, u32[]{:S(2)}) %collective-permute-start.11) | collective-permute-done | bytes 393248 | tf_op jit(solution)/shard_map/ppermute | solution.py:317
  60.0 2.9 %collective-permute-start.23 = (bf16[192,1024]{1,0:T(8,128)(2,1)S(1)}, bf16[192,1024]{1,0:T(8,128)(2,1)S(1)}, u32[]{:S(2)}, u32[]{:S(2)}) collective-permute-start(bf16[192,1024]{1,0:T(8,128)(2,1)S(1)} %get-tuple-element.69), channel_id=1, source_target_pairs={{0,24},{8,16},{16,8},{24,0},{1,25},{9,17},{17,9},{25,1},{2,26},{10... | collective-permute-start | bytes 1179656 | tf_op jit(solution)/shard_map/ppermute | solution.py:317
  62.8 7.5 %collective-permute-done.12.refs_2_ = bf16[192,1024]{1,0:T(8,128)(2,1)S(1)} collective-permute-done((bf16[192,1024]{1,0:T(8,128)(2,1)S(1)}, bf16[192,1024]{1,0:T(8,128)(2,1)S(1)}, u32[]{:S(2)}, u32[]{:S(2)}) %collective-permute-start.12) | collective-permute-done | bytes 393248 | tf_op jit(solution)/shard_map/ppermute | solution.py:317
  73.1 3.8 %collective-permute-done.21.refs_1_ = bf16[192,1024]{1,0:T(8,128)(2,1)S(1)} collective-permute-done((bf16[192,1024]{1,0:T(8,128)(2,1)S(1)}, bf16[192,1024]{1,0:T(8,128)(2,1)S(1)}, u32[]{:S(2)}, u32[]{:S(2)}) %collective-permute-start.21) | collective-permute-done | bytes 393248 | tf_op jit(solution)/shard_map/ppermute | solution.py:317
  76.9 8.2 %collective-permute-done.22.refs_2_ = bf16[192,1024]{1,0:T(8,128)(2,1)S(1)} collective-permute-done((bf16[192,1024]{1,0:T(8,128)(2,1)S(1)}, bf16[192,1024]{1,0:T(8,128)(2,1)S(1)}, u32[]{:S(2)}, u32[]{:S(2)}) %collective-permute-start.22) | collective-permute-done | bytes 393248 | tf_op jit(solution)/shard_map/ppermute | solution.py:317
  85.4 2.3 %weights_other_core.5 = bf16[512,1024]{1,0:T(8,128)(2,1)} custom-call(bf16[192,1024]{1,0:T(8,128)(2,1)S(1)} %get-tuple-element.63.refs_0_, bf16[192,1024]{1,0:T(8,128)(2,1)S(1)} %collective-permute-done.21.refs_1_, bf16[192,1024]{1,0:T(8,128)(2,1)S(1)} %collective-permute-done.22.refs_2_, bf16[192,1024]{1,0:T(8,128)(2,1)S(1)} %collective-permute-done.23.refs_3_, ...), custom_call_target="tpu_custom_call" | custom-call | flops 2000000000 | tf_op jit(solution)/shard_map/weights_other_core/pallas_call | solution.py:412
  91.3 3.1 %collective-permute-start.8 = (bf16[208,256]{1,0:T(8,128)(2,1)}, bf16[208,256]{1,0:T(8,128)(2,1)S(1)}, u32[]{:S(2)}, u32[]{:S(2)}) collective-permute-start(bf16[208,256]{1,0:T(8,128)(2,1)} %get-tuple-element.51), channel_id=1, source_target_pairs={{0,2},{1,3},{2,0},{3,1},{4,6},{5,7},{6,4},{7,5},{8,10},{9,11},{10,... | collective-permute-start | bytes 319496 | tf_op jit(solution)/shard_map/ppermute | solution.py:314
  95.6 2.8 %collective-permute-done.10.refs_2_ = bf16[208,256]{1,0:T(8,128)(2,1)S(1)} collective-permute-done((bf16[208,256]{1,0:T(8,128)(2,1)}, bf16[208,256]{1,0:T(8,128)(2,1)S(1)}, u32[]{:S(2)}, u32[]{:S(2)}) %collective-permute-start.10) | collective-permute-done | bytes 106528 | tf_op jit(solution)/shard_map/ppermute | solution.py:314
  100.2 4.8 %collective-permute-done.9.refs_1_ = bf16[208,256]{1,0:T(8,128)(2,1)S(1)} collective-permute-done((bf16[208,256]{1,0:T(8,128)(2,1)}, bf16[208,256]{1,0:T(8,128)(2,1)S(1)}, u32[]{:S(2)}, u32[]{:S(2)}) %collective-permute-start.9) | collective-permute-done | bytes 106528 | tf_op jit(solution)/shard_map/ppermute | solution.py:314
  119.6 2.5 %weights_own_core.4 = (f32[128,1024]{1,0:T(8,128)S(1)}, bf16[128,1024]{1,0:T(8,128)(2,1)S(1)}, bf16[128,1024]{1,0:T(8,128)(2,1)S(1)}, bf16[128,1024]{1,0:T(8,128)(2,1)S(1)}) custom-call(bf16[192,1024]{1,0:T(8,128)(2,1)S(1)} %get-tuple-element.55.refs_0_, bf16[192,1024]{1,0:T(8,128)(2,1)S(1)} %collective-permute-done.11.refs_1_, ...), custom_call_target="tpu_custom_call" | custom-call | flops 2000000000 | tf_op jit(solution)/shard_map/weights_own_core/pallas_call | solution.py:422
  124.8 2.4 %collective-permute-start.34 = (bf16[128,256]{1,0:T(8,128)(2,1)S(1)}, bf16[128,256]{1,0:T(8,128)(2,1)S(1)}, u32[]{:S(2)}, u32[]{:S(2)}) collective-permute-start(bf16[128,256]{1,0:T(8,128)(2,1)S(1)} %get-tuple-element.78), channel_id=1, source_target_pairs={{0,6},{1,7},{2,4},{3,5},{4,2},{5,3},{6,0},{7,1},{8,14},{9,15},{10,... | collective-permute-start | bytes 196616 | tf_op jit(solution)/shard_map/ppermute | solution.py:314
  127.7 6.8 %collective-permute-done.32.refs_9_ = bf16[128,256]{1,0:T(8,128)(2,1)S(1)} collective-permute-done((bf16[128,256]{1,0:T(8,128)(2,1)S(1)}, bf16[128,256]{1,0:T(8,128)(2,1)S(1)}, u32[]{:S(2)}, u32[]{:S(2)}) %collective-permute-start.32) | collective-permute-done | bytes 65568 | tf_op jit(solution)/shard_map/ppermute | solution.py:314
  135.0 3.9 %collective-permute-start.38 = (bf16[128,256]{1,0:T(8,128)(2,1)S(1)}, bf16[128,256]{1,0:T(8,128)(2,1)S(1)}, u32[]{:S(2)}, u32[]{:S(2)}) collective-permute-start(bf16[128,256]{1,0:T(8,128)(2,1)S(1)} %get-tuple-element.82), channel_id=1, source_target_pairs={{0,6},{1,7},{2,4},{3,5},{4,2},{5,3},{6,0},{7,1},{8,14},{9,15},{10,... | collective-permute-start | bytes 196616 | tf_op jit(solution)/shard_map/ppermute | solution.py:314
  138.9 2.5 %weights_own_core.5 = (f32[128,1024]{1,0:T(8,128)S(1)}, bf16[128,1024]{1,0:T(8,128)(2,1)S(1)}, bf16[128,1024]{1,0:T(8,128)(2,1)S(1)}, bf16[128,1024]{1,0:T(8,128)(2,1)S(1)}) custom-call(bf16[192,1024]{1,0:T(8,128)(2,1)S(1)} %get-tuple-element.63.refs_0_, bf16[192,1024]{1,0:T(8,128)(2,1)S(1)} %collective-permute-done.21.refs_1_, ...), custom_call_target="tpu_custom_call" | custom-call | flops 2000000000 | tf_op jit(solution)/shard_map/weights_own_core/pallas_call | solution.py:422
  146.0 7.6 %collective-permute-start.27 = (bf16[128,1024]{1,0:T(8,128)(2,1)S(1)}, bf16[128,1024]{1,0:T(8,128)(2,1)S(1)}, u32[]{:S(2)}, u32[]{:S(2)}) collective-permute-start(bf16[128,1024]{1,0:T(8,128)(2,1)S(1)} %get-tuple-element.73), channel_id=1, source_target_pairs={{0,6},{1,7},{2,4},{3,5},{4,2},{5,3},{6,0},{7,1},{8,14},{9,15},{10,... | collective-permute-start | bytes 786440 | tf_op jit(solution)/shard_map/ppermute | solution.py:314
  153.5 16.5 %collective-permute-done.19.refs_2_ = bf16[128,1024]{1,0:T(8,128)(2,1)S(1)} collective-permute-done((bf16[128,1024]{1,0:T(8,128)(2,1)S(1)}, bf16[128,1024]{1,0:T(8,128)(2,1)S(1)}, u32[]{:S(2)}, u32[]{:S(2)}) %collective-permute-start.19) | collective-permute-done | bytes 262176 | tf_op jit(solution)/shard_map/ppermute | solution.py:314
  170.0 11.2 %collective-permute-done.26.refs_6_ = bf16[128,1024]{1,0:T(8,128)(2,1)S(1)} collective-permute-done((bf16[128,1024]{1,0:T(8,128)(2,1)S(1)}, bf16[128,1024]{1,0:T(8,128)(2,1)S(1)}, u32[]{:S(2)}, u32[]{:S(2)}) %collective-permute-start.26) | collective-permute-done | bytes 262176 | tf_op jit(solution)/shard_map/ppermute | solution.py:314
  (114 shorter events, 52.1 us)
Async XLA Ops:
  4.6 10.4 %collective-permute-start.3 = (bf16[192,256]{1,0:T(8,128)(2,1)S(1)}, bf16[192,256]{1,0:T(8,128)(2,1)S(1)}, u32[]{:S(2)}, u32[]{:S(2)}) collective-permute-start(bf16[192,256]{1,0:T(8,128)(2,1)S(1)} %pad_maximum_fusion.refs_0_), channel_id=1, source_target_pairs={{0,4},{1,5},{2,6},{3,7},{4,0},{5,1},{6,2},{7,3},{8,12},{9,13},{10,... | collective-permute-start | bytes 294920 | tf_op jit(solution)/shard_map/ppermute | solution.py:314
  7.2 16.1 %collective-permute-start = (bf16[192,256]{1,0:T(8,128)(2,1)S(1)}, bf16[192,256]{1,0:T(8,128)(2,1)S(1)}, u32[]{:S(2)}, u32[]{:S(2)}) collective-permute-start(bf16[192,256]{1,0:T(8,128)(2,1)S(1)} %pad_maximum_fusion.refs_0_), channel_id=1, source_target_pairs={{0,1},{1,0},{2,3},{3,2},{4,5},{5,4},{6,7},{7,6},{8,9},{9,8},{10,11... | collective-permute-start | bytes 294920 | tf_op jit(solution)/shard_map/ppermute | solution.py:314
  7.4 15.9 %collective-permute-start.2 = (bf16[192,256]{1,0:T(8,128)(2,1)S(1)}, bf16[192,256]{1,0:T(8,128)(2,1)S(1)}, u32[]{:S(2)}, u32[]{:S(2)}) collective-permute-start(bf16[192,256]{1,0:T(8,128)(2,1)S(1)} %collective-permute-done.1.refs_2_), channel_id=1, source_target_pairs={{0,1},{1,0},{2,3},{3,2},{4,5},{5,4},{6,7},{7,6},{8,9},{9,8},{10,11... | collective-permute-start | bytes 294920 | tf_op jit(solution)/shard_map/ppermute | solution.py:314
  30.8 12.2 %collective-permute-start.14 = (bf16[192,1024]{1,0:T(8,128)(2,1)S(1)}, bf16[192,1024]{1,0:T(8,128)(2,1)S(1)}, u32[]{:S(2)}, u32[]{:S(2)}) collective-permute-start(bf16[192,1024]{1,0:T(8,128)(2,1)S(1)} %get-tuple-element.47.gq_ref.refs_4_), channel_id=1, source_target_pairs={{0,8},{8,0},{16,24},{24,16},{1,9},{9,1},{17,25},{25,17},{2,10},{10... | collective-permute-start | bytes 1179656 | tf_op jit(solution)/shard_map/ppermute | solution.py:317
  33.0 20.5 %collective-permute-start.15 = (bf16[192,1024]{1,0:T(8,128)(2,1)S(1)}, bf16[192,1024]{1,0:T(8,128)(2,1)S(1)}, u32[]{:S(2)}, u32[]{:S(2)}) collective-permute-start(bf16[192,1024]{1,0:T(8,128)(2,1)S(1)} %get-tuple-element.47.gq_ref.refs_4_), channel_id=1, source_target_pairs={{0,16},{8,24},{16,0},{24,8},{1,17},{9,25},{17,1},{25,9},{2,18},{10... | collective-permute-start | bytes 1179656 | tf_op jit(solution)/shard_map/ppermute | solution.py:317
  34.5 18.9 %collective-permute-start.16 = (bf16[192,1024]{1,0:T(8,128)(2,1)S(1)}, bf16[192,1024]{1,0:T(8,128)(2,1)S(1)}, u32[]{:S(2)}, u32[]{:S(2)}) collective-permute-start(bf16[192,1024]{1,0:T(8,128)(2,1)S(1)} %get-tuple-element.47.gq_ref.refs_4_), channel_id=1, source_target_pairs={{0,24},{8,16},{16,8},{24,0},{1,25},{9,17},{17,9},{25,1},{2,26},{10... | collective-permute-start | bytes 1179656 | tf_op jit(solution)/shard_map/ppermute | solution.py:317
  34.6 25.4 %collective-permute-start.11 = (bf16[192,1024]{1,0:T(8,128)(2,1)S(1)}, bf16[192,1024]{1,0:T(8,128)(2,1)S(1)}, u32[]{:S(2)}, u32[]{:S(2)}) collective-permute-start(bf16[192,1024]{1,0:T(8,128)(2,1)S(1)} %get-tuple-element.56), channel_id=1, source_target_pairs={{0,8},{8,0},{16,24},{24,16},{1,9},{9,1},{17,25},{25,17},{2,10},{10... | collective-permute-start | bytes 1179656 | tf_op jit(solution)/shard_map/ppermute | solution.py:317
  36.5 33.8 %collective-permute-start.12 = (bf16[192,1024]{1,0:T(8,128)(2,1)S(1)}, bf16[192,1024]{1,0:T(8,128)(2,1)S(1)}, u32[]{:S(2)}, u32[]{:S(2)}) collective-permute-start(bf16[192,1024]{1,0:T(8,128)(2,1)S(1)} %get-tuple-element.57), channel_id=1, source_target_pairs={{0,16},{8,24},{16,0},{24,8},{1,17},{9,25},{17,1},{25,9},{2,18},{10... | collective-permute-start | bytes 1179656 | tf_op jit(solution)/shard_map/ppermute | solution.py:317
  43.1 27.3 %collective-permute-start.13 = (bf16[192,1024]{1,0:T(8,128)(2,1)S(1)}, bf16[192,1024]{1,0:T(8,128)(2,1)S(1)}, u32[]{:S(2)}, u32[]{:S(2)}) collective-permute-start(bf16[192,1024]{1,0:T(8,128)(2,1)S(1)} %get-tuple-element.58), channel_id=1, source_target_pairs={{0,24},{8,16},{16,8},{24,0},{1,25},{9,17},{17,9},{25,1},{2,26},{10... | collective-permute-start | bytes 1179656 | tf_op jit(solution)/shard_map/ppermute | solution.py:317
  53.5 23.4 %collective-permute-start.21 = (bf16[192,1024]{1,0:T(8,128)(2,1)S(1)}, bf16[192,1024]{1,0:T(8,128)(2,1)S(1)}, u32[]{:S(2)}, u32[]{:S(2)}) collective-permute-start(bf16[192,1024]{1,0:T(8,128)(2,1)S(1)} %get-tuple-element.67), channel_id=1, source_target_pairs={{0,8},{8,0},{16,24},{24,16},{1,9},{9,1},{17,25},{25,17},{2,10},{10... | collective-permute-start | bytes 1179656 | tf_op jit(solution)/shard_map/ppermute | solution.py:317
  54.4 30.7 %collective-permute-start.22 = (bf16[192,1024]{1,0:T(8,128)(2,1)S(1)}, bf16[192,1024]{1,0:T(8,128)(2,1)S(1)}, u32[]{:S(2)}, u32[]{:S(2)}) collective-permute-start(bf16[192,1024]{1,0:T(8,128)(2,1)S(1)} %get-tuple-element.68), channel_id=1, source_target_pairs={{0,16},{8,24},{16,0},{24,8},{1,17},{9,25},{17,1},{25,9},{2,18},{10... | collective-permute-start | bytes 1179656 | tf_op jit(solution)/shard_map/ppermute | solution.py:317
  60.0 25.4 %collective-permute-start.23 = (bf16[192,1024]{1,0:T(8,128)(2,1)S(1)}, bf16[192,1024]{1,0:T(8,128)(2,1)S(1)}, u32[]{:S(2)}, u32[]{:S(2)}) collective-permute-start(bf16[192,1024]{1,0:T(8,128)(2,1)S(1)} %get-tuple-element.69), channel_id=1, source_target_pairs={{0,24},{8,16},{16,8},{24,0},{1,25},{9,17},{17,9},{25,1},{2,26},{10... | collective-permute-start | bytes 1179656 | tf_op jit(solution)/shard_map/ppermute | solution.py:317
  70.3 18.0 %collective-permute-start.7 = (bf16[4,208,256]{2,1,0:T(8,128)(2,1)S(1)}, bf16[4,208,256]{2,1,0:T(8,128)(2,1)S(1)}, u32[]{:S(2)}, u32[]{:S(2)}) collective-permute-start(bf16[4,208,256]{2,1,0:T(8,128)(2,1)S(1)} %get-tuple-element.49), channel_id=1, source_target_pairs={{0,1},{1,0},{2,3},{3,2},{4,5},{5,4},{6,7},{7,6},{8,9},{9,8},{10,11... | collective-permute-start | bytes 1277960 | tf_op jit(solution)/shard_map/ppermute | solution.py:314
  72.6 46.8 %collective-permute-start.17 = (bf16[512,1024]{1,0:T(8,128)(2,1)}, bf16[512,1024]{1,0:T(8,128)(2,1)}, u32[]{:S(2)}, u32[]{:S(2)}) collective-permute-start(bf16[512,1024]{1,0:T(8,128)(2,1)} %weights_other_core.4), channel_id=1, source_target_pairs={{0,1},{1,0},{2,3},{3,2},{4,5},{5,4},{6,7},{7,6},{8,9},{9,8},{10,11... | collective-permute-start | bytes 3145736 | tf_op jit(solution)/shard_map/ppermute | solution.py:314
  87.7 47.3 %collective-permute-start.24 = (bf16[512,1024]{1,0:T(8,128)(2,1)}, bf16[512,1024]{1,0:T(8,128)(2,1)}, u32[]{:S(2)}, u32[]{:S(2)}) collective-permute-start(bf16[512,1024]{1,0:T(8,128)(2,1)} %weights_other_core.5), channel_id=1, source_target_pairs={{0,1},{1,0},{2,3},{3,2},{4,5},{5,4},{6,7},{7,6},{8,9},{9,8},{10,11... | collective-permute-start | bytes 3145736 | tf_op jit(solution)/shard_map/ppermute | solution.py:314
  94.4 10.6 %collective-permute-start.9 = (bf16[208,256]{1,0:T(8,128)(2,1)}, bf16[208,256]{1,0:T(8,128)(2,1)S(1)}, u32[]{:S(2)}, u32[]{:S(2)}) collective-permute-start(bf16[208,256]{1,0:T(8,128)(2,1)} %get-tuple-element.52), channel_id=1, source_target_pairs={{0,4},{1,5},{2,6},{3,7},{4,0},{5,1},{6,2},{7,3},{8,12},{9,13},{10,... | collective-permute-start | bytes 319496 | tf_op jit(solution)/shard_map/ppermute | solution.py:314
  122.1 23.9 %collective-permute-start.18 = (bf16[128,1024]{1,0:T(8,128)(2,1)S(1)}, bf16[128,1024]{1,0:T(8,128)(2,1)S(1)}, u32[]{:S(2)}, u32[]{:S(2)}) collective-permute-start(bf16[128,1024]{1,0:T(8,128)(2,1)S(1)} %get-tuple-element.60), channel_id=1, source_target_pairs={{0,2},{1,3},{2,0},{3,1},{4,6},{5,7},{6,4},{7,5},{8,10},{9,11},{10,... | collective-permute-start | bytes 786440 | tf_op jit(solution)/shard_map/ppermute | solution.py:314
  122.7 11.8 %collective-permute-start.32 = (bf16[128,256]{1,0:T(8,128)(2,1)S(1)}, bf16[128,256]{1,0:T(8,128)(2,1)S(1)}, u32[]{:S(2)}, u32[]{:S(2)}) collective-permute-start(bf16[128,256]{1,0:T(8,128)(2,1)S(1)} %get-tuple-element.76), channel_id=1, source_target_pairs={{0,2},{1,3},{2,0},{3,1},{4,6},{5,7},{6,4},{7,5},{8,10},{9,11},{10,... | collective-permute-start | bytes 196616 | tf_op jit(solution)/shard_map/ppermute | solution.py:314
  124.8 16.6 %collective-permute-start.34 = (bf16[128,256]{1,0:T(8,128)(2,1)S(1)}, bf16[128,256]{1,0:T(8,128)(2,1)S(1)}, u32[]{:S(2)}, u32[]{:S(2)}) collective-permute-start(bf16[128,256]{1,0:T(8,128)(2,1)S(1)} %get-tuple-element.78), channel_id=1, source_target_pairs={{0,6},{1,7},{2,4},{3,5},{4,2},{5,3},{6,0},{7,1},{8,14},{9,15},{10,... | collective-permute-start | bytes 196616 | tf_op jit(solution)/shard_map/ppermute | solution.py:314
  141.4 28.6 %collective-permute-start.19 = (bf16[128,1024]{1,0:T(8,128)(2,1)S(1)}, bf16[128,1024]{1,0:T(8,128)(2,1)S(1)}, u32[]{:S(2)}, u32[]{:S(2)}) collective-permute-start(bf16[128,1024]{1,0:T(8,128)(2,1)S(1)} %get-tuple-element.61), channel_id=1, source_target_pairs={{0,4},{1,5},{2,6},{3,7},{4,0},{5,1},{6,2},{7,3},{8,12},{9,13},{10,... | collective-permute-start | bytes 786440 | tf_op jit(solution)/shard_map/ppermute | solution.py:314
  141.5 28.5 %collective-permute-start.20 = (bf16[128,1024]{1,0:T(8,128)(2,1)S(1)}, bf16[128,1024]{1,0:T(8,128)(2,1)S(1)}, u32[]{:S(2)}, u32[]{:S(2)}) collective-permute-start(bf16[128,1024]{1,0:T(8,128)(2,1)S(1)} %get-tuple-element.62), channel_id=1, source_target_pairs={{0,6},{1,7},{2,4},{3,5},{4,2},{5,3},{6,0},{7,1},{8,14},{9,15},{10,... | collective-permute-start | bytes 786440 | tf_op jit(solution)/shard_map/ppermute | solution.py:314
  142.9 27.1 %collective-permute-start.25 = (bf16[128,1024]{1,0:T(8,128)(2,1)S(1)}, bf16[128,1024]{1,0:T(8,128)(2,1)S(1)}, u32[]{:S(2)}, u32[]{:S(2)}) collective-permute-start(bf16[128,1024]{1,0:T(8,128)(2,1)S(1)} %get-tuple-element.71), channel_id=1, source_target_pairs={{0,2},{1,3},{2,0},{3,1},{4,6},{5,7},{6,4},{7,5},{8,10},{9,11},{10,... | collective-permute-start | bytes 786440 | tf_op jit(solution)/shard_map/ppermute | solution.py:314
  145.0 36.3 %collective-permute-start.26 = (bf16[128,1024]{1,0:T(8,128)(2,1)S(1)}, bf16[128,1024]{1,0:T(8,128)(2,1)S(1)}, u32[]{:S(2)}, u32[]{:S(2)}) collective-permute-start(bf16[128,1024]{1,0:T(8,128)(2,1)S(1)} %get-tuple-element.72), channel_id=1, source_target_pairs={{0,4},{1,5},{2,6},{3,7},{4,0},{5,1},{6,2},{7,3},{8,12},{9,13},{10,... | collective-permute-start | bytes 786440 | tf_op jit(solution)/shard_map/ppermute | solution.py:314
  146.0 35.3 %collective-permute-start.27 = (bf16[128,1024]{1,0:T(8,128)(2,1)S(1)}, bf16[128,1024]{1,0:T(8,128)(2,1)S(1)}, u32[]{:S(2)}, u32[]{:S(2)}) collective-permute-start(bf16[128,1024]{1,0:T(8,128)(2,1)S(1)} %get-tuple-element.73), channel_id=1, source_target_pairs={{0,6},{1,7},{2,4},{3,5},{4,2},{5,3},{6,0},{7,1},{8,14},{9,15},{10,... | collective-permute-start | bytes 786440 | tf_op jit(solution)/shard_map/ppermute | solution.py:314
  (38 other events, 350.8 us)

commit v2 on v1

v2 whole, which is shorter than its diff:
```python
import functools
import math

import jax
import jax.numpy as jnp
import numpy as np
from jax import lax
from jax.experimental import pallas as pl
from jax.experimental.pallas import tpu as pltpu
from jax.sharding import PartitionSpec as P

THETA_BASE = 500000.0
NEG_LARGE = -1e30
DOC_VALUES = 8
EXTRA = 16
F32 = jnp.float32
BF16 = jnp.bfloat16
VMEM = pl.BlockSpec(memory_space=pltpu.VMEM)
SMEM = pl.BlockSpec(memory_space=pltpu.SMEM)
ANY = pl.BlockSpec(memory_space=pl.ANY)


def rope_tables(seq_len, head_dim):
    inverse_freq = THETA_BASE ** (-2.0 * np.arange(head_dim // 2) / head_dim)
    angles = np.arange(seq_len)[:, None] * inverse_freq[None, :]
    angles = np.concatenate([angles, angles], axis=1)
    sign = np.where(np.arange(head_dim) < head_dim // 2, 1.0, -1.0)
    return np.concatenate(
        [np.cos(angles).astype(np.float32), (np.sin(angles) * sign).astype(np.float32)], axis=1
    )


def unrotate(rows, cosine, signed_sine):
    return rows * cosine + pltpu.roll(rows, rows.shape[-1] // 2, 1) * signed_sine


def span_of(pair, half, shards):
    return pair if half == 0 else 2 * shards - 1 - pair


def spread_max(out_max, ds_max, width):
    high = ds_max.astype(BF16).astype(F32)
    middle = (ds_max - high).astype(BF16).astype(F32)
    low = ds_max - high - middle
    row = lax.broadcasted_iota(jnp.int32, (EXTRA, width), 0)
    return jnp.where(
        row == 0,
        out_max,
        jnp.where(row == 1, high, jnp.where(row == 2, middle, jnp.where(row == 3, low, 0.0))),
    )


def read_max(rows):
    wide = rows.astype(F32)
    return wide[0:1], wide[1:2] + wide[2:3] + wide[3:4]


def join_max(parts):
    pairs = [read_max(part) for part in parts]
    out_max, ds_max = pairs[0]
    for other_out, other_ds in pairs[1:]:
        out_max, ds_max = jnp.maximum(out_max, other_out), jnp.maximum(ds_max, other_ds)
    return spread_max(out_max, ds_max, parts[0].shape[1])


def attend_kernel(shards, heads, order, rope, bounds, out_top, q_cats, g_cats, *refs):
    pieces = refs[:shards]
    (gq_ref, keep_ref, send_ref, keys, values, score_buf, dprob_buf, dq_acc, dk_acc, dv_acc) = refs[shards:]
    lanes, head_dim = q_cats.shape[1:]
    span_len = lanes // heads
    tok_dev = 2 * span_len
    scale = 1.0 / math.sqrt(head_dim)
    for index in range(shards):
        rows = pl.ds(index * tok_dev, tok_dev)
        keys[rows] = pieces[index][:, :head_dim]
        values[rows] = pieces[index][:, head_dim:]
    dk_acc[...] = jnp.zeros_like(dk_acc)
    dv_acc[...] = jnp.zeros_like(dv_acc)
    ds_top = jnp.zeros((1, lanes), F32)
    sub = lax.broadcasted_iota(jnp.int32, (span_len, 1), 0)

    for half in range(2):
        count = order[half, 2, 0]
        doc_first = bounds[half, 0:1]
        query_pos = bounds[half, 1:2]
        own = pl.ds(half * span_len, span_len)
        q_cat, g_cat = q_cats.at[half], g_cats.at[half]

        def score_step(index, top):
            block = order[half, 0, index]
            key_pos = order[half, 1, index] * span_len + sub
            rows = pl.ds(pl.multiple_of(block * span_len, span_len), span_len)
            scores = lax.dot_general(
                keys[rows], q_cat[...], (((1,), (1,)), ((), ())), preferred_element_type=F32
            )
            allowed = (key_pos <= query_pos) & (key_pos >= doc_first)
            scores = jnp.where(allowed, scores, NEG_LARGE)
            score_buf[index] = scores
            dprob_buf[index] = lax.dot_general(
                values[rows], g_cat[...], (((1,), (1,)), ((), ())), preferred_element_type=F32
            )
            return jnp.maximum(top, jnp.max(scores, axis=0, keepdims=True))

        top = lax.fori_loop(0, count, score_step, jnp.full((1, lanes), NEG_LARGE, F32))

        def exp_step(index, sums):
            total, weighted = sums
            expd = jnp.exp((score_buf[index] - top) * scale)
            score_buf[index] = expd
            return (
                total + jnp.sum(expd, axis=0, keepdims=True),
                weighted + jnp.sum(expd * dprob_buf[index], axis=0, keepdims=True),
            )

        zero_row = jnp.zeros((1, lanes), F32)
        total, weighted = lax.fori_loop(0, count, exp_step, (zero_row, zero_row))
        inverse = 1.0 / total
        delta = weighted * inverse
        dq_acc[...] = jnp.zeros_like(dq_acc)

        def grad_step(index, ds_now):
            block = order[half, 0, index]
            rows = pl.ds(pl.multiple_of(block * span_len, span_len), span_len)
            probs = score_buf[index] * inverse
            dscores = probs * (dprob_buf[index] - delta)
            probs_low = probs.astype(BF16)
            ds_low = dscores.astype(BF16)
            dv_acc[rows] += jnp.dot(probs_low, g_cat[...], preferred_element_type=F32)
            dk_acc[rows] += jnp.dot(ds_low, q_cat[...], preferred_element_type=F32)
            dq_acc[...] += lax.dot_general(
                keys[rows], ds_low, (((0,), (0,)), ((), ())), preferred_element_type=F32
            )
            return jnp.maximum(ds_now, jnp.max(jnp.abs(dscores), axis=0, keepdims=True))

        ds_top = lax.fori_loop(0, count, grad_step, ds_top)
        cosine = rope[half, :, :head_dim]
        signed_sine = rope[half, :, head_dim:]
        grad_q = dq_acc[...].T * scale
        for head in range(heads):
            part = grad_q[head * span_len : (head + 1) * span_len]
            gq_ref[own, pl.ds(head * head_dim, head_dim)] = unrotate(part, cosine, signed_sine).astype(BF16)

    extra = spread_max(jnp.max(out_top[...]), jnp.max(ds_top), 2 * head_dim)
    for index in range(shards):
        rows = pl.ds(index * tok_dev, tok_dev)
        target = (keep_ref, send_ref)[index % 2]
        kind = target.dtype
        target[index // 2, :tok_dev, :head_dim] = dk_acc[rows].astype(kind)
        target[index // 2, :tok_dev, head_dim:] = dv_acc[rows].astype(kind)
        target[index // 2, tok_dev:] = extra.astype(kind)


def merge_kernel(keep_ref, got_ref, next_ref, send_ref):
    tok_dev = keep_ref.shape[1] - EXTRA
    extra = join_max([keep_ref[0, tok_dev:], got_ref[0, tok_dev:]])
    for index in range(keep_ref.shape[0]):
        both = keep_ref[index, :tok_dev] + got_ref[index, :tok_dev].astype(F32)
        target = (next_ref, send_ref)[index % 2]
        target[index // 2, :tok_dev] = both.astype(target.dtype)
        target[index // 2, tok_dev:] = extra.astype(target.dtype)


def finish_kernel(rope, gq_ref, keep_ref, got_ref, rows_ref, gkv_ref):
    tok_dev = gq_ref.shape[0]
    head_dim = keep_ref.shape[2] // 2
    total = keep_ref[0, :tok_dev] + got_ref[0, :tok_dev].astype(F32)
    extra = join_max([keep_ref[0, tok_dev:], got_ref[0, tok_dev:]])
    wide = rope[...].reshape(tok_dev, 2 * head_dim)
    grad_k = unrotate(
        total[:, :head_dim] * (1.0 / math.sqrt(head_dim)), wide[:, :head_dim], wide[:, head_dim:]
    ).astype(BF16)
    grad_v = total[:, head_dim:].astype(BF16)
    gkv_ref[:tok_dev, :head_dim] = grad_k
    gkv_ref[:tok_dev, head_dim:] = grad_v
    gkv_ref[tok_dev:] = extra.astype(BF16)
    width = gq_ref.shape[1]
    rows_ref[:, :width] = gq_ref[...]
    rows_ref[:, width : width + head_dim] = grad_k
    rows_ref[:, width + head_dim :] = grad_v


def partial_kernel(groups, count, first, adds, *refs):
    xs, gs = refs[: groups * count], refs[groups * count : (groups + 1) * count]
    rest = refs[(groups + 1) * count :]
    tok_dev = xs[0].shape[0]
    tile = xs[0].shape[1] // (2 * first[1])
    for index in range(first[1] * groups):
        block, group = index // groups, index % groups
        cols = slice((first[0] + block) * tile, (first[0] + block + 1) * tile)
        total = None
        for x_ref, g_ref in zip(xs[group * count : (group + 1) * count], gs):
            term = lax.dot_general(
                x_ref[:, cols], g_ref[:tok_dev], (((0,), (0,)), ((), ())), preferred_element_type=F32
            )
            total = term if total is None else total + term
        rows = slice(index * tile, (index + 1) * tile)
        if adds:
            total = total + rest[0][rows].astype(F32)
            target = rest[1 + block % 2]
            place = block // 2 * groups + group
            target[place * tile : (place + 1) * tile] = total.astype(target.dtype)
        else:
            rest[0][rows] = total.astype(BF16)


def total_kernel(places, *refs):
    out_ref, amax_ref = refs[-2:]
    used = 0
    for (rows, cols), count in places:
        total = refs[used][: rows.stop - rows.start]
        for ref in refs[used + 1 : used + count]:
            total = total + ref[: rows.stop - rows.start].astype(F32)
        out_ref[rows, cols] = total
        used += count
    maxima = [ref[ref.shape[0] - EXTRA :] for ref in refs[used:-2]]
    out_max, ds_max = read_max(join_max(maxima))
    lane = lax.broadcasted_iota(jnp.int32, (1, 2), 1)
    amax_ref[0] = jnp.where(lane == 0, out_max[:, :2], ds_max[:, :2])


def prepare_kernel(replicas, shards, order, tile, pair_ref, docs_ref, table_ref, q_ref, g_ref, *refs):
    rope_sems, sems, q_buf, g_buf = refs[-4:]
    packs = len(refs) > 10
    outs, (list_ref, bounds_ref, top_ref, rope_ref, q_cat, g_cat) = refs[packs : -10 - packs], refs[-10 - packs : -4 - packs]
    waits = [pltpu.make_async_copy(q_ref, q_buf, sems.at[0]), pltpu.make_async_copy(g_ref, g_buf, sems.at[1])]
    if packs:
        x_ref = refs[-5]
        waits.append(pltpu.make_async_copy(refs[0], x_ref, sems.at[2]))
    for copy in waits:
        copy.start()
    tok_dev = q_ref.shape[0]
    span_len = tok_dev // 2
    lanes, head_dim = q_cat.shape[1:]
    rep, me = lax.axis_index("dp"), lax.axis_index("context")
    pair = pair_ref[me]
    copies = []
    for half in range(2):
        start = pl.multiple_of(span_of(pair, half, shards) * span_len, 8)
        copy = pltpu.make_async_copy(table_ref.at[pl.ds(start, span_len)], rope_ref.at[half], rope_sems.at[half])
        copy.start()
        copies.append(copy)
    docs = docs_ref[...]
    starts = [jnp.sum(jnp.where(docs < value, 1.0, 0.0)) for value in range(1, DOC_VALUES)]
    lane_row = lax.broadcasted_iota(jnp.int32, (1, lanes), 1) % span_len
    for half in range(2):
        span = span_of(pair, half, shards)
        base = span * span_len
        base_f = base.astype(F32)
        first_start = jnp.float32(0.0)
        for start in starts:
            first_start = jnp.maximum(first_start, jnp.where(start <= base_f, start, 0.0))
        first_key = first_start.astype(jnp.int32)

        def listing(block, count):
            other = pair_ref[me ^ (block // 2)]
            key_span = jnp.where(block % 2 == 0, other, 2 * shards - 1 - other)
            list_ref[half, 0, count] = block
            list_ref[half, 1, count] = key_span
            needed = (key_span <= span) & (key_span * span_len + span_len > first_key)
            return count + needed.astype(jnp.int32)

        list_ref[half, 2, 0] = lax.fori_loop(0, 2 * shards, listing, jnp.int32(0))
        query_pos = base + lane_row
        query_f = query_pos.astype(F32)
        doc_start = jnp.zeros((1, lanes), F32)
        for start in starts:
            doc_start = jnp.maximum(doc_start, jnp.where(start <= query_f, start, 0.0))
        bounds_ref[half, 0:1] = doc_start.astype(jnp.int32)
        bounds_ref[half, 1:2] = query_pos
    waits[0].wait()
    waits[1].wait()
    for half in range(2):
        own = slice(half * span_len, (half + 1) * span_len)
        for head in range(q_ref.shape[1] // head_dim):
            rows = slice(head * span_len, (head + 1) * span_len)
            cols = slice(head * head_dim, (head + 1) * head_dim)
            q_cat[half, rows] = q_buf[own, cols]
            g_cat[half, rows] = g_buf[own, cols]
    top_ref[...] = jnp.max(jnp.abs(g_cat[...].astype(F32)).reshape(-1, 8, head_dim), axis=0)
    if packs:
        waits[2].wait()
        for half in range(2):
            for step in range(replicas):
                for place, relative in enumerate(order):
                    source = (((rep ^ step) * shards + (me ^ relative)) * 2 + half) * tile
                    outs[half * replicas + step][:, place * tile : (place + 1) * tile] = x_ref[
                        :, pl.ds(pl.multiple_of(source, tile), tile)
                    ]
    for copy in copies:
        copy.wait()


def params(mebibytes):
    return pltpu.CompilerParams(vmem_limit_bytes=mebibytes << 20)


def cost(microseconds):
    return pl.CostEstimate(flops=int(microseconds * 1.0e6), bytes_accessed=0, transcendentals=0)


def local(query_rows, key_rows, value_rows, out_grads, layer_input, doc_ids, pair_span):
    shards = lax.axis_size("context")
    replicas = lax.axis_size("dp")
    tok_dev = query_rows.shape[1]
    head_dim = key_rows.shape[2]
    width = query_rows.shape[2]
    heads = width // head_dim
    model_width = layer_input.shape[2]
    span_len = tok_dev // 2
    seq_len = tok_dev * shards
    qkv_width = width + 2 * head_dim
    lanes = heads * span_len
    slice_rows = model_width // (replicas * shards)
    tile = slice_rows // 2
    table = jnp.asarray(rope_tables(seq_len, head_dim))
    order = list(range(1, shards, 2)) + list(range(0, shards, 2))

    def context_move(x, step):
        return lax.ppermute(x, "context", [(i, i ^ step) for i in range(shards)])

    def dp_move(x, step):
        return lax.ppermute(x, "dp", [(i, i ^ step) for i in range(replicas)])

    def struct(shape, kind=BF16):
        return jax.ShapeDtypeStruct(shape, kind)

    own_kv = jnp.concatenate([key_rows[0], value_rows[0]], axis=1)
    pieces = [None] * shards
    pieces[0] = own_kv
    for step in range(2, shards, 2):
        pieces[step] = context_move(own_kv, step)
    pieces[1] = context_move(own_kv, 1)

    x_local = layer_input[0]
    packs = tile % 128 == 0
    outs = [struct((tok_dev, shards * tile))] * (2 * replicas if packs else 0) + [
        struct((2, 3, 2 * shards + 1), jnp.int32),
        struct((2, 2, lanes), jnp.int32),
        struct((8, head_dim), F32),
        struct((2, span_len, 2 * head_dim), F32),
        struct((2, lanes, head_dim)),
        struct((2, lanes, head_dim)),
    ]
    prepared = pl.pallas_call(
        functools.partial(prepare_kernel, replicas, shards, order, tile),
        out_shape=outs,
        in_specs=[SMEM, VMEM] + [ANY] * (3 + packs),
        out_specs=[SMEM if out.dtype == jnp.int32 and out.shape[1] == 3 else VMEM for out in outs],
        scratch_shapes=([pltpu.VMEM((tok_dev, model_width), BF16)] if packs else [])
        + [
            pltpu.SemaphoreType.DMA((2,)),
            pltpu.SemaphoreType.DMA((3,)),
            pltpu.VMEM((tok_dev, width), BF16),
            pltpu.VMEM((tok_dev, width), BF16),
        ],
        compiler_params=params(60),
        cost_estimate=cost(4),
        name="prepare",
    )(pair_span, doc_ids, table, query_rows[0], out_grads[0], *([x_local] if packs else []))
    packed = prepared[:-6]
    rope = prepared[-3]
    pieces = lax.optimization_barrier((pieces, rope))[0]
    for step in range(2, shards, 2):
        pieces[step + 1] = context_move(pieces[step], 1)
    if tile % 128:
        me, rep = lax.axis_index("context"), lax.axis_index("dp")
        parts = []
        for step in range(replicas):
            part = lax.dynamic_slice_in_dim(x_local, (rep ^ step) * shards * slice_rows, shards * slice_rows, 1)
            part = part.reshape(tok_dev, shards, 2, tile)
            parts.append(jnp.take(part, jnp.asarray(order, jnp.int32) ^ me, axis=1))
        packed = [part[:, :, half].reshape(tok_dev, shards * tile) for half in range(2) for part in parts]
    x_halves = [list(packed[:replicas]), list(packed[replicas:])]
    x_halves[0] = lax.optimization_barrier((x_halves[0], pieces[1:3]))[0]
    x_halves[0][1:] = [dp_move(x_halves[0][step], step) for step in range(1, replicas)]

    buf = (2 * shards, span_len, lanes)
    grad_q, keep, send = pl.pallas_call(
        functools.partial(attend_kernel, shards, heads),
        out_shape=[
            struct((tok_dev, width)),
            struct((shards // 2, tok_dev + EXTRA, 2 * head_dim), F32),
            struct((shards // 2, tok_dev + EXTRA, 2 * head_dim)),
        ],
        in_specs=[SMEM] + [VMEM] * (5 + shards),
        out_specs=[VMEM] * 3,
        scratch_shapes=[
            pltpu.VMEM((seq_len, head_dim), BF16),
            pltpu.VMEM((seq_len, head_dim), BF16),
            pltpu.VMEM(buf, F32),
            pltpu.VMEM(buf, F32),
            pltpu.VMEM((head_dim, lanes), F32),
            pltpu.VMEM((seq_len, head_dim), F32),
            pltpu.VMEM((seq_len, head_dim), F32),
        ],
        compiler_params=params(60),
        cost_estimate=cost(12),
        name="attend",
    )(prepared[-6], rope, prepared[-5], prepared[-4], prepared[-2], prepared[-1], *pieces)

    grad_q, x_halves[0] = lax.optimization_barrier((grad_q, x_halves[0]))
    gq = [grad_q] + [dp_move(grad_q, step) for step in range(1, replicas)]

    block = (tok_dev + EXTRA, 2 * head_dim)
    got, step = context_move(send, 1), 2
    while step < shards:
        count = shards // 2 // step
        keep, send = pl.pallas_call(
            merge_kernel,
            out_shape=[struct((count,) + block, F32), struct((count,) + block)],
            in_specs=[VMEM] * 2,
            out_specs=[VMEM] * 2,
            cost_estimate=cost(2),
            name="merge_rows",
        )(keep, got)
        got, step = context_move(send, step), step * 2

    half_shards = shards // 2

    def other_core(groups, gs):
        rows, cols = len(groups) * tile, gs[0].shape[1]
        return pl.pallas_call(
            functools.partial(partial_kernel, len(groups), replicas, (0, half_shards), False),
            out_shape=struct((half_shards * rows, cols)),
            in_specs=[VMEM] * ((len(groups) + 1) * replicas),
            out_specs=VMEM,
            compiler_params=params(16),
            cost_estimate=cost(2),
            name="weights_other_core",
        )(*[x for xs in groups for x in xs], *gs)

    def own_core(groups, gs, arrived):
        rows, cols = len(groups) * tile, gs[0].shape[1]
        return pl.pallas_call(
            functools.partial(partial_kernel, len(groups), replicas, (half_shards, half_shards), True),
            out_shape=[struct((half_shards // 2 * rows, cols), F32), struct((half_shards // 2 * rows, cols))],
            in_specs=[VMEM] * ((len(groups) + 1) * replicas + 1),
            out_specs=[VMEM] * 2,
            compiler_params=params(16),
            cost_estimate=cost(2),
            name="weights_own_core",
        )(*[x for xs in groups for x in xs], *gs, arrived)

    def split_blocks(x, rows):
        parts = x.reshape(-1, 2, rows, x.shape[1])
        return parts[:, 0].reshape(-1, x.shape[1]), parts[:, 1].reshape(-1, x.shape[1])

    def next_terms(kept, got, rows):
        kept_even, kept_odd = split_blocks(kept, rows)
        got_even, got_odd = split_blocks(got, rows)
        return kept_even + got_even.astype(F32), (kept_odd + got_odd.astype(F32)).astype(BF16)

    def tie(value, *others):
        return lax.optimization_barrier((value, others))[0]

    gq = tie(gq, keep, got)
    away = other_core([x_halves[0]], gq)
    arrived = context_move(away, 1)
    keep, got = tie((keep, got), away)
    grad_rows, grad_kv = pl.pallas_call(
        finish_kernel,
        out_shape=[struct((tok_dev, qkv_width)), struct(block)],
        in_specs=[VMEM] * 4,
        out_specs=[VMEM] * 2,
        cost_estimate=cost(2),
        name="finish_rows",
    )(rope, grad_q, keep, got)
    second = tie(x_halves[1][1:], gq)
    x_halves[1][1:] = [dp_move(x, step) for step, x in enumerate(second, 1)]
    gkv = [grad_kv] + [dp_move(grad_kv, step) for step in range(1, replicas)]

    def first_steps(groups, gs, arrived):
        kept, sent = own_core(groups, gs, arrived)
        return kept, context_move(sent, 2)

    def last_steps(kept, got, rows):
        terms, step, sent = [kept, got], 4, got
        while step < shards:
            kept, sent = next_terms(kept, got, rows)
            got, step = context_move(sent, step), step * 2
            terms.append(got)
        return terms, sent

    first = first_steps([x_halves[0]], gq, tie(arrived, grad_kv))
    first, sent = last_steps(*first, tile)
    x_halves[1] = tie(x_halves[1], first)
    away = other_core([x_halves[1]], gq)
    arrived = context_move(away, 1)
    second = first_steps([x_halves[1]], gq, arrived)
    gkv = tie(gkv, second[0])
    away = other_core(x_halves, gkv)
    arrived = context_move(away, 1)
    second, sent = last_steps(*second, tile)
    third = first_steps(x_halves, gkv, tie(arrived, sent))
    third, sent = last_steps(*third, 2 * tile)
    terms = [first, second, third]
    places = [
        ((slice(0, tile), slice(0, width)), len(terms[0])),
        ((slice(tile, 2 * tile), slice(0, width)), len(terms[1])),
        ((slice(0, 2 * tile), slice(width, qkv_width)), len(terms[2])),
    ]
    grad_weight, amax = pl.pallas_call(
        functools.partial(total_kernel, places),
        out_shape=[struct((slice_rows, qkv_width), F32), struct((1, 1, 2), F32)],
        in_specs=[VMEM] * (sum(len(part) for part in terms) + replicas),
        out_specs=[VMEM] * 2,
        compiler_params=params(16),
        name="total_weights",
    )(*[x for part in terms for x in part], *gkv)
    return (grad_rows[None], grad_weight, amax)


def solution(mesh):
    in_specs = (
        P("dp", "context", None),
        P("dp", "context", None),
        P("dp", "context", None),
        P("dp", "context", None),
        P("dp", "context", None),
        P("dp", None),
        P(),
    )
    out_specs = (P("dp", "context", None), P(("dp", "context"), None), P("dp", "context", None))
    return jax.shard_map(local, mesh=mesh, in_specs=in_specs, out_specs=out_specs, check_vma=False)
```

time: 186 us -> 137 us (0.74); the launches traced: 183 us -> 136 us
  waiting for transfers between devices: 94 us -> 70.1 us
  starting transfers between devices: 51.9 us -> 33.3 us
  local copies, waits for them, and re-layouts: 8.44 us -> 2 us
  Pallas kernels: 26.5 us -> 29 us
    ppermute x12, waiting for transfers between devices: 42.6 us -> 23 us  [dp_move(): return lax.ppermute(x, 'dp', [(i, i ^ step) for i in range(replicas)])]
    ppermute x27 -> x19, starting transfers between devices: 33.7 us -> 19.3 us  [context_move(): return lax.ppermute(x, 'context', [(i, i ^ step) for i in range(shards)])]
    unnamed x46 -> x36, local copies, waits for them, and re-layouts: 8.44 us -> 2 us
    ppermute x27 -> x19, waiting for transfers between devices: 51.4 us -> 47.1 us  [context_move(): return lax.ppermute(x, 'context', [(i, i ^ step) for i in range(shards)])]
    ppermute x12, starting transfers between devices: 18.2 us -> 14 us  [dp_move(): return lax.ppermute(x, 'dp', [(i, i ^ step) for i in range(replicas)])]
    pallas_call x1, Pallas kernels: 1.79 us -> 5.73 us  [local(): pl.pallas_call(functools.partial(prepare_kernel, replicas, shards, order,...]
    pallas_call x10 -> x9, Pallas kernels: 15.1 us -> 14.2 us  [the longest x3 4.68 us: own_core(): pl.pallas_call(functools.partial(partial_kernel, len(groups), replicas, (...]
  transfers between devices with their start and end apart: 39 -> 31, of which waited for: 18 -> 16; matrix products, arithmetic and copies ran while one was open for 0% -> 0% of each run, Pallas kernels for 10% -> 14%
where the time goes in v2:
time: 137 us; the launch traced here: 136 us
  waiting for transfers between devices  70.1 us (51%)
  starting transfers between devices  33.3 us (24%)
  Pallas kernels  29 us (21%)
  local copies, waits for them, and re-layouts  2 us (1%)
    ppermute x19, waiting for transfers between devices, context_move(): return lax.ppermute(x, 'context', [(i, i ^ step) for i in range(shards)])  47.1 us
    ppermute x12, waiting for transfers between devices, dp_move(): return lax.ppermute(x, 'dp', [(i, i ^ step) for i in range(replicas)])  23 us
    ppermute x19, starting transfers between devices, context_move(): return lax.ppermute(x, 'context', [(i, i ^ step) for i in range(shards)])  19.3 us
    ppermute x12, starting transfers between devices, dp_move(): return lax.ppermute(x, 'dp', [(i, i ^ step) for i in range(replicas)])  14 us
    pallas_call x1, Pallas kernels, local(): pl.pallas_call(functools.partial(attend_kernel, shards, heads), out_shape...  6.95 us
    pallas_call x1, Pallas kernels, local(): pl.pallas_call(functools.partial(prepare_kernel, replicas, shards, order,...  5.73 us
    pallas_call x3, Pallas kernels, own_core(): pl.pallas_call(functools.partial(partial_kernel, len(groups), replicas, (...  4.68 us
    pallas_call x3, Pallas kernels, other_core(): pl.pallas_call(functools.partial(partial_kernel, len(groups), replicas, (...  4.31 us
  transfers between devices with their start and end apart: 31, of which 16 were waited for; matrix products, arithmetic and copies ran while one was open for 0% of the time, Pallas kernels for 14%

profile of v2, /device:TPU:0, one launch (start us, length us, event | category | flops | bytes accessed | tf_op | source)
XLA Modules:
  0.0 136.3 jit_solution(2555417646058684592)
XLA Ops:
  2.0 2.6 %collective-permute-start.1 = (bf16[192,256]{1,0:T(8,128)(2,1)S(1)}, bf16[192,256]{1,0:T(8,128)(2,1)S(1)}, u32[]{:S(2)}, u32[]{:S(2)}) collective-permute-start(bf16[192,256]{1,0:T(8,128)(2,1)S(1)} %pad_maximum_fusion.refs_0_), channel_id=1, source_target_pairs={{0,2},{1,3},{2,0},{3,1},{4,6},{5,7},{6,4},{7,5},{8,10},{9,11},{10,... | collective-permute-start | bytes 294920 | tf_op jit(solution)/shard_map/ppermute | solution.py:319
  4.6 2.6 %collective-permute-start.2 = (bf16[192,256]{1,0:T(8,128)(2,1)S(1)}, bf16[192,256]{1,0:T(8,128)(2,1)S(1)}, u32[]{:S(2)}, u32[]{:S(2)}) collective-permute-start(bf16[192,256]{1,0:T(8,128)(2,1)S(1)} %pad_maximum_fusion.refs_0_), channel_id=1, source_target_pairs={{0,4},{1,5},{2,6},{3,7},{4,0},{5,1},{6,2},{7,3},{8,12},{9,13},{10,... | collective-permute-start | bytes 294920 | tf_op jit(solution)/shard_map/ppermute | solution.py:319
  7.2 5.7 %prepare.1 = (bf16[192,1024]{1,0:T(8,128)(2,1)}, bf16[192,1024]{1,0:T(8,128)(2,1)}, bf16[192,1024]{1,0:T(8,128)(2,1)}, bf16[192,1024]{1,0:T(8,128)(2,1)}, bf16[1...) custom-call(s32[8]{0:T(128)} %pair_ref.1, ...), custom_call_target="tpu_custom_call" | custom-call | flops 4000000 | tf_op jit(solution)/shard_map/prepare/pallas_call | solution.py:344
  13.0 2.4 %collective-permute-done.2.refs_4_ = bf16[192,256]{1,0:T(8,128)(2,1)S(1)} collective-permute-done((bf16[192,256]{1,0:T(8,128)(2,1)S(1)}, bf16[192,256]{1,0:T(8,128)(2,1)S(1)}, u32[]{:S(2)}, u32[]{:S(2)}) %collective-permute-start.2) | collective-permute-done | bytes 98336 | tf_op jit(solution)/shard_map/ppermute | solution.py:319
  20.2 7.0 %attend.1 = (bf16[192,1024]{1,0:T(8,128)(2,1)}, f32[4,208,256]{2,1,0:T(8,128)}, bf16[4,208,256]{2,1,0:T(8,128)(2,1)}) custom-call(s32[2,3,17]{2,1,0:T(4,128)} %get-tuple-element.68.order, f32[2,96,256]{2,1,0:T(8,128)} %get-tuple-element.67.rope, s32[2,2,768]{2,1,0:T(2,128)} %get-tuple-element.69.bounds, f32[8,128]{1,0:T(8,128)} %get-tuple-element.70.out_top, ...), custom_call_target="tpu_custom_call" | custom-call | flops 12000000 | tf_op jit(solution)/shard_map/attend/pallas_call | solution.py:378
  28.2 9.2 %collective-permute-done.8.refs_2_ = bf16[192,1024]{1,0:T(8,128)(2,1)S(1)} collective-permute-done((bf16[192,1024]{1,0:T(8,128)(2,1)}, bf16[192,1024]{1,0:T(8,128)(2,1)S(1)}, u32[]{:S(2)}, u32[]{:S(2)}) %collective-permute-start.8) | collective-permute-done | bytes 393248 | tf_op jit(solution)/shard_map/ppermute | solution.py:322
  40.9 2.1 %merge_rows.2 = (f32[2,208,256]{2,1,0:T(8,128)}, bf16[2,208,256]{2,1,0:T(8,128)(2,1)}) custom-call(f32[4,208,256]{2,1,0:T(8,128)} %get-tuple-element.88.keep_ref, bf16[4,208,256]{2,1,0:T(8,128)(2,1)} %collective-permute-done.10.got_ref), custom_call_target="tpu_custom_call" | custom-call | flops 2000000 | tf_op jit(solution)/shard_map/merge_rows/pallas_call | solution.py:408
  44.8 4.3 %collective-permute-done.11.got_ref = bf16[2,208,256]{2,1,0:T(8,128)(2,1)S(1)} collective-permute-done((bf16[2,208,256]{2,1,0:T(8,128)(2,1)}, bf16[2,208,256]{2,1,0:T(8,128)(2,1)S(1)}, u32[]{:S(2)}, u32[]{:S(2)}) %collective-permute-start.11) | collective-permute-done | bytes 213024 | tf_op jit(solution)/shard_map/ppermute | solution.py:319
  51.6 2.8 %collective-permute-start.12 = (bf16[1,208,256]{2,1,0:T(8,128)(2,1)}, bf16[1,208,256]{2,1,0:T(8,128)(2,1)S(1)}, u32[]{:S(2)}, u32[]{:S(2)}) collective-permute-start(bf16[1,208,256]{2,1,0:T(8,128)(2,1)} %get-tuple-element.93), channel_id=1, source_target_pairs={{0,4},{1,5},{2,6},{3,7},{4,0},{5,1},{6,2},{7,3},{8,12},{9,13},{10,... | collective-permute-start | bytes 319496 | tf_op jit(solution)/shard_map/ppermute | solution.py:319
  54.5 3.2 %collective-permute-done.14.refs_6_ = bf16[192,1024]{1,0:T(8,128)(2,1)S(1)} collective-permute-done((bf16[192,1024]{1,0:T(8,128)(2,1)}, bf16[192,1024]{1,0:T(8,128)(2,1)S(1)}, u32[]{:S(2)}, u32[]{:S(2)}) %collective-permute-start.14) | collective-permute-done | bytes 393248 | tf_op jit(solution)/shard_map/ppermute | solution.py:322
  58.3 2.2 %weights_other_core.3 = bf16[512,1024]{1,0:T(8,128)(2,1)} custom-call(bf16[192,1024]{1,0:T(8,128)(2,1)S(1)} %copy-done.2, bf16[192,1024]{1,0:T(8,128)(2,1)S(1)} %collective-permute-done.7.refs_1_, bf16[192,1024]{1,0:T(8,128)(2,1)S(1)} %collective-permute-done.8.refs_2_, bf16[192,1024]{1,0:T(8,128)(2,1)S(1)} %collective-permute-done.9.refs_3_, ...), custom_call_target="tpu_custom_call" | custom-call | flops 2000000 | tf_op jit(solution)/shard_map/weights_other_core/pallas_call | solution.py:422
  60.5 2.1 %finish_rows.1 = (bf16[192,1280]{1,0:T(8,128)(2,1)}, bf16[208,256]{1,0:T(8,128)(2,1)}) custom-call(f32[2,96,256]{2,1,0:T(8,128)} %get-tuple-element.67.rope, bf16[192,1024]{1,0:T(8,128)(2,1)} %get-tuple-element.98.refs_4_.gq_ref, f32[1,208,256]{2,1,0:T(8,128)} %get-tuple-element.102.keep_ref, bf16[1,208,256]{2,1,0:T(8,128)(2,1)} %copy-done.7), custom_call_target="tpu_custom_call" | custom-call | flops 2000000 | tf_op jit(solution)/shard_map/finish_rows/pallas_call | solution.py:460
  63.6 2.6 %weights_own_core.3 = (f32[256,1024]{1,0:T(8,128)S(1)}, bf16[256,1024]{1,0:T(8,128)(2,1)S(1)}) custom-call(bf16[192,1024]{1,0:T(8,128)(2,1)S(1)} %copy-done.2, bf16[192,1024]{1,0:T(8,128)(2,1)S(1)} %collective-permute-done.7.refs_1_, bf16[192,1024]{1,0:T(8,128)(2,1)S(1)} %collective-permute-done.8.refs_2_, ...), custom_call_target="tpu_custom_call" | custom-call | flops 2000000 | tf_op jit(solution)/shard_map/weights_own_core/pallas_call | solution.py:434
  71.7 8.7 %collective-permute-done.17.refs_1_ = bf16[256,1024]{1,0:T(8,128)(2,1)S(1)} collective-permute-done((bf16[256,1024]{1,0:T(8,128)(2,1)S(1)}, bf16[256,1024]{1,0:T(8,128)(2,1)S(1)}, u32[]{:S(2)}, u32[]{:S(2)}) %collective-permute-start.17) | collective-permute-done | bytes 524320 | tf_op jit(solution)/shard_map/ppermute | solution.py:319
  80.4 2.9 %collective-permute-start.18 = (bf16[128,1024]{1,0:T(8,128)(2,1)S(1)}, bf16[128,1024]{1,0:T(8,128)(2,1)S(1)}, u32[]{:S(2)}, u32[]{:S(2)}) collective-permute-start(bf16[128,1024]{1,0:T(8,128)(2,1)S(1)} %fusion.2), channel_id=1, source_target_pairs={{0,4},{1,5},{2,6},{3,7},{4,0},{5,1},{6,2},{7,3},{8,12},{9,13},{10,... | collective-permute-start | bytes 786440 | tf_op jit(solution)/shard_map/ppermute | solution.py:319
  83.3 5.0 %collective-permute-done.20.refs_2_.refs_6_ = bf16[192,1024]{1,0:T(8,128)(2,1)S(1)} collective-permute-done((bf16[192,1024]{1,0:T(8,128)(2,1)S(1)}, bf16[192,1024]{1,0:T(8,128)(2,1)S(1)}, u32[]{:S(2)}, u32[]{:S(2)}) %collective-permute-start.20) | collective-permute-done | bytes 393248 | tf_op jit(solution)/shard_map/ppermute | solution.py:322
  88.3 6.4 %collective-permute-done.18.refs_2_ = bf16[128,1024]{1,0:T(8,128)(2,1)S(1)} collective-permute-done((bf16[128,1024]{1,0:T(8,128)(2,1)S(1)}, bf16[128,1024]{1,0:T(8,128)(2,1)S(1)}, u32[]{:S(2)}, u32[]{:S(2)}) %collective-permute-start.18) | collective-permute-done | bytes 262176 | tf_op jit(solution)/shard_map/ppermute | solution.py:319
  96.1 2.6 %collective-permute-done.22.refs_8_ = bf16[512,1024]{1,0:T(8,128)(2,1)S(1)} collective-permute-done((bf16[512,1024]{1,0:T(8,128)(2,1)S(1)}, bf16[512,1024]{1,0:T(8,128)(2,1)S(1)}, u32[]{:S(2)}, u32[]{:S(2)}) %collective-permute-start.22) | collective-permute-done | bytes 1048608 | tf_op jit(solution)/shard_map/ppermute | solution.py:319
  105.4 2.9 %collective-permute-done.26.refs_10_.refs_11_ = bf16[208,256]{1,0:T(8,128)(2,1)S(1)} collective-permute-done((bf16[208,256]{1,0:T(8,128)(2,1)S(1)}, bf16[208,256]{1,0:T(8,128)(2,1)S(1)}, u32[]{:S(2)}, u32[]{:S(2)}) %collective-permute-start.26) | collective-permute-done | bytes 106528 | tf_op jit(solution)/shard_map/ppermute | solution.py:322
  109.2 4.9 %collective-permute-done.23.refs_4_ = bf16[256,1024]{1,0:T(8,128)(2,1)S(1)} collective-permute-done((bf16[256,1024]{1,0:T(8,128)(2,1)S(1)}, bf16[256,1024]{1,0:T(8,128)(2,1)S(1)}, u32[]{:S(2)}, u32[]{:S(2)}) %collective-permute-start.23) | collective-permute-done | bytes 524320 | tf_op jit(solution)/shard_map/ppermute | solution.py:319
  115.3 2.8 %collective-permute-start.24 = (bf16[128,1024]{1,0:T(8,128)(2,1)S(1)}, bf16[128,1024]{1,0:T(8,128)(2,1)S(1)}, u32[]{:S(2)}, u32[]{:S(2)}) collective-permute-start(bf16[128,1024]{1,0:T(8,128)(2,1)S(1)} %fusion.3), channel_id=1, source_target_pairs={{0,4},{1,5},{2,6},{3,7},{4,0},{5,1},{6,2},{7,3},{8,12},{9,13},{10,... | collective-permute-start | bytes 786440 | tf_op jit(solution)/shard_map/ppermute | solution.py:319
  118.1 10.0 %collective-permute-done.29.refs_7_ = bf16[512,256]{1,0:T(8,128)(2,1)S(1)} collective-permute-done((bf16[512,256]{1,0:T(8,128)(2,1)S(1)}, bf16[512,256]{1,0:T(8,128)(2,1)S(1)}, u32[]{:S(2)}, u32[]{:S(2)}) %collective-permute-start.29) | collective-permute-done | bytes 262176 | tf_op jit(solution)/shard_map/ppermute | solution.py:319
  128.2 2.6 %collective-permute-done.24.refs_5_ = bf16[128,1024]{1,0:T(8,128)(2,1)S(1)} collective-permute-done((bf16[128,1024]{1,0:T(8,128)(2,1)S(1)}, bf16[128,1024]{1,0:T(8,128)(2,1)S(1)}, u32[]{:S(2)}, u32[]{:S(2)}) %collective-permute-start.24) | collective-permute-done | bytes 262176 | tf_op jit(solution)/shard_map/ppermute | solution.py:319
  130.8 4.2 %collective-permute-done.30.refs_8_ = bf16[256,256]{1,0:T(8,128)(2,1)S(1)} collective-permute-done((bf16[256,256]{1,0:T(8,128)(2,1)S(1)}, bf16[256,256]{1,0:T(8,128)(2,1)S(1)}, u32[]{:S(2)}, u32[]{:S(2)}) %collective-permute-start.30) | collective-permute-done | bytes 131104 | tf_op jit(solution)/shard_map/ppermute | solution.py:319
  (90 shorter events, 33.5 us)
Async XLA Ops:
  1.5 11.5 %collective-permute-start = (bf16[192,256]{1,0:T(8,128)(2,1)S(1)}, bf16[192,256]{1,0:T(8,128)(2,1)S(1)}, u32[]{:S(2)}, u32[]{:S(2)}) collective-permute-start(bf16[192,256]{1,0:T(8,128)(2,1)S(1)} %pad_maximum_fusion.refs_0_), channel_id=1, source_target_pairs={{0,1},{1,0},{2,3},{3,2},{4,5},{5,4},{6,7},{7,6},{8,9},{9,8},{10,11... | collective-permute-start | bytes 294920 | tf_op jit(solution)/shard_map/ppermute | solution.py:319
  2.0 11.0 %collective-permute-start.1 = (bf16[192,256]{1,0:T(8,128)(2,1)S(1)}, bf16[192,256]{1,0:T(8,128)(2,1)S(1)}, u32[]{:S(2)}, u32[]{:S(2)}) collective-permute-start(bf16[192,256]{1,0:T(8,128)(2,1)S(1)} %pad_maximum_fusion.refs_0_), channel_id=1, source_target_pairs={{0,2},{1,3},{2,0},{3,1},{4,6},{5,7},{6,4},{7,5},{8,10},{9,11},{10,... | collective-permute-start | bytes 294920 | tf_op jit(solution)/shard_map/ppermute | solution.py:319
  4.6 10.8 %collective-permute-start.2 = (bf16[192,256]{1,0:T(8,128)(2,1)S(1)}, bf16[192,256]{1,0:T(8,128)(2,1)S(1)}, u32[]{:S(2)}, u32[]{:S(2)}) collective-permute-start(bf16[192,256]{1,0:T(8,128)(2,1)S(1)} %pad_maximum_fusion.refs_0_), channel_id=1, source_target_pairs={{0,4},{1,5},{2,6},{3,7},{4,0},{5,1},{6,2},{7,3},{8,12},{9,13},{10,... | collective-permute-start | bytes 294920 | tf_op jit(solution)/shard_map/ppermute | solution.py:319
  7.2 8.2 %collective-permute-start.3 = (bf16[192,256]{1,0:T(8,128)(2,1)S(1)}, bf16[192,256]{1,0:T(8,128)(2,1)S(1)}, u32[]{:S(2)}, u32[]{:S(2)}) collective-permute-start(bf16[192,256]{1,0:T(8,128)(2,1)S(1)} %pad_maximum_fusion.refs_0_), channel_id=1, source_target_pairs={{0,6},{1,7},{2,4},{3,5},{4,2},{5,3},{6,0},{7,1},{8,14},{9,15},{10,... | collective-permute-start | bytes 294920 | tf_op jit(solution)/shard_map/ppermute | solution.py:319
  16.1 12.1 %collective-permute-start.7 = (bf16[192,1024]{1,0:T(8,128)(2,1)}, bf16[192,1024]{1,0:T(8,128)(2,1)S(1)}, u32[]{:S(2)}, u32[]{:S(2)}) collective-permute-start(bf16[192,1024]{1,0:T(8,128)(2,1)} %get-tuple-element.84), channel_id=1, source_target_pairs={{0,8},{8,0},{16,24},{24,16},{1,9},{9,1},{17,25},{25,17},{2,10},{10... | collective-permute-start | bytes 1179656 | tf_op jit(solution)/shard_map/ppermute | solution.py:322
  17.5 19.8 %collective-permute-start.8 = (bf16[192,1024]{1,0:T(8,128)(2,1)}, bf16[192,1024]{1,0:T(8,128)(2,1)S(1)}, u32[]{:S(2)}, u32[]{:S(2)}) collective-permute-start(bf16[192,1024]{1,0:T(8,128)(2,1)} %get-tuple-element.85), channel_id=1, source_target_pairs={{0,16},{8,24},{16,0},{24,8},{1,17},{9,25},{17,1},{25,9},{2,18},{10... | collective-permute-start | bytes 1179656 | tf_op jit(solution)/shard_map/ppermute | solution.py:322
  19.1 18.3 %collective-permute-start.9 = (bf16[192,1024]{1,0:T(8,128)(2,1)}, bf16[192,1024]{1,0:T(8,128)(2,1)S(1)}, u32[]{:S(2)}, u32[]{:S(2)}) collective-permute-start(bf16[192,1024]{1,0:T(8,128)(2,1)} %get-tuple-element.86), channel_id=1, source_target_pairs={{0,24},{8,16},{16,8},{24,0},{1,25},{9,17},{17,9},{25,1},{2,26},{10... | collective-permute-start | bytes 1179656 | tf_op jit(solution)/shard_map/ppermute | solution.py:322
  27.2 13.7 %collective-permute-start.10 = (bf16[4,208,256]{2,1,0:T(8,128)(2,1)}, bf16[4,208,256]{2,1,0:T(8,128)(2,1)}, u32[]{:S(2)}, u32[]{:S(2)}) collective-permute-start(bf16[4,208,256]{2,1,0:T(8,128)(2,1)} %get-tuple-element.89), channel_id=1, source_target_pairs={{0,1},{1,0},{2,3},{3,2},{4,5},{5,4},{6,7},{7,6},{8,9},{9,8},{10,11... | collective-permute-start | bytes 1277960 | tf_op jit(solution)/shard_map/ppermute | solution.py:319
  37.4 17.1 %collective-permute-start.13 = (bf16[192,1024]{1,0:T(8,128)(2,1)}, bf16[192,1024]{1,0:T(8,128)(2,1)S(1)}, u32[]{:S(2)}, u32[]{:S(2)}) collective-permute-start(bf16[192,1024]{1,0:T(8,128)(2,1)} %get-tuple-element.98.refs_4_.gq_ref), channel_id=1, source_target_pairs={{0,8},{8,0},{16,24},{24,16},{1,9},{9,1},{17,25},{25,17},{2,10},{10... | collective-permute-start | bytes 1179656 | tf_op jit(solution)/shard_map/ppermute | solution.py:322
  38.6 19.0 %collective-permute-start.14 = (bf16[192,1024]{1,0:T(8,128)(2,1)}, bf16[192,1024]{1,0:T(8,128)(2,1)S(1)}, u32[]{:S(2)}, u32[]{:S(2)}) collective-permute-start(bf16[192,1024]{1,0:T(8,128)(2,1)} %get-tuple-element.98.refs_4_.gq_ref), channel_id=1, source_target_pairs={{0,16},{8,24},{16,0},{24,8},{1,17},{9,25},{17,1},{25,9},{2,18},{10... | collective-permute-start | bytes 1179656 | tf_op jit(solution)/shard_map/ppermute | solution.py:322
  39.4 18.2 %collective-permute-start.15 = (bf16[192,1024]{1,0:T(8,128)(2,1)}, bf16[192,1024]{1,0:T(8,128)(2,1)S(1)}, u32[]{:S(2)}, u32[]{:S(2)}) collective-permute-start(bf16[192,1024]{1,0:T(8,128)(2,1)} %get-tuple-element.98.refs_4_.gq_ref), channel_id=1, source_target_pairs={{0,24},{8,16},{16,8},{24,0},{1,25},{9,17},{17,9},{25,1},{2,26},{10... | collective-permute-start | bytes 1179656 | tf_op jit(solution)/shard_map/ppermute | solution.py:322
  43.0 6.1 %collective-permute-start.11 = (bf16[2,208,256]{2,1,0:T(8,128)(2,1)}, bf16[2,208,256]{2,1,0:T(8,128)(2,1)S(1)}, u32[]{:S(2)}, u32[]{:S(2)}) collective-permute-start(bf16[2,208,256]{2,1,0:T(8,128)(2,1)} %get-tuple-element.91), channel_id=1, source_target_pairs={{0,2},{1,3},{2,0},{3,1},{4,6},{5,7},{6,4},{7,5},{8,10},{9,11},{10,... | collective-permute-start | bytes 638984 | tf_op jit(solution)/shard_map/ppermute | solution.py:319
  51.6 6.0 %collective-permute-start.12 = (bf16[1,208,256]{2,1,0:T(8,128)(2,1)}, bf16[1,208,256]{2,1,0:T(8,128)(2,1)S(1)}, u32[]{:S(2)}, u32[]{:S(2)}) collective-permute-start(bf16[1,208,256]{2,1,0:T(8,128)(2,1)} %get-tuple-element.93), channel_id=1, source_target_pairs={{0,4},{1,5},{2,6},{3,7},{4,0},{5,1},{6,2},{7,3},{8,12},{9,13},{10,... | collective-permute-start | bytes 319496 | tf_op jit(solution)/shard_map/ppermute | solution.py:319
  66.2 14.2 %collective-permute-start.17 = (bf16[256,1024]{1,0:T(8,128)(2,1)S(1)}, bf16[256,1024]{1,0:T(8,128)(2,1)S(1)}, u32[]{:S(2)}, u32[]{:S(2)}) collective-permute-start(bf16[256,1024]{1,0:T(8,128)(2,1)S(1)} %get-tuple-element.108), channel_id=1, source_target_pairs={{0,2},{1,3},{2,0},{3,1},{4,6},{5,7},{6,4},{7,5},{8,10},{9,11},{10,... | collective-permute-start | bytes 1572872 | tf_op jit(solution)/shard_map/ppermute | solution.py:319
  68.2 15.1 %collective-permute-start.19 = (bf16[192,1024]{1,0:T(8,128)(2,1)S(1)}, bf16[192,1024]{1,0:T(8,128)(2,1)S(1)}, u32[]{:S(2)}, u32[]{:S(2)}) collective-permute-start(bf16[192,1024]{1,0:T(8,128)(2,1)S(1)} %copy-done.17), channel_id=1, source_target_pairs={{0,8},{8,0},{16,24},{24,16},{1,9},{9,1},{17,25},{25,17},{2,10},{10... | collective-permute-start | bytes 1179656 | tf_op jit(solution)/shard_map/ppermute | solution.py:322
  69.3 19.0 %collective-permute-start.20 = (bf16[192,1024]{1,0:T(8,128)(2,1)S(1)}, bf16[192,1024]{1,0:T(8,128)(2,1)S(1)}, u32[]{:S(2)}, u32[]{:S(2)}) collective-permute-start(bf16[192,1024]{1,0:T(8,128)(2,1)S(1)} %copy-done.16), channel_id=1, source_target_pairs={{0,16},{8,24},{16,0},{24,8},{1,17},{9,25},{17,1},{25,9},{2,18},{10... | collective-permute-start | bytes 1179656 | tf_op jit(solution)/shard_map/ppermute | solution.py:322
  70.1 18.2 %collective-permute-start.21 = (bf16[192,1024]{1,0:T(8,128)(2,1)S(1)}, bf16[192,1024]{1,0:T(8,128)(2,1)S(1)}, u32[]{:S(2)}, u32[]{:S(2)}) collective-permute-start(bf16[192,1024]{1,0:T(8,128)(2,1)S(1)} %copy-done.15), channel_id=1, source_target_pairs={{0,24},{8,16},{16,8},{24,0},{1,25},{9,17},{17,9},{25,1},{2,26},{10... | collective-permute-start | bytes 1179656 | tf_op jit(solution)/shard_map/ppermute | solution.py:322
  80.4 14.3 %collective-permute-start.18 = (bf16[128,1024]{1,0:T(8,128)(2,1)S(1)}, bf16[128,1024]{1,0:T(8,128)(2,1)S(1)}, u32[]{:S(2)}, u32[]{:S(2)}) collective-permute-start(bf16[128,1024]{1,0:T(8,128)(2,1)S(1)} %fusion.2), channel_id=1, source_target_pairs={{0,4},{1,5},{2,6},{3,7},{4,0},{5,1},{6,2},{7,3},{8,12},{9,13},{10,... | collective-permute-start | bytes 786440 | tf_op jit(solution)/shard_map/ppermute | solution.py:319
  100.0 14.1 %collective-permute-start.23 = (bf16[256,1024]{1,0:T(8,128)(2,1)S(1)}, bf16[256,1024]{1,0:T(8,128)(2,1)S(1)}, u32[]{:S(2)}, u32[]{:S(2)}) collective-permute-start(bf16[256,1024]{1,0:T(8,128)(2,1)S(1)} %get-tuple-element.121), channel_id=1, source_target_pairs={{0,2},{1,3},{2,0},{3,1},{4,6},{5,7},{6,4},{7,5},{8,10},{9,11},{10,... | collective-permute-start | bytes 1572872 | tf_op jit(solution)/shard_map/ppermute | solution.py:319
  101.3 7.0 %collective-permute-start.26 = (bf16[208,256]{1,0:T(8,128)(2,1)S(1)}, bf16[208,256]{1,0:T(8,128)(2,1)S(1)}, u32[]{:S(2)}, u32[]{:S(2)}) collective-permute-start(bf16[208,256]{1,0:T(8,128)(2,1)S(1)} %copy-done.4), channel_id=1, source_target_pairs={{0,16},{8,24},{16,0},{24,8},{1,17},{9,25},{17,1},{25,9},{2,18},{10... | collective-permute-start | bytes 319496 | tf_op jit(solution)/shard_map/ppermute | solution.py:322
  102.2 6.1 %collective-permute-start.27 = (bf16[208,256]{1,0:T(8,128)(2,1)S(1)}, bf16[208,256]{1,0:T(8,128)(2,1)S(1)}, u32[]{:S(2)}, u32[]{:S(2)}) collective-permute-start(bf16[208,256]{1,0:T(8,128)(2,1)S(1)} %copy-done.4), channel_id=1, source_target_pairs={{0,24},{8,16},{16,8},{24,0},{1,25},{9,17},{17,9},{25,1},{2,26},{10... | collective-permute-start | bytes 319496 | tf_op jit(solution)/shard_map/ppermute | solution.py:322
  114.9 13.1 %collective-permute-start.29 = (bf16[512,256]{1,0:T(8,128)(2,1)S(1)}, bf16[512,256]{1,0:T(8,128)(2,1)S(1)}, u32[]{:S(2)}, u32[]{:S(2)}) collective-permute-start(bf16[512,256]{1,0:T(8,128)(2,1)S(1)} %get-tuple-element.128), channel_id=1, source_target_pairs={{0,2},{1,3},{2,0},{3,1},{4,6},{5,7},{6,4},{7,5},{8,10},{9,11},{10,... | collective-permute-start | bytes 786440 | tf_op jit(solution)/shard_map/ppermute | solution.py:319
  115.3 15.5 %collective-permute-start.24 = (bf16[128,1024]{1,0:T(8,128)(2,1)S(1)}, bf16[128,1024]{1,0:T(8,128)(2,1)S(1)}, u32[]{:S(2)}, u32[]{:S(2)}) collective-permute-start(bf16[128,1024]{1,0:T(8,128)(2,1)S(1)} %fusion.3), channel_id=1, source_target_pairs={{0,4},{1,5},{2,6},{3,7},{4,0},{5,1},{6,2},{7,3},{8,12},{9,13},{10,... | collective-permute-start | bytes 786440 | tf_op jit(solution)/shard_map/ppermute | solution.py:319
  128.1 6.9 %collective-permute-start.30 = (bf16[256,256]{1,0:T(8,128)(2,1)S(1)}, bf16[256,256]{1,0:T(8,128)(2,1)S(1)}, u32[]{:S(2)}, u32[]{:S(2)}) collective-permute-start(bf16[256,256]{1,0:T(8,128)(2,1)S(1)} %fusion.5), channel_id=1, source_target_pairs={{0,4},{1,5},{2,6},{3,7},{4,0},{5,1},{6,2},{7,3},{8,12},{9,13},{10,... | collective-permute-start | bytes 393224 | tf_op jit(solution)/shard_map/ppermute | solution.py:319
  (25 other events, 190.2 us)

commit v3 on v2

v3 whole, which is shorter than its diff:
```python
import functools
import math

import jax
import jax.numpy as jnp
import numpy as np
from jax import lax
from jax.experimental import pallas as pl
from jax.experimental.pallas import tpu as pltpu
from jax.sharding import PartitionSpec as P

THETA_BASE = 500000.0
NEG_LARGE = -1e30
DOC_VALUES = 8
EXTRA = 16
F32 = jnp.float32
BF16 = jnp.bfloat16
VMEM = pl.BlockSpec(memory_space=pltpu.VMEM)
SMEM = pl.BlockSpec(memory_space=pltpu.SMEM)
ANY = pl.BlockSpec(memory_space=pl.ANY)


def rope_tables(seq_len, head_dim):
    inverse_freq = THETA_BASE ** (-2.0 * np.arange(head_dim // 2) / head_dim)
    angles = np.arange(seq_len)[:, None] * inverse_freq[None, :]
    angles = np.concatenate([angles, angles], axis=1)
    sign = np.where(np.arange(head_dim) < head_dim // 2, 1.0, -1.0)
    return np.concatenate(
        [np.cos(angles).astype(np.float32), (np.sin(angles) * sign).astype(np.float32)], axis=1
    )


def unrotate(rows, cosine, signed_sine):
    return rows * cosine + pltpu.roll(rows, rows.shape[-1] // 2, 1) * signed_sine


def span_of(pair, half, shards):
    return pair if half == 0 else 2 * shards - 1 - pair


def spread_max(out_max, ds_max, width):
    high = ds_max.astype(BF16).astype(F32)
    middle = (ds_max - high).astype(BF16).astype(F32)
    low = ds_max - high - middle
    row = lax.broadcasted_iota(jnp.int32, (EXTRA, width), 0)
    return jnp.where(
        row == 0,
        out_max,
        jnp.where(row == 1, high, jnp.where(row == 2, middle, jnp.where(row == 3, low, 0.0))),
    )


def read_max(rows):
    wide = rows.astype(F32)
    return wide[0:1], wide[1:2] + wide[2:3] + wide[3:4]


def join_max(parts):
    pairs = [read_max(part) for part in parts]
    out_max, ds_max = pairs[0]
    for other_out, other_ds in pairs[1:]:
        out_max, ds_max = jnp.maximum(out_max, other_out), jnp.maximum(ds_max, other_ds)
    return spread_max(out_max, ds_max, parts[0].shape[1])


def attend_kernel(shards, heads, order, rope, bounds, out_top, q_cats, g_cats, kv_ref, *refs):
    gq_ref, keep_ref, send_ref, key_list, value_list, score_buf, dprob_buf, dq_acc, dk_acc, dv_acc = refs
    lanes, head_dim = q_cats.shape[1:]
    span_len = lanes // heads
    tok_dev = 2 * span_len
    scale = 1.0 / math.sqrt(head_dim)
    me = lax.axis_index("context")
    dk_acc[...] = jnp.zeros_like(dk_acc)
    dv_acc[...] = jnp.zeros_like(dv_acc)
    ds_top = jnp.zeros((1, lanes), F32)
    sub = lax.broadcasted_iota(jnp.int32, (2 * span_len, 1), 0)

    for half in range(2):
        count = order[half, 2, 0]
        steps = (count + 1) // 2

        def listing(index, unused):
            source = pl.ds(pl.multiple_of(order[half, 0, index] * span_len, span_len), span_len)
            target = pl.ds(pl.multiple_of(index * span_len, span_len), span_len)
            key_list[target] = kv_ref[source, :head_dim]
            value_list[target] = kv_ref[source, head_dim:]
            return unused

        lax.fori_loop(0, count, listing, 0)
        spare = pl.ds(pl.multiple_of(count * span_len, span_len), span_len)
        key_list[spare] = jnp.zeros((span_len, head_dim), BF16)
        value_list[spare] = jnp.zeros((span_len, head_dim), BF16)
        doc_first = bounds[half, 0:1]
        query_pos = bounds[half, 1:2]
        own = pl.ds(half * span_len, span_len)
        q_cat, g_cat = q_cats.at[half], g_cats.at[half]

        def score_step(index, top):
            rows = pl.ds(pl.multiple_of(index * 2 * span_len, 2 * span_len), 2 * span_len)
            start = jnp.where(sub < span_len, order[half, 1, 2 * index], order[half, 1, 2 * index + 1] - 1)
            key_pos = start * span_len + sub
            scores = lax.dot_general(
                key_list[rows], q_cat[...], (((1,), (1,)), ((), ())), preferred_element_type=F32
            )
            allowed = (key_pos <= query_pos) & (key_pos >= doc_first)
            scores = jnp.where(allowed, scores, NEG_LARGE)
            score_buf[index] = scores
            dprob_buf[index] = lax.dot_general(
                value_list[rows], g_cat[...], (((1,), (1,)), ((), ())), preferred_element_type=F32
            )
            return jnp.maximum(top, jnp.max(scores, axis=0, keepdims=True))

        top = lax.fori_loop(0, steps, score_step, jnp.full((1, lanes), NEG_LARGE, F32))

        def exp_step(index, sums):
            total, weighted = sums
            expd = jnp.exp((score_buf[index] - top) * scale)
            score_buf[index] = expd
            return (
                total + jnp.sum(expd, axis=0, keepdims=True),
                weighted + jnp.sum(expd * dprob_buf[index], axis=0, keepdims=True),
            )

        zero_row = jnp.zeros((1, lanes), F32)
        total, weighted = lax.fori_loop(0, steps, exp_step, (zero_row, zero_row))
        inverse = 1.0 / total
        delta = weighted * inverse
        dq_acc[...] = jnp.zeros_like(dq_acc)

        def grad_step(index, ds_now):
            rows = pl.ds(pl.multiple_of(index * 2 * span_len, 2 * span_len), 2 * span_len)
            probs = score_buf[index] * inverse
            dscores = probs * (dprob_buf[index] - delta)
            probs_low = probs.astype(BF16)
            ds_low = dscores.astype(BF16)
            grad_v = jnp.dot(probs_low, g_cat[...], preferred_element_type=F32)
            grad_k = jnp.dot(ds_low, q_cat[...], preferred_element_type=F32)
            for part in range(2):
                block = pl.ds(pl.multiple_of(order[half, 0, 2 * index + part] * span_len, span_len), span_len)
                own_part = slice(part * span_len, (part + 1) * span_len)
                dv_acc[block] += grad_v[own_part]
                dk_acc[block] += grad_k[own_part]
            dq_acc[...] += lax.dot_general(
                key_list[rows], ds_low, (((0,), (0,)), ((), ())), preferred_element_type=F32
            )
            return jnp.maximum(ds_now, jnp.max(jnp.abs(dscores), axis=0, keepdims=True))

        ds_top = lax.fori_loop(0, steps, grad_step, ds_top)
        cosine = rope[half, :, :head_dim]
        signed_sine = rope[half, :, head_dim:]
        grad_q = dq_acc[...].T * scale
        for head in range(heads):
            part = grad_q[head * span_len : (head + 1) * span_len]
            gq_ref[own, pl.ds(head * head_dim, head_dim)] = unrotate(part, cosine, signed_sine).astype(BF16)

    extra = spread_max(jnp.max(out_top[...]), jnp.max(ds_top), 2 * head_dim)
    for index in range(shards):
        rows = pl.ds(pl.multiple_of((me ^ index) * tok_dev, tok_dev), tok_dev)
        target = (keep_ref, send_ref)[index % 2]
        kind = target.dtype
        target[index // 2, :tok_dev, :head_dim] = dk_acc[rows].astype(kind)
        target[index // 2, :tok_dev, head_dim:] = dv_acc[rows].astype(kind)
        target[index // 2, tok_dev:] = extra.astype(kind)


def merge_kernel(keep_ref, got_ref, next_ref, send_ref):
    tok_dev = keep_ref.shape[1] - EXTRA
    extra = join_max([keep_ref[0, tok_dev:], got_ref[0, tok_dev:]])
    for index in range(keep_ref.shape[0]):
        both = keep_ref[index, :tok_dev] + got_ref[index, :tok_dev].astype(F32)
        target = (next_ref, send_ref)[index % 2]
        target[index // 2, :tok_dev] = both.astype(target.dtype)
        target[index // 2, tok_dev:] = extra.astype(target.dtype)


def finish_kernel(rope, gq_ref, keep_ref, got_ref, rows_ref, gkv_ref):
    tok_dev, width = gq_ref.shape
    head_dim = keep_ref.shape[2] // 2
    total = keep_ref[0, :tok_dev] + got_ref[0, :tok_dev].astype(F32)
    extra = join_max([keep_ref[0, tok_dev:], got_ref[0, tok_dev:]])
    wide = rope[...].reshape(tok_dev, 2 * head_dim)
    grad_k = unrotate(
        total[:, :head_dim] * (1.0 / math.sqrt(head_dim)), wide[:, :head_dim], wide[:, head_dim:]
    ).astype(BF16)
    grad_v = total[:, head_dim:].astype(BF16)
    gkv_ref[:tok_dev, :head_dim] = grad_k
    gkv_ref[:tok_dev, head_dim:] = grad_v
    gkv_ref[tok_dev:] = extra.astype(BF16)
    rows_ref[:, :width] = gq_ref[...]
    rows_ref[:, width : width + head_dim] = grad_k
    rows_ref[:, width + head_dim :] = grad_v


def partial_kernel(count, firsts, blocks, tile, adds, *refs):
    groups = len(firsts)
    xs, gs = refs[: groups * count], refs[groups * count : (groups + 1) * count]
    rest = refs[(groups + 1) * count :]
    tok_dev = xs[0].shape[0]
    for index in range(blocks * groups):
        block, group = index // groups, index % groups
        cols = slice((firsts[group] + block) * tile, (firsts[group] + block + 1) * tile)
        total = None
        for x_ref, g_ref in zip(xs[group * count : (group + 1) * count], gs):
            term = lax.dot_general(
                x_ref[:, cols], g_ref[:tok_dev], (((0,), (0,)), ((), ())), preferred_element_type=F32
            )
            total = term if total is None else total + term
        rows = slice(index * tile, (index + 1) * tile)
        if adds:
            total = total + rest[0][rows].astype(F32)
            target = rest[1 + block % 2]
            place = block // 2 * groups + group
            target[place * tile : (place + 1) * tile] = total.astype(target.dtype)
        else:
            rest[0][rows] = total.astype(BF16)


def total_kernel(places, *refs):
    out_ref, amax_ref = refs[-2:]
    used = 0
    for (rows, cols), count in places:
        total = refs[used][: rows.stop - rows.start]
        for ref in refs[used + 1 : used + count]:
            total = total + ref[: rows.stop - rows.start].astype(F32)
        out_ref[rows, cols] = total
        used += count
    maxima = [ref[ref.shape[0] - EXTRA :] for ref in refs[used:-2]]
    out_max, ds_max = read_max(join_max(maxima))
    lane = lax.broadcasted_iota(jnp.int32, (1, 2), 1)
    amax_ref[0] = jnp.where(lane == 0, out_max[:, :2], ds_max[:, :2])


def prepare_kernel(replicas, shards, order, pair_ref, docs_ref, k_ref, v_ref, table_ref, q_ref, g_ref, *refs):
    rope_sems, sems, x_sems, q_buf, g_buf = refs[-5:]
    x_refs, outs = refs[:-12], refs[-12:-5]
    list_ref, kv_ref, bounds_ref, top_ref, rope_ref, q_cat, g_cat = outs
    x_copies = []
    if x_refs:
        rep, own = lax.axis_index("dp"), lax.axis_index("context")
        tile = x_refs[1].shape[1] // shards
        for step in range(replicas):
            for place, relative in enumerate(order):
                block = (rep ^ step) * shards + (own ^ relative)
                half = place // (shards // 2)
                spots = ((0, x_refs[1 + step], place), (1, x_refs[1 + (1 + half) * replicas + step], place % (shards // 2)))
                for part, target, spot in spots:
                    source = pl.multiple_of((block * 2 + part) * tile, tile)
                    copy = pltpu.make_async_copy(
                        x_refs[0].at[:, pl.ds(source, tile)],
                        target.at[:, pl.ds(spot * tile, tile)],
                        x_sems.at[part, step, place],
                    )
                    copy.start()
                    x_copies.append(copy)
    kv_ref[:, : k_ref.shape[1]] = k_ref[...]
    kv_ref[:, k_ref.shape[1] :] = v_ref[...]
    waits = [pltpu.make_async_copy(q_ref, q_buf, sems.at[0]), pltpu.make_async_copy(g_ref, g_buf, sems.at[1])]
    for copy in waits:
        copy.start()
    tok_dev = q_ref.shape[0]
    span_len = tok_dev // 2
    lanes, head_dim = q_cat.shape[1:]
    me = lax.axis_index("context")
    pair = pair_ref[me]
    copies = []
    for half in range(2):
        start = pl.multiple_of(span_of(pair, half, shards) * span_len, 8)
        copy = pltpu.make_async_copy(table_ref.at[pl.ds(start, span_len)], rope_ref.at[half], rope_sems.at[half])
        copy.start()
        copies.append(copy)
    docs = docs_ref[...]
    starts = [jnp.sum(jnp.where(docs < value, 1.0, 0.0)) for value in range(1, DOC_VALUES)]
    lane_row = lax.broadcasted_iota(jnp.int32, (1, lanes), 1) % span_len
    for half in range(2):
        span = span_of(pair, half, shards)
        base = span * span_len
        base_f = base.astype(F32)
        first_start = jnp.float32(0.0)
        for start in starts:
            first_start = jnp.maximum(first_start, jnp.where(start <= base_f, start, 0.0))
        first_key = first_start.astype(jnp.int32)

        def listing(block, count):
            other = pair_ref[block // 2]
            key_span = jnp.where(block % 2 == 0, other, 2 * shards - 1 - other)
            list_ref[half, 0, count] = block
            list_ref[half, 1, count] = key_span
            needed = (key_span <= span) & (key_span * span_len + span_len > first_key)
            return count + needed.astype(jnp.int32)

        count = lax.fori_loop(0, 2 * shards, listing, jnp.int32(0))
        list_ref[half, 2, 0] = count
        list_ref[half, 0, count] = 2 * shards
        list_ref[half, 1, count] = 2 * shards
        query_pos = base + lane_row
        query_f = query_pos.astype(F32)
        doc_start = jnp.zeros((1, lanes), F32)
        for start in starts:
            doc_start = jnp.maximum(doc_start, jnp.where(start <= query_f, start, 0.0))
        bounds_ref[half, 0:1] = doc_start.astype(jnp.int32)
        bounds_ref[half, 1:2] = query_pos
    waits[0].wait()
    waits[1].wait()
    for half in range(2):
        own = slice(half * span_len, (half + 1) * span_len)
        for head in range(q_ref.shape[1] // head_dim):
            rows = slice(head * span_len, (head + 1) * span_len)
            cols = slice(head * head_dim, (head + 1) * head_dim)
            q_cat[half, rows] = q_buf[own, cols]
            g_cat[half, rows] = g_buf[own, cols]
    top_ref[...] = jnp.max(jnp.abs(g_cat[...].astype(F32)).reshape(-1, 8, head_dim), axis=0)
    for copy in copies + x_copies:
        copy.wait()


def params(mebibytes):
    return pltpu.CompilerParams(vmem_limit_bytes=mebibytes << 20)


def cost(microseconds):
    return pl.CostEstimate(flops=int(microseconds * 1.0e6), bytes_accessed=0, transcendentals=0)


def local(query_rows, key_rows, value_rows, out_grads, layer_input, doc_ids, pair_span):
    shards = lax.axis_size("context")
    replicas = lax.axis_size("dp")
    tok_dev = query_rows.shape[1]
    head_dim = key_rows.shape[2]
    width = query_rows.shape[2]
    heads = width // head_dim
    model_width = layer_input.shape[2]
    span_len = tok_dev // 2
    seq_len = tok_dev * shards
    qkv_width = width + 2 * head_dim
    lanes = heads * span_len
    slice_rows = model_width // (replicas * shards)
    tile = slice_rows // 2
    packs = tile % 128 == 0
    half_shards = shards // 2
    table = jnp.asarray(rope_tables(seq_len, head_dim))
    order = list(range(1, shards, 2)) + list(range(0, shards, 2))

    def context_move(x, step):
        return lax.ppermute(x, "context", [(i, i ^ step) for i in range(shards)])

    def dp_move(x, step):
        return lax.ppermute(x, "dp", [(i, i ^ step) for i in range(replicas)])

    def struct(shape, kind=BF16):
        return jax.ShapeDtypeStruct(shape, kind)

    outs = [
        struct((2, 3, 2 * shards + 1), jnp.int32),
        struct((tok_dev, 2 * head_dim)),
        struct((2, 2, lanes), jnp.int32),
        struct((8, head_dim), F32),
        struct((2, span_len, 2 * head_dim), F32),
        struct((2, lanes, head_dim)),
        struct((2, lanes, head_dim)),
    ]
    x_shapes = [(tok_dev, count * tile) for count in (shards, half_shards, half_shards) for _ in range(replicas)]
    if packs:
        outs = [struct(shape) for shape in x_shapes] + outs
    prepared = pl.pallas_call(
        functools.partial(prepare_kernel, replicas, shards, order),
        out_shape=outs,
        in_specs=[SMEM] + [VMEM] * 3 + [ANY] * (3 + packs),
        out_specs=[VMEM] * (len(outs) - 7) + [SMEM] + [VMEM] * 6,
        scratch_shapes=[
            pltpu.SemaphoreType.DMA((2,)),
            pltpu.SemaphoreType.DMA((2,)),
            pltpu.SemaphoreType.DMA((2, replicas, shards)),
            pltpu.VMEM((tok_dev, width), BF16),
            pltpu.VMEM((tok_dev, width), BF16),
        ],
        compiler_params=params(60),
        cost_estimate=cost(4),
        name="prepare",
    )(pair_span, doc_ids, key_rows[0], value_rows[0], table, query_rows[0], out_grads[0], *([layer_input[0]] if packs else []))
    order_list, own_kv, bounds, out_top, rope, q_cats, g_cats = prepared[-7:]
    if packs:
        columns = [list(prepared[first : first + replicas]) for first in range(0, 3 * replicas, replicas)]
    else:
        me, rep = lax.axis_index("context"), lax.axis_index("dp")
        columns = [[], [], []]
        for step in range(replicas):
            part = lax.dynamic_slice_in_dim(layer_input[0], (rep ^ step) * shards * slice_rows, shards * slice_rows, 1)
            part = jnp.take(part.reshape(tok_dev, shards, 2, tile), jnp.asarray(order, jnp.int32) ^ me, axis=1)
            pieces = part[:, :, 0], part[:, :half_shards, 1], part[:, half_shards:, 1]
            for group, piece in zip(columns, pieces):
                group.append(piece.reshape(tok_dev, -1))
    x_first, x_odd, x_even = columns

    def tie(value, *others):
        return lax.optimization_barrier((value, others))[0]

    def exchange(parts):
        return [parts[0]] + [dp_move(parts[step], step) for step in range(1, replicas)]

    x_first = exchange(x_first)
    kv_all = lax.all_gather(own_kv, "context", axis=0, tiled=True)
    x_odd = exchange(tie(x_odd, kv_all, x_first))

    buf = (shards + 1, 2 * span_len, lanes)
    padded = (seq_len + 2 * span_len, head_dim)
    grad_q, keep, send = pl.pallas_call(
        functools.partial(attend_kernel, shards, heads),
        out_shape=[
            struct((tok_dev, width)),
            struct((shards // 2, tok_dev + EXTRA, 2 * head_dim), F32),
            struct((shards // 2, tok_dev + EXTRA, 2 * head_dim)),
        ],
        in_specs=[SMEM] + [VMEM] * 6,
        out_specs=[VMEM] * 3,
        scratch_shapes=[
            pltpu.VMEM(padded, BF16),
            pltpu.VMEM(padded, BF16),
            pltpu.VMEM(buf, F32),
            pltpu.VMEM(buf, F32),
            pltpu.VMEM((head_dim, lanes), F32),
            pltpu.VMEM(padded, F32),
            pltpu.VMEM(padded, F32),
        ],
        compiler_params=params(60),
        cost_estimate=cost(12),
        name="attend",
    )(order_list, rope, bounds, out_top, q_cats, g_cats, kv_all)

    grad_q, send = tie((grad_q, send), x_odd)
    gq = exchange([grad_q] * replicas)

    block = (tok_dev + EXTRA, 2 * head_dim)
    got, step = context_move(send, 1), 2
    while step < shards:
        count = shards // 2 // step
        keep, send = pl.pallas_call(
            merge_kernel,
            out_shape=[struct((count,) + block, F32), struct((count,) + block)],
            in_specs=[VMEM] * 2,
            out_specs=[VMEM] * 2,
            cost_estimate=cost(2),
            name="merge_rows",
        )(keep, got)
        got, step = context_move(send, step), step * 2

    def partial_weights(groups, gs, arrived=None):
        firsts, parts = [first for first, _ in groups], [x for _, xs in groups for x in xs]
        rows, cols = half_shards * len(groups) * tile, gs[0].shape[1]
        adds = arrived is not None
        out_shape = [struct((rows, cols))]
        if adds:
            out_shape = [struct((rows // 2, cols), F32), struct((rows // 2, cols))]
        result = pl.pallas_call(
            functools.partial(partial_kernel, replicas, firsts, half_shards, tile, adds),
            out_shape=out_shape,
            in_specs=[VMEM] * (len(parts) + replicas + adds),
            out_specs=[VMEM] * len(out_shape),
            compiler_params=params(16),
            cost_estimate=cost(2),
            name="weights_own_core" if adds else "weights_other_core",
        )(*parts, *gs, *([arrived] if adds else []))
        return result if adds else result[0]

    def split_blocks(x, rows):
        parts = x.reshape(-1, 2, rows, x.shape[1])
        return parts[:, 0].reshape(-1, x.shape[1]), parts[:, 1].reshape(-1, x.shape[1])

    def next_terms(kept, got, rows):
        kept_even, kept_odd = split_blocks(kept, rows)
        got_even, got_odd = split_blocks(got, rows)
        return kept_even + got_even.astype(F32), (kept_odd + got_odd.astype(F32)).astype(BF16)

    def last_steps(kept, got, rows):
        terms, step, sent = [kept, got], 4, got
        while step < shards:
            kept, sent = next_terms(kept, got, rows)
            got, step = context_move(sent, step), step * 2
            terms.append(got)
        return terms, sent

    gq = tie(gq, keep, got)
    away = partial_weights([(0, x_first)], gq)
    arrived = context_move(away, 1)
    keep, got = tie((keep, got), away)
    grad_rows, grad_kv = pl.pallas_call(
        finish_kernel,
        out_shape=[struct((tok_dev, qkv_width)), struct(block)],
        in_specs=[VMEM] * 4,
        out_specs=[VMEM] * 2,
        cost_estimate=cost(2),
        name="finish_rows",
    )(rope, grad_q, keep, got)
    x_even = exchange(tie(x_even, gq))
    gkv = exchange([grad_kv] * replicas)
    kept, sent = partial_weights([(half_shards, x_first)], gq, tie(arrived, grad_kv))
    first = kept, context_move(sent, 2)
    away = partial_weights([(0, tie(x_odd, sent))], gq)
    arrived = context_move(away, 1)
    first, sent = last_steps(*first, tile)
    kept, sent = partial_weights([(0, x_even)], gq, tie(arrived, sent))
    second = kept, context_move(sent, 2)
    away = partial_weights([(0, x_first), (0, x_odd)], tie(gkv, sent, first))
    arrived = context_move(away, 1)
    second, sent = last_steps(*second, tile)
    kept, sent = partial_weights([(half_shards, x_first), (0, x_even)], gkv, tie(arrived, sent))
    third = last_steps(kept, context_move(sent, 2), 2 * tile)[0]
    terms = [first, second, third]
    upper, lower, full = slice(0, tile), slice(tile, 2 * tile), slice(0, width)
    spots = [(upper, full), (lower, full), (slice(0, 2 * tile), slice(width, qkv_width))]
    places = [(spot, len(part)) for spot, part in zip(spots, terms)]
    grad_weight, amax = pl.pallas_call(
        functools.partial(total_kernel, places),
        out_shape=[struct((slice_rows, qkv_width), F32), struct((1, 1, 2), F32)],
        in_specs=[VMEM] * (sum(len(part) for part in terms) + replicas),
        out_specs=[VMEM] * 2,
        compiler_params=params(16),
        name="total_weights",
    )(*[x for part in terms for x in part], *gkv)
    return (grad_rows[None], grad_weight, amax)


def solution(mesh):
    in_specs = (
        P("dp", "context", None),
        P("dp", "context", None),
        P("dp", "context", None),
        P("dp", "context", None),
        P("dp", "context", None),
        P("dp", None),
        P(),
    )
    out_specs = (P("dp", "context", None), P(("dp", "context"), None), P("dp", "context", None))
    return jax.shard_map(local, mesh=mesh, in_specs=in_specs, out_specs=out_specs, check_vma=False)
```

time: 137 us -> 132 us (0.964)
  blocking collectives: 0 us -> 17.5 us
  waiting for transfers between devices: 70.1 us -> 54.6 us
  starting transfers between devices: 33.3 us -> 28.7 us
    all_gather x0 -> x1, blocking collectives: none -> 17.5 us  [local(): kv_all = lax.all_gather(own_kv, 'context', axis=0, tiled=True)]
    ppermute x12 -> x15, waiting for transfers between devices: 23 us -> 12.4 us  [dp_move(): return lax.ppermute(x, 'dp', [(i, i ^ step) for i in range(replicas)])]
    ppermute x19 -> x12, starting transfers between devices: 19.3 us -> 10.1 us  [context_move(): return lax.ppermute(x, 'context', [(i, i ^ step) for i in range(shards)])]
    ppermute x19 -> x12, waiting for transfers between devices: 47.1 us -> 42.2 us  [context_move(): return lax.ppermute(x, 'context', [(i, i ^ step) for i in range(shards)])]
    ppermute x12 -> x15, starting transfers between devices: 14 us -> 18.6 us  [dp_move(): return lax.ppermute(x, 'dp', [(i, i ^ step) for i in range(replicas)])]
  transfers between devices with their start and end apart: 31 -> 27, of which waited for: 16 -> 15; matrix products, arithmetic and copies ran while one was open for 0% -> 0% of each run, Pallas kernels for 14% -> 11%
where the time goes in v3:
time: 132 us
  waiting for transfers between devices  54.6 us (41%)
  Pallas kernels  28.8 us (22%)
  starting transfers between devices  28.7 us (22%)
  blocking collectives  17.5 us (13%)
  local copies, waits for them, and re-layouts  1.42 us (1%)
    ppermute x12, waiting for transfers between devices, context_move(): return lax.ppermute(x, 'context', [(i, i ^ step) for i in range(shards)])  42.2 us
    ppermute x15, starting transfers between devices, dp_move(): return lax.ppermute(x, 'dp', [(i, i ^ step) for i in range(replicas)])  18.6 us
    all_gather x1, blocking collectives, local(): kv_all = lax.all_gather(own_kv, 'context', axis=0, tiled=True)  17.5 us
    ppermute x15, waiting for transfers between devices, dp_move(): return lax.ppermute(x, 'dp', [(i, i ^ step) for i in range(replicas)])  12.4 us
    ppermute x12, starting transfers between devices, context_move(): return lax.ppermute(x, 'context', [(i, i ^ step) for i in range(shards)])  10.1 us
    pallas_call x6, Pallas kernels, partial_weights(): pl.pallas_call(functools.partial(partial_kernel, replicas, firsts, half_s...  9.01 us
    pallas_call x1, Pallas kernels, local(): pl.pallas_call(functools.partial(attend_kernel, shards, heads), out_shape...  6.33 us
    pallas_call x1, Pallas kernels, local(): pl.pallas_call(functools.partial(prepare_kernel, replicas, shards, order)...  6.2 us
  transfers between devices with their start and end apart: 27, of which 15 were waited for; matrix products, arithmetic and copies ran while one was open for 0% of the time, Pallas kernels for 11%

profile of v3, /device:TPU:0, one launch (start us, length us, event | category | flops | bytes accessed | tf_op | source)
XLA Modules:
  0.0 132.1 jit_solution(15451954337622955614)
XLA Ops:
  0.6 6.2 %prepare.1 = (bf16[192,1024]{1,0:T(8,128)(2,1)}, bf16[192,1024]{1,0:T(8,128)(2,1)}, bf16[192,1024]{1,0:T(8,128)(2,1)}, bf16[192,1024]{1,0:T(8,128)(2,1)}, bf16[1...) custom-call(s32[8]{0:T(128)} %pair_ref.1, ...), custom_call_target="tpu_custom_call" | custom-call | flops 4000000 | tf_op jit(solution)/shard_map/prepare/pallas_call | solution.py:364
  6.8 3.0 %collective-permute-start = (bf16[192,1024]{1,0:T(8,128)(2,1)}, bf16[192,1024]{1,0:T(8,128)(2,1)S(1)}, u32[]{:S(2)}, u32[]{:S(2)}) collective-permute-start(bf16[192,1024]{1,0:T(8,128)(2,1)} %get-tuple-element.80), channel_id=1, source_target_pairs={{0,8},{8,0},{16,24},{24,16},{1,9},{9,1},{17,25},{25,17},{2,10},{10... | collective-permute-start | bytes 1179656 | tf_op jit(solution)/shard_map/ppermute | solution.py:347
  9.8 1.5 %collective-permute-start.1 = (bf16[192,1024]{1,0:T(8,128)(2,1)}, bf16[192,1024]{1,0:T(8,128)(2,1)S(1)}, u32[]{:S(2)}, u32[]{:S(2)}) collective-permute-start(bf16[192,1024]{1,0:T(8,128)(2,1)} %get-tuple-element.81), channel_id=1, source_target_pairs={{0,16},{8,24},{16,0},{24,8},{1,17},{9,25},{17,1},{25,9},{2,18},{10... | collective-permute-start | bytes 1179656 | tf_op jit(solution)/shard_map/ppermute | solution.py:347
  11.4 17.5 %all_gather.3.kv_ref = bf16[1536,256]{1,0:T(8,128)(2,1)} all-gather(bf16[192,256]{1,0:T(8,128)(2,1)} %get-tuple-element.72), channel_id=1, replica_groups=mesh['dp'=4,'context'=8] {'context'}, dimensions={0}, use_global_device_ids=true | all-gather | bytes 884736 | tf_op jit(solution)/shard_map/all_gather | solution.py:401
  32.6 6.3 %attend.1 = (bf16[192,1024]{1,0:T(8,128)(2,1)}, f32[4,208,256]{2,1,0:T(8,128)}, bf16[4,208,256]{2,1,0:T(8,128)(2,1)}) custom-call(s32[2,3,17]{2,1,0:T(4,128)} %get-tuple-element.67.order, f32[2,96,256]{2,1,0:T(8,128)} %get-tuple-element.66.rope, s32[2,2,768]{2,1,0:T(2,128)} %get-tuple-element.68.bounds, f32[8,128]{1,0:T(8,128)} %get-tuple-element.69.out_top, ...), custom_call_target="tpu_custom_call" | custom-call | flops 12000000 | tf_op jit(solution)/shard_map/attend/pallas_call | solution.py:406
  38.9 2.9 %collective-permute-done.4.refs_2_.refs_6_ = bf16[192,512]{1,0:T(8,128)(2,1)S(1)} collective-permute-done((bf16[192,512]{1,0:T(8,128)(2,1)}, bf16[192,512]{1,0:T(8,128)(2,1)S(1)}, u32[]{:S(2)}, u32[]{:S(2)}) %collective-permute-start.4) | collective-permute-done | bytes 196640 | tf_op jit(solution)/shard_map/ppermute | solution.py:347
  43.7 2.4 %collective-permute-start.10 = (bf16[192,1024]{1,0:T(8,128)(2,1)}, bf16[192,1024]{1,0:T(8,128)(2,1)S(1)}, u32[]{:S(2)}, u32[]{:S(2)}) collective-permute-start(bf16[192,1024]{1,0:T(8,128)(2,1)} %get-tuple-element.94.refs_4_.gq_ref), channel_id=1, source_target_pairs={{0,16},{8,24},{16,0},{24,8},{1,17},{9,25},{17,1},{25,9},{2,18},{10... | collective-permute-start | bytes 1179656 | tf_op jit(solution)/shard_map/ppermute | solution.py:347
  46.1 2.1 %merge_rows.2 = (f32[2,208,256]{2,1,0:T(8,128)}, bf16[2,208,256]{2,1,0:T(8,128)(2,1)}) custom-call(f32[4,208,256]{2,1,0:T(8,128)} %get-tuple-element.88.keep_ref, bf16[4,208,256]{2,1,0:T(8,128)(2,1)} %collective-permute-done.6.got_ref), custom_call_target="tpu_custom_call" | custom-call | flops 2000000 | tf_op jit(solution)/shard_map/merge_rows/pallas_call | solution.py:436
  49.6 6.1 %collective-permute-done.7.got_ref = bf16[2,208,256]{2,1,0:T(8,128)(2,1)} collective-permute-done((bf16[2,208,256]{2,1,0:T(8,128)(2,1)}, bf16[2,208,256]{2,1,0:T(8,128)(2,1)}, u32[]{:S(2)}, u32[]{:S(2)}) %collective-permute-start.7) | collective-permute-done | bytes 213024 | tf_op jit(solution)/shard_map/ppermute | solution.py:344
  55.7 1.8 %merge_rows.3 = (f32[1,208,256]{2,1,0:T(8,128)}, bf16[1,208,256]{2,1,0:T(8,128)(2,1)}) custom-call(f32[2,208,256]{2,1,0:T(8,128)} %get-tuple-element.90.keep_ref, bf16[2,208,256]{2,1,0:T(8,128)(2,1)} %collective-permute-done.7.got_ref), custom_call_target="tpu_custom_call" | custom-call | flops 2000000 | tf_op jit(solution)/shard_map/merge_rows/pallas_call | solution.py:436
  57.5 1.7 %collective-permute-start.8 = (bf16[1,208,256]{2,1,0:T(8,128)(2,1)}, bf16[1,208,256]{2,1,0:T(8,128)(2,1)S(1)}, u32[]{:S(2)}, u32[]{:S(2)}) collective-permute-start(bf16[1,208,256]{2,1,0:T(8,128)(2,1)} %get-tuple-element.93), channel_id=1, source_target_pairs={{0,4},{1,5},{2,6},{3,7},{4,0},{5,1},{6,2},{7,3},{8,12},{9,13},{10,... | collective-permute-start | bytes 319496 | tf_op jit(solution)/shard_map/ppermute | solution.py:344
  59.2 5.1 %collective-permute-done.10.refs_6_ = bf16[192,1024]{1,0:T(8,128)(2,1)S(1)} collective-permute-done((bf16[192,1024]{1,0:T(8,128)(2,1)}, bf16[192,1024]{1,0:T(8,128)(2,1)S(1)}, u32[]{:S(2)}, u32[]{:S(2)}) %collective-permute-start.10) | collective-permute-done | bytes 393248 | tf_op jit(solution)/shard_map/ppermute | solution.py:347
  65.5 2.3 %weights_other_core.3 = bf16[512,1024]{1,0:T(8,128)(2,1)} custom-call(bf16[192,1024]{1,0:T(8,128)(2,1)S(1)} %copy-done.2, bf16[192,1024]{1,0:T(8,128)(2,1)S(1)} %collective-permute-done.refs_1_, bf16[192,1024]{1,0:T(8,128)(2,1)S(1)} %collective-permute-done.1.refs_2_, bf16[192,1024]{1,0:T(8,128)(2,1)S(1)} %collective-permute-done.2.refs_3_, ...), custom_call_target="tpu_custom_call" | custom-call | flops 2000000 | tf_op jit(solution)/shard_map/weights_other_core/pallas_call | solution.py:453
  67.8 2.1 %finish_rows.1 = (bf16[192,1280]{1,0:T(8,128)(2,1)}, bf16[208,256]{1,0:T(8,128)(2,1)}) custom-call(f32[2,96,256]{2,1,0:T(8,128)} %get-tuple-element.66.rope, bf16[192,1024]{1,0:T(8,128)(2,1)} %get-tuple-element.94.refs_4_.gq_ref, f32[1,208,256]{2,1,0:T(8,128)} %get-tuple-element.98.keep_ref, bf16[1,208,256]{2,1,0:T(8,128)(2,1)} %copy-done.12), custom_call_target="tpu_custom_call" | custom-call | flops 2000000 | tf_op jit(solution)/shard_map/finish_rows/pallas_call | solution.py:485
  70.8 2.6 %weights_own_core.3 = (f32[256,1024]{1,0:T(8,128)S(1)}, bf16[256,1024]{1,0:T(8,128)(2,1)S(1)}) custom-call(bf16[192,1024]{1,0:T(8,128)(2,1)S(1)} %copy-done.2, bf16[192,1024]{1,0:T(8,128)(2,1)S(1)} %collective-permute-done.refs_1_, bf16[192,1024]{1,0:T(8,128)(2,1)S(1)} %collective-permute-done.1.refs_2_, ...), custom_call_target="tpu_custom_call" | custom-call | flops 2000000 | tf_op jit(solution)/shard_map/weights_own_core/pallas_call | solution.py:453
  79.2 10.0 %collective-permute-done.13.refs_1_ = bf16[256,1024]{1,0:T(8,128)(2,1)S(1)} collective-permute-done((bf16[256,1024]{1,0:T(8,128)(2,1)S(1)}, bf16[256,1024]{1,0:T(8,128)(2,1)S(1)}, u32[]{:S(2)}, u32[]{:S(2)}) %collective-permute-start.13) | collective-permute-done | bytes 524320 | tf_op jit(solution)/shard_map/ppermute | solution.py:344
  92.0 1.8 %collective-permute-start.19 = (bf16[256,1024]{1,0:T(8,128)(2,1)S(1)}, bf16[256,1024]{1,0:T(8,128)(2,1)S(1)}, u32[]{:S(2)}, u32[]{:S(2)}) collective-permute-start(bf16[256,1024]{1,0:T(8,128)(2,1)S(1)} %get-tuple-element.119), channel_id=1, source_target_pairs={{0,2},{1,3},{2,0},{3,1},{4,6},{5,7},{6,4},{7,5},{8,10},{9,11},{10,... | collective-permute-start | bytes 1572872 | tf_op jit(solution)/shard_map/ppermute | solution.py:344
  97.4 2.3 %collective-permute-done.21.refs_9_.refs_10_ = bf16[208,256]{1,0:T(8,128)(2,1)S(1)} collective-permute-done((bf16[208,256]{1,0:T(8,128)(2,1)S(1)}, bf16[208,256]{1,0:T(8,128)(2,1)S(1)}, u32[]{:S(2)}, u32[]{:S(2)}) %collective-permute-start.21) | collective-permute-done | bytes 106528 | tf_op jit(solution)/shard_map/ppermute | solution.py:347
  101.6 2.2 %collective-permute-done.14.refs_2_ = bf16[128,1024]{1,0:T(8,128)(2,1)S(1)} collective-permute-done((bf16[128,1024]{1,0:T(8,128)(2,1)S(1)}, bf16[128,1024]{1,0:T(8,128)(2,1)S(1)}, u32[]{:S(2)}, u32[]{:S(2)}) %collective-permute-start.14) | collective-permute-done | bytes 262176 | tf_op jit(solution)/shard_map/ppermute | solution.py:344
  104.7 6.1 %collective-permute-done.19.refs_4_ = bf16[256,1024]{1,0:T(8,128)(2,1)S(1)} collective-permute-done((bf16[256,1024]{1,0:T(8,128)(2,1)S(1)}, bf16[256,1024]{1,0:T(8,128)(2,1)S(1)}, u32[]{:S(2)}, u32[]{:S(2)}) %collective-permute-start.19) | collective-permute-done | bytes 524320 | tf_op jit(solution)/shard_map/ppermute | solution.py:344
  111.7 2.4 %collective-permute-start.20 = (bf16[128,1024]{1,0:T(8,128)(2,1)S(1)}, bf16[128,1024]{1,0:T(8,128)(2,1)S(1)}, u32[]{:S(2)}, u32[]{:S(2)}) collective-permute-start(bf16[128,1024]{1,0:T(8,128)(2,1)S(1)} %fusion.3), channel_id=1, source_target_pairs={{0,4},{1,5},{2,6},{3,7},{4,0},{5,1},{6,2},{7,3},{8,12},{9,13},{10,... | collective-permute-start | bytes 786440 | tf_op jit(solution)/shard_map/ppermute | solution.py:344
  114.1 9.1 %collective-permute-done.25.refs_7_ = bf16[512,256]{1,0:T(8,128)(2,1)S(1)} collective-permute-done((bf16[512,256]{1,0:T(8,128)(2,1)S(1)}, bf16[512,256]{1,0:T(8,128)(2,1)S(1)}, u32[]{:S(2)}, u32[]{:S(2)}) %collective-permute-start.25) | collective-permute-done | bytes 262176 | tf_op jit(solution)/shard_map/ppermute | solution.py:344
  123.5 1.7 %collective-permute-done.20.refs_5_ = bf16[128,1024]{1,0:T(8,128)(2,1)S(1)} collective-permute-done((bf16[128,1024]{1,0:T(8,128)(2,1)S(1)}, bf16[128,1024]{1,0:T(8,128)(2,1)S(1)}, u32[]{:S(2)}, u32[]{:S(2)}) %collective-permute-start.20) | collective-permute-done | bytes 262176 | tf_op jit(solution)/shard_map/ppermute | solution.py:344
  125.2 5.7 %collective-permute-done.26.refs_8_ = bf16[256,256]{1,0:T(8,128)(2,1)S(1)} collective-permute-done((bf16[256,256]{1,0:T(8,128)(2,1)S(1)}, bf16[256,256]{1,0:T(8,128)(2,1)S(1)}, u32[]{:S(2)}, u32[]{:S(2)}) %collective-permute-start.26) | collective-permute-done | bytes 131104 | tf_op jit(solution)/shard_map/ppermute | solution.py:344
  (78 shorter events, 26.5 us)
Async XLA Ops:
  6.8 22.0 %collective-permute-start = (bf16[192,1024]{1,0:T(8,128)(2,1)}, bf16[192,1024]{1,0:T(8,128)(2,1)S(1)}, u32[]{:S(2)}, u32[]{:S(2)}) collective-permute-start(bf16[192,1024]{1,0:T(8,128)(2,1)} %get-tuple-element.80), channel_id=1, source_target_pairs={{0,8},{8,0},{16,24},{24,16},{1,9},{9,1},{17,25},{25,17},{2,10},{10... | collective-permute-start | bytes 1179656 | tf_op jit(solution)/shard_map/ppermute | solution.py:347
  9.8 19.2 %collective-permute-start.1 = (bf16[192,1024]{1,0:T(8,128)(2,1)}, bf16[192,1024]{1,0:T(8,128)(2,1)S(1)}, u32[]{:S(2)}, u32[]{:S(2)}) collective-permute-start(bf16[192,1024]{1,0:T(8,128)(2,1)} %get-tuple-element.81), channel_id=1, source_target_pairs={{0,16},{8,24},{16,0},{24,8},{1,17},{9,25},{17,1},{25,9},{2,18},{10... | collective-permute-start | bytes 1179656 | tf_op jit(solution)/shard_map/ppermute | solution.py:347
  11.4 17.7 %collective-permute-start.2 = (bf16[192,1024]{1,0:T(8,128)(2,1)}, bf16[192,1024]{1,0:T(8,128)(2,1)S(1)}, u32[]{:S(2)}, u32[]{:S(2)}) collective-permute-start(bf16[192,1024]{1,0:T(8,128)(2,1)} %get-tuple-element.82), channel_id=1, source_target_pairs={{0,24},{8,16},{16,8},{24,0},{1,25},{9,17},{17,9},{25,1},{2,26},{10... | collective-permute-start | bytes 1179656 | tf_op jit(solution)/shard_map/ppermute | solution.py:347
  29.1 9.8 %collective-permute-start.3 = (bf16[192,512]{1,0:T(8,128)(2,1)}, bf16[192,512]{1,0:T(8,128)(2,1)S(1)}, u32[]{:S(2)}, u32[]{:S(2)}) collective-permute-start(bf16[192,512]{1,0:T(8,128)(2,1)} %get-tuple-element.84), channel_id=1, source_target_pairs={{0,8},{8,0},{16,24},{24,16},{1,9},{9,1},{17,25},{25,17},{2,10},{10... | collective-permute-start | bytes 589832 | tf_op jit(solution)/shard_map/ppermute | solution.py:347
  30.5 11.3 %collective-permute-start.4 = (bf16[192,512]{1,0:T(8,128)(2,1)}, bf16[192,512]{1,0:T(8,128)(2,1)S(1)}, u32[]{:S(2)}, u32[]{:S(2)}) collective-permute-start(bf16[192,512]{1,0:T(8,128)(2,1)} %get-tuple-element.85), channel_id=1, source_target_pairs={{0,16},{8,24},{16,0},{24,8},{1,17},{9,25},{17,1},{25,9},{2,18},{10... | collective-permute-start | bytes 589832 | tf_op jit(solution)/shard_map/ppermute | solution.py:347
  32.0 9.8 %collective-permute-start.5 = (bf16[192,512]{1,0:T(8,128)(2,1)}, bf16[192,512]{1,0:T(8,128)(2,1)S(1)}, u32[]{:S(2)}, u32[]{:S(2)}) collective-permute-start(bf16[192,512]{1,0:T(8,128)(2,1)} %get-tuple-element.86), channel_id=1, source_target_pairs={{0,24},{8,16},{16,8},{24,0},{1,25},{9,17},{17,9},{25,1},{2,26},{10... | collective-permute-start | bytes 589832 | tf_op jit(solution)/shard_map/ppermute | solution.py:347
  42.5 16.7 %collective-permute-start.9 = (bf16[192,1024]{1,0:T(8,128)(2,1)}, bf16[192,1024]{1,0:T(8,128)(2,1)S(1)}, u32[]{:S(2)}, u32[]{:S(2)}) collective-permute-start(bf16[192,1024]{1,0:T(8,128)(2,1)} %get-tuple-element.94.refs_4_.gq_ref), channel_id=1, source_target_pairs={{0,8},{8,0},{16,24},{24,16},{1,9},{9,1},{17,25},{25,17},{2,10},{10... | collective-permute-start | bytes 1179656 | tf_op jit(solution)/shard_map/ppermute | solution.py:347
  43.7 20.6 %collective-permute-start.10 = (bf16[192,1024]{1,0:T(8,128)(2,1)}, bf16[192,1024]{1,0:T(8,128)(2,1)S(1)}, u32[]{:S(2)}, u32[]{:S(2)}) collective-permute-start(bf16[192,1024]{1,0:T(8,128)(2,1)} %get-tuple-element.94.refs_4_.gq_ref), channel_id=1, source_target_pairs={{0,16},{8,24},{16,0},{24,8},{1,17},{9,25},{17,1},{25,9},{2,18},{10... | collective-permute-start | bytes 1179656 | tf_op jit(solution)/shard_map/ppermute | solution.py:347
  46.1 18.2 %collective-permute-start.11 = (bf16[192,1024]{1,0:T(8,128)(2,1)}, bf16[192,1024]{1,0:T(8,128)(2,1)S(1)}, u32[]{:S(2)}, u32[]{:S(2)}) collective-permute-start(bf16[192,1024]{1,0:T(8,128)(2,1)} %get-tuple-element.94.refs_4_.gq_ref), channel_id=1, source_target_pairs={{0,24},{8,16},{16,8},{24,0},{1,25},{9,17},{17,9},{25,1},{2,26},{10... | collective-permute-start | bytes 1179656 | tf_op jit(solution)/shard_map/ppermute | solution.py:347
  48.2 7.4 %collective-permute-start.7 = (bf16[2,208,256]{2,1,0:T(8,128)(2,1)}, bf16[2,208,256]{2,1,0:T(8,128)(2,1)}, u32[]{:S(2)}, u32[]{:S(2)}) collective-permute-start(bf16[2,208,256]{2,1,0:T(8,128)(2,1)} %get-tuple-element.91), channel_id=1, source_target_pairs={{0,2},{1,3},{2,0},{3,1},{4,6},{5,7},{6,4},{7,5},{8,10},{9,11},{10,... | collective-permute-start | bytes 638984 | tf_op jit(solution)/shard_map/ppermute | solution.py:344
  57.5 7.4 %collective-permute-start.8 = (bf16[1,208,256]{2,1,0:T(8,128)(2,1)}, bf16[1,208,256]{2,1,0:T(8,128)(2,1)S(1)}, u32[]{:S(2)}, u32[]{:S(2)}) collective-permute-start(bf16[1,208,256]{2,1,0:T(8,128)(2,1)} %get-tuple-element.93), channel_id=1, source_target_pairs={{0,4},{1,5},{2,6},{3,7},{4,0},{5,1},{6,2},{7,3},{8,12},{9,13},{10,... | collective-permute-start | bytes 319496 | tf_op jit(solution)/shard_map/ppermute | solution.py:344
  74.7 15.9 %collective-permute-start.18 = (bf16[512,1024]{1,0:T(8,128)(2,1)S(1)}, bf16[512,1024]{1,0:T(8,128)(2,1)S(1)}, u32[]{:S(2)}, u32[]{:S(2)}) collective-permute-start(bf16[512,1024]{1,0:T(8,128)(2,1)S(1)} %weights_other_core.4), channel_id=1, source_target_pairs={{0,1},{1,0},{2,3},{3,2},{4,5},{5,4},{6,7},{7,6},{8,9},{9,8},{10,11... | collective-permute-start | bytes 3145736 | tf_op jit(solution)/shard_map/ppermute | solution.py:344
  74.9 14.3 %collective-permute-start.13 = (bf16[256,1024]{1,0:T(8,128)(2,1)S(1)}, bf16[256,1024]{1,0:T(8,128)(2,1)S(1)}, u32[]{:S(2)}, u32[]{:S(2)}) collective-permute-start(bf16[256,1024]{1,0:T(8,128)(2,1)S(1)} %get-tuple-element.104), channel_id=1, source_target_pairs={{0,2},{1,3},{2,0},{3,1},{4,6},{5,7},{6,4},{7,5},{8,10},{9,11},{10,... | collective-permute-start | bytes 1572872 | tf_op jit(solution)/shard_map/ppermute | solution.py:344
  75.7 15.0 %collective-permute-start.15 = (bf16[192,512]{1,0:T(8,128)(2,1)S(1)}, bf16[192,512]{1,0:T(8,128)(2,1)S(1)}, u32[]{:S(2)}, u32[]{:S(2)}) collective-permute-start(bf16[192,512]{1,0:T(8,128)(2,1)S(1)} %copy-done.15), channel_id=1, source_target_pairs={{0,8},{8,0},{16,24},{24,16},{1,9},{9,1},{17,25},{25,17},{2,10},{10... | collective-permute-start | bytes 589832 | tf_op jit(solution)/shard_map/ppermute | solution.py:347
  77.2 13.5 %collective-permute-start.16 = (bf16[192,512]{1,0:T(8,128)(2,1)S(1)}, bf16[192,512]{1,0:T(8,128)(2,1)S(1)}, u32[]{:S(2)}, u32[]{:S(2)}) collective-permute-start(bf16[192,512]{1,0:T(8,128)(2,1)S(1)} %copy-done.14), channel_id=1, source_target_pairs={{0,16},{8,24},{16,0},{24,8},{1,17},{9,25},{17,1},{25,9},{2,18},{10... | collective-permute-start | bytes 589832 | tf_op jit(solution)/shard_map/ppermute | solution.py:347
  78.0 12.7 %collective-permute-start.17 = (bf16[192,512]{1,0:T(8,128)(2,1)S(1)}, bf16[192,512]{1,0:T(8,128)(2,1)S(1)}, u32[]{:S(2)}, u32[]{:S(2)}) collective-permute-start(bf16[192,512]{1,0:T(8,128)(2,1)S(1)} %copy-done.13), channel_id=1, source_target_pairs={{0,24},{8,16},{16,8},{24,0},{1,25},{9,17},{17,9},{25,1},{2,26},{10... | collective-permute-start | bytes 589832 | tf_op jit(solution)/shard_map/ppermute | solution.py:347
  89.3 14.5 %collective-permute-start.14 = (bf16[128,1024]{1,0:T(8,128)(2,1)S(1)}, bf16[128,1024]{1,0:T(8,128)(2,1)S(1)}, u32[]{:S(2)}, u32[]{:S(2)}) collective-permute-start(bf16[128,1024]{1,0:T(8,128)(2,1)S(1)} %fusion.2), channel_id=1, source_target_pairs={{0,4},{1,5},{2,6},{3,7},{4,0},{5,1},{6,2},{7,3},{8,12},{9,13},{10,... | collective-permute-start | bytes 786440 | tf_op jit(solution)/shard_map/ppermute | solution.py:344
  92.0 18.7 %collective-permute-start.19 = (bf16[256,1024]{1,0:T(8,128)(2,1)S(1)}, bf16[256,1024]{1,0:T(8,128)(2,1)S(1)}, u32[]{:S(2)}, u32[]{:S(2)}) collective-permute-start(bf16[256,1024]{1,0:T(8,128)(2,1)S(1)} %get-tuple-element.119), channel_id=1, source_target_pairs={{0,2},{1,3},{2,0},{3,1},{4,6},{5,7},{6,4},{7,5},{8,10},{9,11},{10,... | collective-permute-start | bytes 1572872 | tf_op jit(solution)/shard_map/ppermute | solution.py:344
  93.9 5.8 %collective-permute-start.21 = (bf16[208,256]{1,0:T(8,128)(2,1)S(1)}, bf16[208,256]{1,0:T(8,128)(2,1)S(1)}, u32[]{:S(2)}, u32[]{:S(2)}) collective-permute-start(bf16[208,256]{1,0:T(8,128)(2,1)S(1)} %copy-done.3), channel_id=1, source_target_pairs={{0,8},{8,0},{16,24},{24,16},{1,9},{9,1},{17,25},{25,17},{2,10},{10... | collective-permute-start | bytes 319496 | tf_op jit(solution)/shard_map/ppermute | solution.py:347
  96.0 5.6 %collective-permute-start.23 = (bf16[208,256]{1,0:T(8,128)(2,1)S(1)}, bf16[208,256]{1,0:T(8,128)(2,1)S(1)}, u32[]{:S(2)}, u32[]{:S(2)}) collective-permute-start(bf16[208,256]{1,0:T(8,128)(2,1)S(1)} %copy-done.3), channel_id=1, source_target_pairs={{0,24},{8,16},{16,8},{24,0},{1,25},{9,17},{17,9},{25,1},{2,26},{10... | collective-permute-start | bytes 319496 | tf_op jit(solution)/shard_map/ppermute | solution.py:347
  104.6 6.2 %collective-permute-start.24 = (bf16[1024,256]{1,0:T(8,128)(2,1)S(1)}, bf16[1024,256]{1,0:T(8,128)(2,1)S(1)}, u32[]{:S(2)}, u32[]{:S(2)}) collective-permute-start(bf16[1024,256]{1,0:T(8,128)(2,1)S(1)} %weights_other_core.5), channel_id=1, source_target_pairs={{0,1},{1,0},{2,3},{3,2},{4,5},{5,4},{6,7},{7,6},{8,9},{9,8},{10,11... | collective-permute-start | bytes 1572872 | tf_op jit(solution)/shard_map/ppermute | solution.py:344
  111.6 11.6 %collective-permute-start.25 = (bf16[512,256]{1,0:T(8,128)(2,1)S(1)}, bf16[512,256]{1,0:T(8,128)(2,1)S(1)}, u32[]{:S(2)}, u32[]{:S(2)}) collective-permute-start(bf16[512,256]{1,0:T(8,128)(2,1)S(1)} %get-tuple-element.126), channel_id=1, source_target_pairs={{0,2},{1,3},{2,0},{3,1},{4,6},{5,7},{6,4},{7,5},{8,10},{9,11},{10,... | collective-permute-start | bytes 786440 | tf_op jit(solution)/shard_map/ppermute | solution.py:344
  111.7 13.5 %collective-permute-start.20 = (bf16[128,1024]{1,0:T(8,128)(2,1)S(1)}, bf16[128,1024]{1,0:T(8,128)(2,1)S(1)}, u32[]{:S(2)}, u32[]{:S(2)}) collective-permute-start(bf16[128,1024]{1,0:T(8,128)(2,1)S(1)} %fusion.3), channel_id=1, source_target_pairs={{0,4},{1,5},{2,6},{3,7},{4,0},{5,1},{6,2},{7,3},{8,12},{9,13},{10,... | collective-permute-start | bytes 786440 | tf_op jit(solution)/shard_map/ppermute | solution.py:344
  123.2 7.6 %collective-permute-start.26 = (bf16[256,256]{1,0:T(8,128)(2,1)S(1)}, bf16[256,256]{1,0:T(8,128)(2,1)S(1)}, u32[]{:S(2)}, u32[]{:S(2)}) collective-permute-start(bf16[256,256]{1,0:T(8,128)(2,1)S(1)} %fusion.5), channel_id=1, source_target_pairs={{0,4},{1,5},{2,6},{3,7},{4,0},{5,1},{6,2},{7,3},{8,12},{9,13},{10,... | collective-permute-start | bytes 393224 | tf_op jit(solution)/shard_map/ppermute | solution.py:344
  (19 other events, 170.2 us)

commit v4 on v3

--- a/solution.py
+++ b/solution.py
@@ -191,14 +191,13 @@
     rows_ref[:, width + head_dim :] = grad_v
 
 
-def partial_kernel(count, firsts, blocks, tile, adds, *refs):
-    groups = len(firsts)
+def partial_kernel(count, groups, blocks, tile, adds, *refs):
     xs, gs = refs[: groups * count], refs[groups * count : (groups + 1) * count]
     rest = refs[(groups + 1) * count :]
     tok_dev = xs[0].shape[0]
     for index in range(blocks * groups):
         block, group = index // groups, index % groups
-        cols = slice((firsts[group] + block) * tile, (firsts[group] + block + 1) * tile)
+        cols = slice(block * tile, (block + 1) * tile)
         total = None
         for x_ref, g_ref in zip(xs[group * count : (group + 1) * count], gs):
             term = lax.dot_general(
@@ -230,28 +229,36 @@
     amax_ref[0] = jnp.where(lane == 0, out_max[:, :2], ds_max[:, :2])
 
 
+def start_packing(replicas, shards, order, rest, refs, sems):
+    rep, me = lax.axis_index("dp"), lax.axis_index("context")
+    places = [(1, place, place - shards // 2) for place in range(shards // 2, shards)]
+    if not rest:
+        places = [(0, place, place) for place in range(shards)]
+        places += [(1, place, shards + place) for place in range(shards // 2)]
+    tile = refs[1].shape[1] // len(places)
+    copies = []
+    for step in range(replicas):
+        for index, (part, place, spot) in enumerate(places):
+            source = ((((rep ^ step) * shards) + (me ^ order[place])) * 2 + part) * tile
+            copy = pltpu.make_async_copy(
+                refs[0].at[:, pl.ds(pl.multiple_of(source, tile), tile)],
+                refs[1 + step].at[:, pl.ds(spot * tile, tile)],
+                sems.at[step, index],
+            )
+            copy.start()
+            copies.append(copy)
+    return copies
+
+
 def prepare_kernel(replicas, shards, order, pair_ref, docs_ref, k_ref, v_ref, table_ref, q_ref, g_ref, *refs):
     rope_sems, sems, x_sems, q_buf, g_buf = refs[-5:]
     x_refs, outs = refs[:-12], refs[-12:-5]
     list_ref, kv_ref, bounds_ref, top_ref, rope_ref, q_cat, g_cat = outs
     x_copies = []
     if x_refs:
-        rep, own = lax.axis_index("dp"), lax.axis_index("context")
-        tile = x_refs[1].shape[1] // shards
-        for step in range(replicas):
-            for place, relative in enumerate(order):
-                block = (rep ^ step) * shards + (own ^ relative)
-                half = place // (shards // 2)
-                spots = ((0, x_refs[1 + step], place), (1, x_refs[1 + (1 + half) * replicas + step], place % (shards // 2)))
-                for part, target, spot in spots:
-                    source = pl.multiple_of((block * 2 + part) * tile, tile)
-                    copy = pltpu.make_async_copy(
-                        x_refs[0].at[:, pl.ds(source, tile)],
-                        target.at[:, pl.ds(spot * tile, tile)],
-                        x_sems.at[part, step, place],
-                    )
-                    copy.start()
-                    x_copies.append(copy)
+        x_copies = start_packing(replicas, shards, order, False, x_refs[: 1 + replicas], x_sems.at[0])
+        rest_refs = (x_refs[0],) + tuple(x_refs[1 + replicas :])
+        x_copies += start_packing(replicas, shards, order, True, rest_refs, x_sems.at[1])
     kv_ref[:, : k_ref.shape[1]] = k_ref[...]
     kv_ref[:, k_ref.shape[1] :] = v_ref[...]
     waits = [pltpu.make_async_copy(q_ref, q_buf, sems.at[0]), pltpu.make_async_copy(g_ref, g_buf, sems.at[1])]
@@ -358,9 +365,8 @@
         struct((2, lanes, head_dim)),
         struct((2, lanes, head_dim)),
     ]
-    x_shapes = [(tok_dev, count * tile) for count in (shards, half_shards, half_shards) for _ in range(replicas)]
     if packs:
-        outs = [struct(shape) for shape in x_shapes] + outs
+        outs = [struct((tok_dev, count * tile)) for count in (shards + half_shards, half_shards) for _ in range(replicas)] + outs
     prepared = pl.pallas_call(
         functools.partial(prepare_kernel, replicas, shards, order),
         out_shape=outs,
@@ -369,7 +375,7 @@
         scratch_shapes=[
             pltpu.SemaphoreType.DMA((2,)),
             pltpu.SemaphoreType.DMA((2,)),
-            pltpu.SemaphoreType.DMA((2, replicas, shards)),
+            pltpu.SemaphoreType.DMA((2, replicas, shards + half_shards)),
             pltpu.VMEM((tok_dev, width), BF16),
             pltpu.VMEM((tok_dev, width), BF16),
         ],
@@ -379,17 +385,16 @@
     )(pair_span, doc_ids, key_rows[0], value_rows[0], table, query_rows[0], out_grads[0], *([layer_input[0]] if packs else []))
     order_list, own_kv, bounds, out_top, rope, q_cats, g_cats = prepared[-7:]
     if packs:
-        columns = [list(prepared[first : first + replicas]) for first in range(0, 3 * replicas, replicas)]
+        x_most, x_rest = list(prepared[:replicas]), list(prepared[replicas : 2 * replicas])
     else:
         me, rep = lax.axis_index("context"), lax.axis_index("dp")
-        columns = [[], [], []]
+        x_most, x_rest = [], []
         for step in range(replicas):
             part = lax.dynamic_slice_in_dim(layer_input[0], (rep ^ step) * shards * slice_rows, shards * slice_rows, 1)
             part = jnp.take(part.reshape(tok_dev, shards, 2, tile), jnp.asarray(order, jnp.int32) ^ me, axis=1)
-            pieces = part[:, :, 0], part[:, :half_shards, 1], part[:, half_shards:, 1]
-            for group, piece in zip(columns, pieces):
-                group.append(piece.reshape(tok_dev, -1))
-    x_first, x_odd, x_even = columns
+            most = jnp.concatenate([part[:, :, 0], part[:, :half_shards, 1]], axis=1)
+            x_most.append(most.reshape(tok_dev, -1))
+            x_rest.append(part[:, half_shards:, 1].reshape(tok_dev, -1))
 
     def tie(value, *others):
         return lax.optimization_barrier((value, others))[0]
@@ -397,9 +402,8 @@
     def exchange(parts):
         return [parts[0]] + [dp_move(parts[step], step) for step in range(1, replicas)]
 
-    x_first = exchange(x_first)
+    x_most = exchange(x_most)
     kv_all = lax.all_gather(own_kv, "context", axis=0, tiled=True)
-    x_odd = exchange(tie(x_odd, kv_all, x_first))
 
     buf = (shards + 1, 2 * span_len, lanes)
     padded = (seq_len + 2 * span_len, head_dim)
@@ -426,7 +430,7 @@
         name="attend",
     )(order_list, rope, bounds, out_top, q_cats, g_cats, kv_all)
 
-    grad_q, send = tie((grad_q, send), x_odd)
+    grad_q, send = tie((grad_q, send), x_most)
     gq = exchange([grad_q] * replicas)
 
     block = (tok_dev + EXTRA, 2 * head_dim)
@@ -438,22 +442,26 @@
             out_shape=[struct((count,) + block, F32), struct((count,) + block)],
             in_specs=[VMEM] * 2,
             out_specs=[VMEM] * 2,
-            cost_estimate=cost(2),
+            compiler_params=params(8),
+        cost_estimate=cost(2),
             name="merge_rows",
         )(keep, got)
         got, step = context_move(send, step), step * 2
 
     def partial_weights(groups, gs, arrived=None):
-        firsts, parts = [first for first, _ in groups], [x for _, xs in groups for x in xs]
+        parts = [x for _, xs in groups for x in xs]
+        block = (tok_dev, half_shards * tile)
+        specs = [pl.BlockSpec(block, lambda i, first=first: (0, first)) for first, xs in groups for _ in xs]
         rows, cols = half_shards * len(groups) * tile, gs[0].shape[1]
         adds = arrived is not None
         out_shape = [struct((rows, cols))]
         if adds:
             out_shape = [struct((rows // 2, cols), F32), struct((rows // 2, cols))]
         result = pl.pallas_call(
-            functools.partial(partial_kernel, replicas, firsts, half_shards, tile, adds),
+            functools.partial(partial_kernel, replicas, len(groups), half_shards, tile, adds),
             out_shape=out_shape,
-            in_specs=[VMEM] * (len(parts) + replicas + adds),
+            grid=(1,),
+            in_specs=specs + [VMEM] * (replicas + adds),
             out_specs=[VMEM] * len(out_shape),
             compiler_params=params(16),
             cost_estimate=cost(2),
@@ -479,7 +487,7 @@
         return terms, sent
 
     gq = tie(gq, keep, got)
-    away = partial_weights([(0, x_first)], gq)
+    away = partial_weights([(0, x_most)], gq)
     arrived = context_move(away, 1)
     keep, got = tie((keep, got), away)
     grad_rows, grad_kv = pl.pallas_call(
@@ -487,22 +495,23 @@
         out_shape=[struct((tok_dev, qkv_width)), struct(block)],
         in_specs=[VMEM] * 4,
         out_specs=[VMEM] * 2,
+        compiler_params=params(8),
         cost_estimate=cost(2),
         name="finish_rows",
     )(rope, grad_q, keep, got)
-    x_even = exchange(tie(x_even, gq))
+    x_rest = exchange(tie(x_rest, gq))
     gkv = exchange([grad_kv] * replicas)
-    kept, sent = partial_weights([(half_shards, x_first)], gq, tie(arrived, grad_kv))
+    kept, sent = partial_weights([(1, x_most)], gq, tie(arrived, grad_kv))
     first = kept, context_move(sent, 2)
-    away = partial_weights([(0, tie(x_odd, sent))], gq)
+    away = partial_weights([(2, tie(x_most, sent))], gq)
     arrived = context_move(away, 1)
     first, sent = last_steps(*first, tile)
-    kept, sent = partial_weights([(0, x_even)], gq, tie(arrived, sent))
+    kept, sent = partial_weights([(0, x_rest)], gq, tie(arrived, sent))
     second = kept, context_move(sent, 2)
-    away = partial_weights([(0, x_first), (0, x_odd)], tie(gkv, sent, first))
+    away = partial_weights([(0, x_most), (2, x_most)], tie(gkv, sent, first))
     arrived = context_move(away, 1)
     second, sent = last_steps(*second, tile)
-    kept, sent = partial_weights([(half_shards, x_first), (0, x_even)], gkv, tie(arrived, sent))
+    kept, sent = partial_weights([(1, x_most), (0, x_rest)], gkv, tie(arrived, sent))
     third = last_steps(kept, context_move(sent, 2), 2 * tile)[0]
     terms = [first, second, third]
     upper, lower, full = slice(0, tile), slice(tile, 2 * tile), slice(0, width)

time: 132 us -> 125 us (0.947)
  Pallas kernels: 28.8 us -> 23.4 us
  waiting for transfers between devices: 54.6 us -> 50.5 us
  starting transfers between devices: 28.7 us -> 31.8 us
    ppermute x12, starting transfers between devices: 10.1 us -> 16.8 us  [context_move(): return lax.ppermute(x, 'context', [(i, i ^ step) for i in range(shards)])]
    pallas_call x2, Pallas kernels: 3.96 us -> 0.13 us  [local(): pl.pallas_call(merge_kernel, out_shape=[struct((count,) + block, F32), st...]
    ppermute x15 -> x12, starting transfers between devices: 18.6 us -> 15 us  [dp_move(): return lax.ppermute(x, 'dp', [(i, i ^ step) for i in range(replicas)])]
    pallas_call x6, Pallas kernels: 9.01 us -> 6.78 us  [partial_weights(): pl.pallas_call(functools.partial(partial_kernel, replicas, len(groups), h...]
    ppermute x15 -> x12, waiting for transfers between devices: 12.4 us -> 10.2 us  [dp_move(): return lax.ppermute(x, 'dp', [(i, i ^ step) for i in range(replicas)])]
    ppermute x12, waiting for transfers between devices: 42.2 us -> 40.2 us  [context_move(): return lax.ppermute(x, 'context', [(i, i ^ step) for i in range(shards)])]
    pallas_call x1, Pallas kernels: 6.33 us -> 7.94 us  [local(): pl.pallas_call(functools.partial(attend_kernel, shards, heads), out_shape...]
  transfers between devices with their start and end apart: 27 -> 24, of which waited for: 15 -> 14; matrix products, arithmetic and copies ran while one was open for 0% -> 0% of each run, Pallas kernels for 11% -> 9%
where the time goes in v4:
time: 125 us
  waiting for transfers between devices  50.5 us (40%)
  starting transfers between devices  31.8 us (25%)
  Pallas kernels  23.4 us (19%)
  blocking collectives  17.5 us (14%)
    ppermute x12, waiting for transfers between devices, context_move(): return lax.ppermute(x, 'context', [(i, i ^ step) for i in range(shards)])  40.2 us
    all_gather x1, blocking collectives, local(): kv_all = lax.all_gather(own_kv, 'context', axis=0, tiled=True)  17.5 us
    ppermute x12, starting transfers between devices, context_move(): return lax.ppermute(x, 'context', [(i, i ^ step) for i in range(shards)])  16.8 us
    ppermute x12, starting transfers between devices, dp_move(): return lax.ppermute(x, 'dp', [(i, i ^ step) for i in range(replicas)])  15 us
    ppermute x12, waiting for transfers between devices, dp_move(): return lax.ppermute(x, 'dp', [(i, i ^ step) for i in range(replicas)])  10.2 us
    pallas_call x1, Pallas kernels, local(): pl.pallas_call(functools.partial(attend_kernel, shards, heads), out_shape...  7.94 us
    pallas_call x6, Pallas kernels, partial_weights(): pl.pallas_call(functools.partial(partial_kernel, replicas, len(groups), h...  6.78 us
    pallas_call x1, Pallas kernels, local(): pl.pallas_call(functools.partial(prepare_kernel, replicas, shards, order)...  6.43 us
  transfers between devices with their start and end apart: 24, of which 14 were waited for; matrix products, arithmetic and copies ran while one was open for 0% of the time, Pallas kernels for 9%

profile of v4, /device:TPU:0, one launch (start us, length us, event | category | flops | bytes accessed | tf_op | source)
XLA Modules:
  0.0 125.4 jit_solution(10146831714781451680)
XLA Ops:
  0.6 6.4 %prepare.1 = (bf16[192,1536]{1,0:T(8,128)(2,1)}, bf16[192,1536]{1,0:T(8,128)(2,1)}, bf16[192,1536]{1,0:T(8,128)(2,1)}, bf16[192,1536]{1,0:T(8,128)(2,1)}, bf16[1...) custom-call(s32[8]{0:T(128)} %pair_ref.1, ...), custom_call_target="tpu_custom_call" | custom-call | flops 4000000 | tf_op jit(solution)/shard_map/prepare/pallas_call | solution.py:370
  7.1 3.0 %collective-permute-start = (bf16[192,1536]{1,0:T(8,128)(2,1)}, bf16[192,1536]{1,0:T(8,128)(2,1)S(1)}, u32[]{:S(2)}, u32[]{:S(2)}) collective-permute-start(bf16[192,1536]{1,0:T(8,128)(2,1)} %get-tuple-element.68), channel_id=1, source_target_pairs={{0,8},{8,0},{16,24},{24,16},{1,9},{9,1},{17,25},{25,17},{2,10},{10... | collective-permute-start | bytes 1769480 | tf_op jit(solution)/shard_map/ppermute | solution.py:354
  10.1 1.5 %collective-permute-start.1 = (bf16[192,1536]{1,0:T(8,128)(2,1)}, bf16[192,1536]{1,0:T(8,128)(2,1)S(1)}, u32[]{:S(2)}, u32[]{:S(2)}) collective-permute-start(bf16[192,1536]{1,0:T(8,128)(2,1)} %get-tuple-element.69), channel_id=1, source_target_pairs={{0,16},{8,24},{16,0},{24,8},{1,17},{9,25},{17,1},{25,9},{2,18},{10... | collective-permute-start | bytes 1769480 | tf_op jit(solution)/shard_map/ppermute | solution.py:354
  11.6 17.5 %all_gather.3.kv_ref = bf16[1536,256]{1,0:T(8,128)(2,1)} all-gather(bf16[192,256]{1,0:T(8,128)(2,1)} %get-tuple-element.64), channel_id=1, replica_groups=mesh['dp'=4,'context'=8] {'context'}, dimensions={0}, use_global_device_ids=true | all-gather | bytes 884736 | tf_op jit(solution)/shard_map/all_gather | solution.py:406
  29.1 7.9 %attend.1 = (bf16[192,1024]{1,0:T(8,128)(2,1)}, f32[4,208,256]{2,1,0:T(8,128)}, bf16[4,208,256]{2,1,0:T(8,128)(2,1)}) custom-call(s32[2,3,17]{2,1,0:T(4,128)} %get-tuple-element.59.order, f32[2,96,256]{2,1,0:T(8,128)} %get-tuple-element.58.rope, s32[2,2,768]{2,1,0:T(2,128)} %get-tuple-element.60.bounds, f32[8,128]{1,0:T(8,128)} %get-tuple-element.61.out_top, ...), custom_call_target="tpu_custom_call" | custom-call | flops 12000000 | tf_op jit(solution)/shard_map/attend/pallas_call | solution.py:410
  39.0 1.5 %collective-permute-start.7 = (bf16[192,1024]{1,0:T(8,128)(2,1)}, bf16[192,1024]{1,0:T(8,128)(2,1)S(1)}, u32[]{:S(2)}, u32[]{:S(2)}) collective-permute-start(bf16[192,1024]{1,0:T(8,128)(2,1)} %get-tuple-element.78.refs_4_.gq_ref), channel_id=1, source_target_pairs={{0,16},{8,24},{16,0},{24,8},{1,17},{9,25},{17,1},{25,9},{2,18},{10... | collective-permute-start | bytes 1179656 | tf_op jit(solution)/shard_map/ppermute | solution.py:354
  40.5 1.4 %collective-permute-start.8 = (bf16[192,1024]{1,0:T(8,128)(2,1)}, bf16[192,1024]{1,0:T(8,128)(2,1)S(1)}, u32[]{:S(2)}, u32[]{:S(2)}) collective-permute-start(bf16[192,1024]{1,0:T(8,128)(2,1)} %get-tuple-element.78.refs_4_.gq_ref), channel_id=1, source_target_pairs={{0,24},{8,16},{16,8},{24,0},{1,25},{9,17},{17,9},{25,1},{2,26},{10... | collective-permute-start | bytes 1179656 | tf_op jit(solution)/shard_map/ppermute | solution.py:354
  44.1 5.5 %collective-permute-done.4.got_ref = bf16[2,208,256]{2,1,0:T(8,128)(2,1)S(1)} collective-permute-done((bf16[2,208,256]{2,1,0:T(8,128)(2,1)S(1)}, bf16[2,208,256]{2,1,0:T(8,128)(2,1)S(1)}, u32[]{:S(2)}, u32[]{:S(2)}) %collective-permute-start.4) | collective-permute-done | bytes 213024 | tf_op jit(solution)/shard_map/ppermute | solution.py:351
  49.6 3.8 %collective-permute-start.5 = (bf16[1,208,256]{2,1,0:T(8,128)(2,1)S(1)}, bf16[1,208,256]{2,1,0:T(8,128)(2,1)S(1)}, u32[]{:S(2)}, u32[]{:S(2)}) collective-permute-start(bf16[1,208,256]{2,1,0:T(8,128)(2,1)S(1)} %get-tuple-element.77), channel_id=1, source_target_pairs={{0,4},{1,5},{2,6},{3,7},{4,0},{5,1},{6,2},{7,3},{8,12},{9,13},{10,... | collective-permute-start | bytes 319496 | tf_op jit(solution)/shard_map/ppermute | solution.py:351
  53.4 4.3 %collective-permute-done.7.refs_6_ = bf16[192,1024]{1,0:T(8,128)(2,1)S(1)} collective-permute-done((bf16[192,1024]{1,0:T(8,128)(2,1)}, bf16[192,1024]{1,0:T(8,128)(2,1)S(1)}, u32[]{:S(2)}, u32[]{:S(2)}) %collective-permute-start.7) | collective-permute-done | bytes 393248 | tf_op jit(solution)/shard_map/ppermute | solution.py:354
  61.1 1.8 %collective-permute-done.9.refs_8_ = bf16[512,1024]{1,0:T(8,128)(2,1)S(1)} collective-permute-done((bf16[512,1024]{1,0:T(8,128)(2,1)S(1)}, bf16[512,1024]{1,0:T(8,128)(2,1)S(1)}, u32[]{:S(2)}, u32[]{:S(2)}) %collective-permute-start.9) | collective-permute-done | bytes 1048608 | tf_op jit(solution)/shard_map/ppermute | solution.py:351
  65.8 1.7 %collective-permute-start.10 = (bf16[256,1024]{1,0:T(8,128)(2,1)S(1)}, bf16[256,1024]{1,0:T(8,128)(2,1)S(1)}, u32[]{:S(2)}, u32[]{:S(2)}) collective-permute-start(bf16[256,1024]{1,0:T(8,128)(2,1)S(1)} %get-tuple-element.88), channel_id=1, source_target_pairs={{0,2},{1,3},{2,0},{3,1},{4,6},{5,7},{6,4},{7,5},{8,10},{9,11},{10,... | collective-permute-start | bytes 1572872 | tf_op jit(solution)/shard_map/ppermute | solution.py:351
  67.5 1.4 %collective-permute-start.12 = (bf16[192,512]{1,0:T(8,128)(2,1)S(1)}, bf16[192,512]{1,0:T(8,128)(2,1)S(1)}, u32[]{:S(2)}, u32[]{:S(2)}) collective-permute-start(bf16[192,512]{1,0:T(8,128)(2,1)S(1)} %copy-done.7), channel_id=1, source_target_pairs={{0,8},{8,0},{16,24},{24,16},{1,9},{9,1},{17,25},{25,17},{2,10},{10... | collective-permute-start | bytes 589832 | tf_op jit(solution)/shard_map/ppermute | solution.py:354
  71.0 9.0 %collective-permute-done.10.refs_1_ = bf16[256,1024]{1,0:T(8,128)(2,1)S(1)} collective-permute-done((bf16[256,1024]{1,0:T(8,128)(2,1)S(1)}, bf16[256,1024]{1,0:T(8,128)(2,1)S(1)}, u32[]{:S(2)}, u32[]{:S(2)}) %collective-permute-start.10) | collective-permute-done | bytes 524320 | tf_op jit(solution)/shard_map/ppermute | solution.py:351
  80.1 4.5 %collective-permute-start.11 = (bf16[128,1024]{1,0:T(8,128)(2,1)S(1)}, bf16[128,1024]{1,0:T(8,128)(2,1)S(1)}, u32[]{:S(2)}, u32[]{:S(2)}) collective-permute-start(bf16[128,1024]{1,0:T(8,128)(2,1)S(1)} %fusion.2), channel_id=1, source_target_pairs={{0,4},{1,5},{2,6},{3,7},{4,0},{5,1},{6,2},{7,3},{8,12},{9,13},{10,... | collective-permute-start | bytes 786440 | tf_op jit(solution)/shard_map/ppermute | solution.py:351
  85.9 1.8 %collective-permute-start.16 = (bf16[256,1024]{1,0:T(8,128)(2,1)S(1)}, bf16[256,1024]{1,0:T(8,128)(2,1)S(1)}, u32[]{:S(2)}, u32[]{:S(2)}) collective-permute-start(bf16[256,1024]{1,0:T(8,128)(2,1)S(1)} %get-tuple-element.103), channel_id=1, source_target_pairs={{0,2},{1,3},{2,0},{3,1},{4,6},{5,7},{6,4},{7,5},{8,10},{9,11},{10,... | collective-permute-start | bytes 1572872 | tf_op jit(solution)/shard_map/ppermute | solution.py:351
  88.1 1.7 %collective-permute-start.19 = (bf16[208,256]{1,0:T(8,128)(2,1)S(1)}, bf16[208,256]{1,0:T(8,128)(2,1)S(1)}, u32[]{:S(2)}, u32[]{:S(2)}) collective-permute-start(bf16[208,256]{1,0:T(8,128)(2,1)S(1)} %get-tuple-element.104.refs_8_.refs_9_), channel_id=1, source_target_pairs={{0,16},{8,24},{16,0},{24,8},{1,17},{9,25},{17,1},{25,9},{2,18},{10... | collective-permute-start | bytes 319496 | tf_op jit(solution)/shard_map/ppermute | solution.py:354
  89.8 1.4 %collective-permute-start.20 = (bf16[208,256]{1,0:T(8,128)(2,1)S(1)}, bf16[208,256]{1,0:T(8,128)(2,1)S(1)}, u32[]{:S(2)}, u32[]{:S(2)}) collective-permute-start(bf16[208,256]{1,0:T(8,128)(2,1)S(1)} %get-tuple-element.104.refs_8_.refs_9_), channel_id=1, source_target_pairs={{0,24},{8,16},{16,8},{24,0},{1,25},{9,17},{17,9},{25,1},{2,26},{10... | collective-permute-start | bytes 319496 | tf_op jit(solution)/shard_map/ppermute | solution.py:354
  91.2 1.6 %collective-permute-done.18.refs_9_.refs_10_ = bf16[208,256]{1,0:T(8,128)(2,1)S(1)} collective-permute-done((bf16[208,256]{1,0:T(8,128)(2,1)S(1)}, bf16[208,256]{1,0:T(8,128)(2,1)S(1)}, u32[]{:S(2)}, u32[]{:S(2)}) %collective-permute-start.18) | collective-permute-done | bytes 106528 | tf_op jit(solution)/shard_map/ppermute | solution.py:354
  93.9 1.5 %collective-permute-done.20.refs_11_.refs_12_ = bf16[208,256]{1,0:T(8,128)(2,1)S(1)} collective-permute-done((bf16[208,256]{1,0:T(8,128)(2,1)S(1)}, bf16[208,256]{1,0:T(8,128)(2,1)S(1)}, u32[]{:S(2)}, u32[]{:S(2)}) %collective-permute-start.20) | collective-permute-done | bytes 106528 | tf_op jit(solution)/shard_map/ppermute | solution.py:354
  97.4 6.4 %collective-permute-done.16.refs_4_ = bf16[256,1024]{1,0:T(8,128)(2,1)S(1)} collective-permute-done((bf16[256,1024]{1,0:T(8,128)(2,1)S(1)}, bf16[256,1024]{1,0:T(8,128)(2,1)S(1)}, u32[]{:S(2)}, u32[]{:S(2)}) %collective-permute-start.16) | collective-permute-done | bytes 524320 | tf_op jit(solution)/shard_map/ppermute | solution.py:351
  104.8 2.8 %collective-permute-start.17 = (bf16[128,1024]{1,0:T(8,128)(2,1)S(1)}, bf16[128,1024]{1,0:T(8,128)(2,1)S(1)}, u32[]{:S(2)}, u32[]{:S(2)}) collective-permute-start(bf16[128,1024]{1,0:T(8,128)(2,1)S(1)} %fusion.3), channel_id=1, source_target_pairs={{0,4},{1,5},{2,6},{3,7},{4,0},{5,1},{6,2},{7,3},{8,12},{9,13},{10,... | collective-permute-start | bytes 786440 | tf_op jit(solution)/shard_map/ppermute | solution.py:351
  107.6 9.3 %collective-permute-done.22.refs_7_ = bf16[512,256]{1,0:T(8,128)(2,1)S(1)} collective-permute-done((bf16[512,256]{1,0:T(8,128)(2,1)S(1)}, bf16[512,256]{1,0:T(8,128)(2,1)S(1)}, u32[]{:S(2)}, u32[]{:S(2)}) %collective-permute-start.22) | collective-permute-done | bytes 262176 | tf_op jit(solution)/shard_map/ppermute | solution.py:351
  118.3 5.8 %collective-permute-done.23.refs_8_ = bf16[256,256]{1,0:T(8,128)(2,1)S(1)} collective-permute-done((bf16[256,256]{1,0:T(8,128)(2,1)S(1)}, bf16[256,256]{1,0:T(8,128)(2,1)S(1)}, u32[]{:S(2)}, u32[]{:S(2)}) %collective-permute-start.23) | collective-permute-done | bytes 131104 | tf_op jit(solution)/shard_map/ppermute | solution.py:351
  (56 shorter events, 20.9 us)
Async XLA Ops:
  7.1 30.0 %collective-permute-start = (bf16[192,1536]{1,0:T(8,128)(2,1)}, bf16[192,1536]{1,0:T(8,128)(2,1)S(1)}, u32[]{:S(2)}, u32[]{:S(2)}) collective-permute-start(bf16[192,1536]{1,0:T(8,128)(2,1)} %get-tuple-element.68), channel_id=1, source_target_pairs={{0,8},{8,0},{16,24},{24,16},{1,9},{9,1},{17,25},{25,17},{2,10},{10... | collective-permute-start | bytes 1769480 | tf_op jit(solution)/shard_map/ppermute | solution.py:354
  10.1 27.6 %collective-permute-start.1 = (bf16[192,1536]{1,0:T(8,128)(2,1)}, bf16[192,1536]{1,0:T(8,128)(2,1)S(1)}, u32[]{:S(2)}, u32[]{:S(2)}) collective-permute-start(bf16[192,1536]{1,0:T(8,128)(2,1)} %get-tuple-element.69), channel_id=1, source_target_pairs={{0,16},{8,24},{16,0},{24,8},{1,17},{9,25},{17,1},{25,9},{2,18},{10... | collective-permute-start | bytes 1769480 | tf_op jit(solution)/shard_map/ppermute | solution.py:354
  11.6 26.1 %collective-permute-start.2 = (bf16[192,1536]{1,0:T(8,128)(2,1)}, bf16[192,1536]{1,0:T(8,128)(2,1)S(1)}, u32[]{:S(2)}, u32[]{:S(2)}) collective-permute-start(bf16[192,1536]{1,0:T(8,128)(2,1)} %get-tuple-element.70), channel_id=1, source_target_pairs={{0,24},{8,16},{16,8},{24,0},{1,25},{9,17},{17,9},{25,1},{2,26},{10... | collective-permute-start | bytes 1769480 | tf_op jit(solution)/shard_map/ppermute | solution.py:354
  37.7 4.2 %collective-permute-start.3 = (bf16[4,208,256]{2,1,0:T(8,128)(2,1)}, bf16[4,208,256]{2,1,0:T(8,128)(2,1)S(1)}, u32[]{:S(2)}, u32[]{:S(2)}) collective-permute-start(bf16[4,208,256]{2,1,0:T(8,128)(2,1)} %get-tuple-element.73), channel_id=1, source_target_pairs={{0,1},{1,0},{2,3},{3,2},{4,5},{5,4},{6,7},{7,6},{8,9},{9,8},{10,11... | collective-permute-start | bytes 1277960 | tf_op jit(solution)/shard_map/ppermute | solution.py:351
  38.4 15.1 %collective-permute-start.6 = (bf16[192,1024]{1,0:T(8,128)(2,1)}, bf16[192,1024]{1,0:T(8,128)(2,1)S(1)}, u32[]{:S(2)}, u32[]{:S(2)}) collective-permute-start(bf16[192,1024]{1,0:T(8,128)(2,1)} %get-tuple-element.78.refs_4_.gq_ref), channel_id=1, source_target_pairs={{0,8},{8,0},{16,24},{24,16},{1,9},{9,1},{17,25},{25,17},{2,10},{10... | collective-permute-start | bytes 1179656 | tf_op jit(solution)/shard_map/ppermute | solution.py:354
  39.0 18.7 %collective-permute-start.7 = (bf16[192,1024]{1,0:T(8,128)(2,1)}, bf16[192,1024]{1,0:T(8,128)(2,1)S(1)}, u32[]{:S(2)}, u32[]{:S(2)}) collective-permute-start(bf16[192,1024]{1,0:T(8,128)(2,1)} %get-tuple-element.78.refs_4_.gq_ref), channel_id=1, source_target_pairs={{0,16},{8,24},{16,0},{24,8},{1,17},{9,25},{17,1},{25,9},{2,18},{10... | collective-permute-start | bytes 1179656 | tf_op jit(solution)/shard_map/ppermute | solution.py:354
  40.5 18.3 %collective-permute-start.8 = (bf16[192,1024]{1,0:T(8,128)(2,1)}, bf16[192,1024]{1,0:T(8,128)(2,1)S(1)}, u32[]{:S(2)}, u32[]{:S(2)}) collective-permute-start(bf16[192,1024]{1,0:T(8,128)(2,1)} %get-tuple-element.78.refs_4_.gq_ref), channel_id=1, source_target_pairs={{0,24},{8,16},{16,8},{24,0},{1,25},{9,17},{17,9},{25,1},{2,26},{10... | collective-permute-start | bytes 1179656 | tf_op jit(solution)/shard_map/ppermute | solution.py:354
  43.1 6.5 %collective-permute-start.4 = (bf16[2,208,256]{2,1,0:T(8,128)(2,1)S(1)}, bf16[2,208,256]{2,1,0:T(8,128)(2,1)S(1)}, u32[]{:S(2)}, u32[]{:S(2)}) collective-permute-start(bf16[2,208,256]{2,1,0:T(8,128)(2,1)S(1)} %get-tuple-element.75), channel_id=1, source_target_pairs={{0,2},{1,3},{2,0},{3,1},{4,6},{5,7},{6,4},{7,5},{8,10},{9,11},{10,... | collective-permute-start | bytes 638984 | tf_op jit(solution)/shard_map/ppermute | solution.py:351
  49.6 9.2 %collective-permute-start.5 = (bf16[1,208,256]{2,1,0:T(8,128)(2,1)S(1)}, bf16[1,208,256]{2,1,0:T(8,128)(2,1)S(1)}, u32[]{:S(2)}, u32[]{:S(2)}) collective-permute-start(bf16[1,208,256]{2,1,0:T(8,128)(2,1)S(1)} %get-tuple-element.77), channel_id=1, source_target_pairs={{0,4},{1,5},{2,6},{3,7},{4,0},{5,1},{6,2},{7,3},{8,12},{9,13},{10,... | collective-permute-start | bytes 319496 | tf_op jit(solution)/shard_map/ppermute | solution.py:351
  60.2 2.7 %collective-permute-start.9 = (bf16[512,1024]{1,0:T(8,128)(2,1)S(1)}, bf16[512,1024]{1,0:T(8,128)(2,1)S(1)}, u32[]{:S(2)}, u32[]{:S(2)}) collective-permute-start(bf16[512,1024]{1,0:T(8,128)(2,1)S(1)} %weights_other_core.3), channel_id=1, source_target_pairs={{0,1},{1,0},{2,3},{3,2},{4,5},{5,4},{6,7},{7,6},{8,9},{9,8},{10,11... | collective-permute-start | bytes 3145736 | tf_op jit(solution)/shard_map/ppermute | solution.py:351
  65.6 19.0 %collective-permute-start.15 = (bf16[512,1024]{1,0:T(8,128)(2,1)S(1)}, bf16[512,1024]{1,0:T(8,128)(2,1)S(1)}, u32[]{:S(2)}, u32[]{:S(2)}) collective-permute-start(bf16[512,1024]{1,0:T(8,128)(2,1)S(1)} %weights_other_core.4), channel_id=1, source_target_pairs={{0,1},{1,0},{2,3},{3,2},{4,5},{5,4},{6,7},{7,6},{8,9},{9,8},{10,11... | collective-permute-start | bytes 3145736 | tf_op jit(solution)/shard_map/ppermute | solution.py:351
  65.8 14.2 %collective-permute-start.10 = (bf16[256,1024]{1,0:T(8,128)(2,1)S(1)}, bf16[256,1024]{1,0:T(8,128)(2,1)S(1)}, u32[]{:S(2)}, u32[]{:S(2)}) collective-permute-start(bf16[256,1024]{1,0:T(8,128)(2,1)S(1)} %get-tuple-element.88), channel_id=1, source_target_pairs={{0,2},{1,3},{2,0},{3,1},{4,6},{5,7},{6,4},{7,5},{8,10},{9,11},{10,... | collective-permute-start | bytes 1572872 | tf_op jit(solution)/shard_map/ppermute | solution.py:351
  67.5 17.1 %collective-permute-start.12 = (bf16[192,512]{1,0:T(8,128)(2,1)S(1)}, bf16[192,512]{1,0:T(8,128)(2,1)S(1)}, u32[]{:S(2)}, u32[]{:S(2)}) collective-permute-start(bf16[192,512]{1,0:T(8,128)(2,1)S(1)} %copy-done.7), channel_id=1, source_target_pairs={{0,8},{8,0},{16,24},{24,16},{1,9},{9,1},{17,25},{25,17},{2,10},{10... | collective-permute-start | bytes 589832 | tf_op jit(solution)/shard_map/ppermute | solution.py:354
  68.9 15.7 %collective-permute-start.13 = (bf16[192,512]{1,0:T(8,128)(2,1)S(1)}, bf16[192,512]{1,0:T(8,128)(2,1)S(1)}, u32[]{:S(2)}, u32[]{:S(2)}) collective-permute-start(bf16[192,512]{1,0:T(8,128)(2,1)S(1)} %copy-done.6), channel_id=1, source_target_pairs={{0,16},{8,24},{16,0},{24,8},{1,17},{9,25},{17,1},{25,9},{2,18},{10... | collective-permute-start | bytes 589832 | tf_op jit(solution)/shard_map/ppermute | solution.py:354
  69.7 14.9 %collective-permute-start.14 = (bf16[192,512]{1,0:T(8,128)(2,1)S(1)}, bf16[192,512]{1,0:T(8,128)(2,1)S(1)}, u32[]{:S(2)}, u32[]{:S(2)}) collective-permute-start(bf16[192,512]{1,0:T(8,128)(2,1)S(1)} %copy-done.5), channel_id=1, source_target_pairs={{0,24},{8,16},{16,8},{24,0},{1,25},{9,17},{17,9},{25,1},{2,26},{10... | collective-permute-start | bytes 589832 | tf_op jit(solution)/shard_map/ppermute | solution.py:354
  80.1 16.5 %collective-permute-start.11 = (bf16[128,1024]{1,0:T(8,128)(2,1)S(1)}, bf16[128,1024]{1,0:T(8,128)(2,1)S(1)}, u32[]{:S(2)}, u32[]{:S(2)}) collective-permute-start(bf16[128,1024]{1,0:T(8,128)(2,1)S(1)} %fusion.2), channel_id=1, source_target_pairs={{0,4},{1,5},{2,6},{3,7},{4,0},{5,1},{6,2},{7,3},{8,12},{9,13},{10,... | collective-permute-start | bytes 786440 | tf_op jit(solution)/shard_map/ppermute | solution.py:351
  85.9 18.0 %collective-permute-start.16 = (bf16[256,1024]{1,0:T(8,128)(2,1)S(1)}, bf16[256,1024]{1,0:T(8,128)(2,1)S(1)}, u32[]{:S(2)}, u32[]{:S(2)}) collective-permute-start(bf16[256,1024]{1,0:T(8,128)(2,1)S(1)} %get-tuple-element.103), channel_id=1, source_target_pairs={{0,2},{1,3},{2,0},{3,1},{4,6},{5,7},{6,4},{7,5},{8,10},{9,11},{10,... | collective-permute-start | bytes 1572872 | tf_op jit(solution)/shard_map/ppermute | solution.py:351
  87.7 5.1 %collective-permute-start.18 = (bf16[208,256]{1,0:T(8,128)(2,1)S(1)}, bf16[208,256]{1,0:T(8,128)(2,1)S(1)}, u32[]{:S(2)}, u32[]{:S(2)}) collective-permute-start(bf16[208,256]{1,0:T(8,128)(2,1)S(1)} %get-tuple-element.104.refs_8_.refs_9_), channel_id=1, source_target_pairs={{0,8},{8,0},{16,24},{24,16},{1,9},{9,1},{17,25},{25,17},{2,10},{10... | collective-permute-start | bytes 319496 | tf_op jit(solution)/shard_map/ppermute | solution.py:354
  88.1 5.8 %collective-permute-start.19 = (bf16[208,256]{1,0:T(8,128)(2,1)S(1)}, bf16[208,256]{1,0:T(8,128)(2,1)S(1)}, u32[]{:S(2)}, u32[]{:S(2)}) collective-permute-start(bf16[208,256]{1,0:T(8,128)(2,1)S(1)} %get-tuple-element.104.refs_8_.refs_9_), channel_id=1, source_target_pairs={{0,16},{8,24},{16,0},{24,8},{1,17},{9,25},{17,1},{25,9},{2,18},{10... | collective-permute-start | bytes 319496 | tf_op jit(solution)/shard_map/ppermute | solution.py:354
  89.8 5.6 %collective-permute-start.20 = (bf16[208,256]{1,0:T(8,128)(2,1)S(1)}, bf16[208,256]{1,0:T(8,128)(2,1)S(1)}, u32[]{:S(2)}, u32[]{:S(2)}) collective-permute-start(bf16[208,256]{1,0:T(8,128)(2,1)S(1)} %get-tuple-element.104.refs_8_.refs_9_), channel_id=1, source_target_pairs={{0,24},{8,16},{16,8},{24,0},{1,25},{9,17},{17,9},{25,1},{2,26},{10... | collective-permute-start | bytes 319496 | tf_op jit(solution)/shard_map/ppermute | solution.py:354
  97.4 6.6 %collective-permute-start.21 = (bf16[1024,256]{1,0:T(8,128)(2,1)S(1)}, bf16[1024,256]{1,0:T(8,128)(2,1)S(1)}, u32[]{:S(2)}, u32[]{:S(2)}) collective-permute-start(bf16[1024,256]{1,0:T(8,128)(2,1)S(1)} %weights_other_core.5), channel_id=1, source_target_pairs={{0,1},{1,0},{2,3},{3,2},{4,5},{5,4},{6,7},{7,6},{8,9},{9,8},{10,11... | collective-permute-start | bytes 1572872 | tf_op jit(solution)/shard_map/ppermute | solution.py:351
  104.8 12.2 %collective-permute-start.22 = (bf16[512,256]{1,0:T(8,128)(2,1)S(1)}, bf16[512,256]{1,0:T(8,128)(2,1)S(1)}, u32[]{:S(2)}, u32[]{:S(2)}) collective-permute-start(bf16[512,256]{1,0:T(8,128)(2,1)S(1)} %get-tuple-element.110), channel_id=1, source_target_pairs={{0,2},{1,3},{2,0},{3,1},{4,6},{5,7},{6,4},{7,5},{8,10},{9,11},{10,... | collective-permute-start | bytes 786440 | tf_op jit(solution)/shard_map/ppermute | solution.py:351
  104.8 13.4 %collective-permute-start.17 = (bf16[128,1024]{1,0:T(8,128)(2,1)S(1)}, bf16[128,1024]{1,0:T(8,128)(2,1)S(1)}, u32[]{:S(2)}, u32[]{:S(2)}) collective-permute-start(bf16[128,1024]{1,0:T(8,128)(2,1)S(1)} %fusion.3), channel_id=1, source_target_pairs={{0,4},{1,5},{2,6},{3,7},{4,0},{5,1},{6,2},{7,3},{8,12},{9,13},{10,... | collective-permute-start | bytes 786440 | tf_op jit(solution)/shard_map/ppermute | solution.py:351
  117.0 7.1 %collective-permute-start.23 = (bf16[256,256]{1,0:T(8,128)(2,1)S(1)}, bf16[256,256]{1,0:T(8,128)(2,1)S(1)}, u32[]{:S(2)}, u32[]{:S(2)}) collective-permute-start(bf16[256,256]{1,0:T(8,128)(2,1)S(1)} %fusion.5), channel_id=1, source_target_pairs={{0,4},{1,5},{2,6},{3,7},{4,0},{5,1},{6,2},{7,3},{8,12},{9,13},{10,... | collective-permute-start | bytes 393224 | tf_op jit(solution)/shard_map/ppermute | solution.py:351
  (8 other events, 87.9 us)

commit v5 on v4

--- a/solution.py
+++ b/solution.py
@@ -13,6 +13,7 @@
 NEG_LARGE = -1e30
 DOC_VALUES = 8
 EXTRA = 16
+GROUP = 3
 F32 = jnp.float32
 BF16 = jnp.bfloat16
 VMEM = pl.BlockSpec(memory_space=pltpu.VMEM)
@@ -73,11 +74,11 @@
     dk_acc[...] = jnp.zeros_like(dk_acc)
     dv_acc[...] = jnp.zeros_like(dv_acc)
     ds_top = jnp.zeros((1, lanes), F32)
-    sub = lax.broadcasted_iota(jnp.int32, (2 * span_len, 1), 0)
+    sub = lax.broadcasted_iota(jnp.int32, (GROUP * span_len, 1), 0)
 
     for half in range(2):
         count = order[half, 2, 0]
-        steps = (count + 1) // 2
+        steps = (count + GROUP - 1) // GROUP
 
         def listing(index, unused):
             source = pl.ds(pl.multiple_of(order[half, 0, index] * span_len, span_len), span_len)
@@ -87,17 +88,19 @@
             return unused
 
         lax.fori_loop(0, count, listing, 0)
-        spare = pl.ds(pl.multiple_of(count * span_len, span_len), span_len)
-        key_list[spare] = jnp.zeros((span_len, head_dim), BF16)
-        value_list[spare] = jnp.zeros((span_len, head_dim), BF16)
+        spare = pl.ds(pl.multiple_of(count * span_len, span_len), (GROUP - 1) * span_len)
+        key_list[spare] = jnp.zeros(((GROUP - 1) * span_len, head_dim), BF16)
+        value_list[spare] = jnp.zeros(((GROUP - 1) * span_len, head_dim), BF16)
         doc_first = bounds[half, 0:1]
         query_pos = bounds[half, 1:2]
         own = pl.ds(half * span_len, span_len)
         q_cat, g_cat = q_cats.at[half], g_cats.at[half]
 
         def score_step(index, top):
-            rows = pl.ds(pl.multiple_of(index * 2 * span_len, 2 * span_len), 2 * span_len)
-            start = jnp.where(sub < span_len, order[half, 1, 2 * index], order[half, 1, 2 * index + 1] - 1)
+            rows = pl.ds(pl.multiple_of(index * GROUP * span_len, span_len), GROUP * span_len)
+            start = order[half, 1, GROUP * index + GROUP - 1] - (GROUP - 1)
+            for part in range(GROUP - 2, -1, -1):
+                start = jnp.where(sub < (part + 1) * span_len, order[half, 1, GROUP * index + part] - part, start)
             key_pos = start * span_len + sub
             scores = lax.dot_general(
                 key_list[rows], q_cat[...], (((1,), (1,)), ((), ())), preferred_element_type=F32
@@ -128,15 +131,15 @@
         dq_acc[...] = jnp.zeros_like(dq_acc)
 
         def grad_step(index, ds_now):
-            rows = pl.ds(pl.multiple_of(index * 2 * span_len, 2 * span_len), 2 * span_len)
+            rows = pl.ds(pl.multiple_of(index * GROUP * span_len, span_len), GROUP * span_len)
             probs = score_buf[index] * inverse
             dscores = probs * (dprob_buf[index] - delta)
             probs_low = probs.astype(BF16)
             ds_low = dscores.astype(BF16)
             grad_v = jnp.dot(probs_low, g_cat[...], preferred_element_type=F32)
             grad_k = jnp.dot(ds_low, q_cat[...], preferred_element_type=F32)
-            for part in range(2):
-                block = pl.ds(pl.multiple_of(order[half, 0, 2 * index + part] * span_len, span_len), span_len)
+            for part in range(GROUP):
+                block = pl.ds(pl.multiple_of(order[half, 0, GROUP * index + part] * span_len, span_len), span_len)
                 own_part = slice(part * span_len, (part + 1) * span_len)
                 dv_acc[block] += grad_v[own_part]
                 dk_acc[block] += grad_k[own_part]
@@ -250,15 +253,18 @@
     return copies
 
 
+def pack_rest_kernel(replicas, shards, order, *refs):
+    for copy in start_packing(replicas, shards, order, True, refs[:-1], refs[-1]):
+        copy.wait()
+
+
 def prepare_kernel(replicas, shards, order, pair_ref, docs_ref, k_ref, v_ref, table_ref, q_ref, g_ref, *refs):
     rope_sems, sems, x_sems, q_buf, g_buf = refs[-5:]
     x_refs, outs = refs[:-12], refs[-12:-5]
     list_ref, kv_ref, bounds_ref, top_ref, rope_ref, q_cat, g_cat = outs
     x_copies = []
     if x_refs:
-        x_copies = start_packing(replicas, shards, order, False, x_refs[: 1 + replicas], x_sems.at[0])
-        rest_refs = (x_refs[0],) + tuple(x_refs[1 + replicas :])
-        x_copies += start_packing(replicas, shards, order, True, rest_refs, x_sems.at[1])
+        x_copies = start_packing(replicas, shards, order, False, x_refs, x_sems)
     kv_ref[:, : k_ref.shape[1]] = k_ref[...]
     kv_ref[:, k_ref.shape[1] :] = v_ref[...]
     waits = [pltpu.make_async_copy(q_ref, q_buf, sems.at[0]), pltpu.make_async_copy(g_ref, g_buf, sems.at[1])]
@@ -297,8 +303,9 @@
 
         count = lax.fori_loop(0, 2 * shards, listing, jnp.int32(0))
         list_ref[half, 2, 0] = count
-        list_ref[half, 0, count] = 2 * shards
-        list_ref[half, 1, count] = 2 * shards
+        for spare in range(GROUP - 1):
+            list_ref[half, 0, count + spare] = 2 * shards
+            list_ref[half, 1, count + spare] = 2 * shards
         query_pos = base + lane_row
         query_f = query_pos.astype(F32)
         doc_start = jnp.zeros((1, lanes), F32)
@@ -357,7 +364,7 @@
         return jax.ShapeDtypeStruct(shape, kind)
 
     outs = [
-        struct((2, 3, 2 * shards + 1), jnp.int32),
+        struct((2, 3, 2 * shards + GROUP), jnp.int32),
         struct((tok_dev, 2 * head_dim)),
         struct((2, 2, lanes), jnp.int32),
         struct((8, head_dim), F32),
@@ -366,7 +373,7 @@
         struct((2, lanes, head_dim)),
     ]
     if packs:
-        outs = [struct((tok_dev, count * tile)) for count in (shards + half_shards, half_shards) for _ in range(replicas)] + outs
+        outs = [struct((tok_dev, (shards + half_shards) * tile))] * replicas + outs
     prepared = pl.pallas_call(
         functools.partial(prepare_kernel, replicas, shards, order),
         out_shape=outs,
@@ -375,7 +382,7 @@
         scratch_shapes=[
             pltpu.SemaphoreType.DMA((2,)),
             pltpu.SemaphoreType.DMA((2,)),
-            pltpu.SemaphoreType.DMA((2, replicas, shards + half_shards)),
+            pltpu.SemaphoreType.DMA((replicas, shards + half_shards)),
             pltpu.VMEM((tok_dev, width), BF16),
             pltpu.VMEM((tok_dev, width), BF16),
         ],
@@ -385,7 +392,7 @@
     )(pair_span, doc_ids, key_rows[0], value_rows[0], table, query_rows[0], out_grads[0], *([layer_input[0]] if packs else []))
     order_list, own_kv, bounds, out_top, rope, q_cats, g_cats = prepared[-7:]
     if packs:
-        x_most, x_rest = list(prepared[:replicas]), list(prepared[replicas : 2 * replicas])
+        x_most = list(prepared[:replicas])
     else:
         me, rep = lax.axis_index("context"), lax.axis_index("dp")
         x_most, x_rest = [], []
@@ -405,8 +412,8 @@
     x_most = exchange(x_most)
     kv_all = lax.all_gather(own_kv, "context", axis=0, tiled=True)
 
-    buf = (shards + 1, 2 * span_len, lanes)
-    padded = (seq_len + 2 * span_len, head_dim)
+    buf = ((2 * shards + GROUP - 1) // GROUP, GROUP * span_len, lanes)
+    padded = (seq_len + GROUP * span_len, head_dim)
     grad_q, keep, send = pl.pallas_call(
         functools.partial(attend_kernel, shards, heads),
         out_shape=[
@@ -432,6 +439,18 @@
 
     grad_q, send = tie((grad_q, send), x_most)
     gq = exchange([grad_q] * replicas)
+    if packs:
+        x_rest = pl.pallas_call(
+            functools.partial(pack_rest_kernel, replicas, shards, order),
+            out_shape=[struct((tok_dev, half_shards * tile))] * replicas,
+            in_specs=[ANY],
+            out_specs=[VMEM] * replicas,
+            scratch_shapes=[pltpu.SemaphoreType.DMA((replicas, half_shards))],
+            compiler_params=params(8),
+            cost_estimate=cost(2),
+            name="pack_rest",
+        )(tie(layer_input[0], send))
+        x_rest = list(x_rest)
 
     block = (tok_dev + EXTRA, 2 * head_dim)
     got, step = context_move(send, 1), 2
@@ -486,7 +505,7 @@
             terms.append(got)
         return terms, sent
 
-    gq = tie(gq, keep, got)
+    gq = tie(gq, keep, got, x_rest)
     away = partial_weights([(0, x_most)], gq)
     arrived = context_move(away, 1)
     keep, got = tie((keep, got), away)
@@ -501,9 +520,9 @@
     )(rope, grad_q, keep, got)
     x_rest = exchange(tie(x_rest, gq))
     gkv = exchange([grad_kv] * replicas)
-    kept, sent = partial_weights([(1, x_most)], gq, tie(arrived, grad_kv))
+    away = partial_weights([(2, tie(x_most, away))], gq)
+    kept, sent = partial_weights([(1, x_most)], gq, tie(arrived, grad_kv, away))
     first = kept, context_move(sent, 2)
-    away = partial_weights([(2, tie(x_most, sent))], gq)
     arrived = context_move(away, 1)
     first, sent = last_steps(*first, tile)
     kept, sent = partial_weights([(0, x_rest)], gq, tie(arrived, sent))

time: 125 us -> 121 us (0.968)
  starting transfers between devices: 31.8 us -> 27.4 us
  waiting for transfers between devices: 50.5 us -> 47.3 us
  local copies, waits for them, and re-layouts: 1.18 us -> 3.06 us
    ppermute x12, starting transfers between devices: 16.8 us -> 12.4 us  [context_move(): return lax.ppermute(x, 'context', [(i, i ^ step) for i in range(shards)])]
    ppermute x12, waiting for transfers between devices: 10.2 us -> 7.93 us  [dp_move(): return lax.ppermute(x, 'dp', [(i, i ^ step) for i in range(replicas)])]
    unnamed x16 -> x10, local copies, waits for them, and re-layouts: 1.18 us -> 3.06 us
    pallas_call x1, Pallas kernels: 7.94 us -> 9.68 us  [local(): pl.pallas_call(functools.partial(attend_kernel, shards, heads), out_shape...]
  transfers between devices with their start and end apart: 24 -> 24, of which waited for: 14 -> 11; matrix products, arithmetic and copies ran while one was open for 0% -> 0% of each run, Pallas kernels for 9% -> 13%
where the time goes in v5:
time: 121 us
  waiting for transfers between devices  47.3 us (39%)
  starting transfers between devices  27.4 us (23%)
  Pallas kernels  24.6 us (20%)
  blocking collectives  17.5 us (14%)
  local copies, waits for them, and re-layouts  3.06 us (3%)
    ppermute x12, waiting for transfers between devices, context_move(): return lax.ppermute(x, 'context', [(i, i ^ step) for i in range(shards)])  39.4 us
    all_gather x1, blocking collectives, local(): kv_all = lax.all_gather(own_kv, 'context', axis=0, tiled=True)  17.5 us
    ppermute x12, starting transfers between devices, dp_move(): return lax.ppermute(x, 'dp', [(i, i ^ step) for i in range(replicas)])  15.1 us
    ppermute x12, starting transfers between devices, context_move(): return lax.ppermute(x, 'context', [(i, i ^ step) for i in range(shards)])  12.4 us
    pallas_call x1, Pallas kernels, local(): pl.pallas_call(functools.partial(attend_kernel, shards, heads), out_shape...  9.68 us
    ppermute x12, waiting for transfers between devices, dp_move(): return lax.ppermute(x, 'dp', [(i, i ^ step) for i in range(replicas)])  7.93 us
    pallas_call x6, Pallas kernels, partial_weights(): pl.pallas_call(functools.partial(partial_kernel, replicas, len(groups), h...  6.8 us
    pallas_call x1, Pallas kernels, local(): pl.pallas_call(functools.partial(prepare_kernel, replicas, shards, order)...  5.44 us
  transfers between devices with their start and end apart: 24, of which 11 were waited for; matrix products, arithmetic and copies ran while one was open for 0% of the time, Pallas kernels for 13%

profile of v5, /device:TPU:0, one launch (start us, length us, event | category | flops | bytes accessed | tf_op | source)
XLA Modules:
  0.0 120.9 jit_solution(1112905604391653912)
XLA Ops:
  0.6 5.4 %prepare.1 = (bf16[192,1536]{1,0:T(8,128)(2,1)}, bf16[192,1536]{1,0:T(8,128)(2,1)}, bf16[192,1536]{1,0:T(8,128)(2,1)}, bf16[192,1536]{1,0:T(8,128)(2,1)}, s32[2,...) custom-call(s32[8]{0:T(128)} %pair_ref.1, ...), custom_call_target="tpu_custom_call" | custom-call | flops 4000000 | tf_op jit(solution)/shard_map/prepare/pallas_call | solution.py:377
  6.1 3.0 %collective-permute-start = (bf16[192,1536]{1,0:T(8,128)(2,1)}, bf16[192,1536]{1,0:T(8,128)(2,1)S(1)}, u32[]{:S(2)}, u32[]{:S(2)}) collective-permute-start(bf16[192,1536]{1,0:T(8,128)(2,1)} %get-tuple-element.69), channel_id=1, source_target_pairs={{0,8},{8,0},{16,24},{24,16},{1,9},{9,1},{17,25},{25,17},{2,10},{10... | collective-permute-start | bytes 1769480 | tf_op jit(solution)/shard_map/ppermute | solution.py:361
  9.1 1.5 %collective-permute-start.1 = (bf16[192,1536]{1,0:T(8,128)(2,1)}, bf16[192,1536]{1,0:T(8,128)(2,1)S(1)}, u32[]{:S(2)}, u32[]{:S(2)}) collective-permute-start(bf16[192,1536]{1,0:T(8,128)(2,1)} %get-tuple-element.70), channel_id=1, source_target_pairs={{0,16},{8,24},{16,0},{24,8},{1,17},{9,25},{17,1},{25,9},{2,18},{10... | collective-permute-start | bytes 1769480 | tf_op jit(solution)/shard_map/ppermute | solution.py:361
  10.6 17.5 %all_gather.3.kv_ref = bf16[1536,256]{1,0:T(8,128)(2,1)} all-gather(bf16[192,256]{1,0:T(8,128)(2,1)} %get-tuple-element.65), channel_id=1, replica_groups=mesh['dp'=4,'context'=8] {'context'}, dimensions={0}, use_global_device_ids=true | all-gather | bytes 884736 | tf_op jit(solution)/shard_map/all_gather | solution.py:413
  28.1 9.7 %attend.1 = (bf16[192,1024]{1,0:T(8,128)(2,1)}, f32[4,208,256]{2,1,0:T(8,128)}, bf16[4,208,256]{2,1,0:T(8,128)(2,1)}) custom-call(s32[2,3,19]{2,1,0:T(4,128)} %get-tuple-element.60.order, f32[2,96,256]{2,1,0:T(8,128)} %get-tuple-element.59.rope, s32[2,2,768]{2,1,0:T(2,128)} %get-tuple-element.61.bounds, f32[8,128]{1,0:T(8,128)} %get-tuple-element.62.out_top, ...), custom_call_target="tpu_custom_call" | custom-call | flops 12000000 | tf_op jit(solution)/shard_map/attend/pallas_call | solution.py:417
  38.3 1.8 %collective-permute-start.7 = (bf16[192,1024]{1,0:T(8,128)(2,1)}, bf16[192,1024]{1,0:T(8,128)(2,1)S(1)}, u32[]{:S(2)}, u32[]{:S(2)}) collective-permute-start(bf16[192,1024]{1,0:T(8,128)(2,1)} %get-tuple-element.84.refs_4_.gq_ref), channel_id=1, source_target_pairs={{0,16},{8,24},{16,0},{24,8},{1,17},{9,25},{17,1},{25,9},{2,18},{10... | collective-permute-start | bytes 1179656 | tf_op jit(solution)/shard_map/ppermute | solution.py:361
  40.1 1.4 %collective-permute-start.8 = (bf16[192,1024]{1,0:T(8,128)(2,1)}, bf16[192,1024]{1,0:T(8,128)(2,1)S(1)}, u32[]{:S(2)}, u32[]{:S(2)}) collective-permute-start(bf16[192,1024]{1,0:T(8,128)(2,1)} %get-tuple-element.84.refs_4_.gq_ref), channel_id=1, source_target_pairs={{0,24},{8,16},{16,8},{24,0},{1,25},{9,17},{17,9},{25,1},{2,26},{10... | collective-permute-start | bytes 1179656 | tf_op jit(solution)/shard_map/ppermute | solution.py:361
  43.1 6.4 %collective-permute-done.4.got_ref = bf16[2,208,256]{2,1,0:T(8,128)(2,1)S(1)} collective-permute-done((bf16[2,208,256]{2,1,0:T(8,128)(2,1)S(1)}, bf16[2,208,256]{2,1,0:T(8,128)(2,1)S(1)}, u32[]{:S(2)}, u32[]{:S(2)}) %collective-permute-start.4) | collective-permute-done | bytes 213024 | tf_op jit(solution)/shard_map/ppermute | solution.py:358
  49.6 2.1 %collective-permute-start.5 = (bf16[1,208,256]{2,1,0:T(8,128)(2,1)S(1)}, bf16[1,208,256]{2,1,0:T(8,128)(2,1)S(1)}, u32[]{:S(2)}, u32[]{:S(2)}) collective-permute-start(bf16[1,208,256]{2,1,0:T(8,128)(2,1)S(1)} %get-tuple-element.78), channel_id=1, source_target_pairs={{0,4},{1,5},{2,6},{3,7},{4,0},{5,1},{6,2},{7,3},{8,12},{9,13},{10,... | collective-permute-start | bytes 319496 | tf_op jit(solution)/shard_map/ppermute | solution.py:358
  51.7 1.9 %copy-done.1 = bf16[1,192,8192]{2,1,0:T(8,128)(2,1)S(1)} copy-done((bf16[1,192,8192]{2,1,0:T(8,128)(2,1)S(1)}, bf16[1,192,8192]{2,1,0:T(8,128)(2,1)}, u32[]{:S(2)}) %copy-start.1) | copy-done | bytes 3145752
  54.0 4.1 %collective-permute-done.7.refs_6_ = bf16[192,1024]{1,0:T(8,128)(2,1)S(1)} collective-permute-done((bf16[192,1024]{1,0:T(8,128)(2,1)}, bf16[192,1024]{1,0:T(8,128)(2,1)S(1)}, u32[]{:S(2)}, u32[]{:S(2)}) %collective-permute-start.7) | collective-permute-done | bytes 393248 | tf_op jit(solution)/shard_map/ppermute | solution.py:361
  63.6 1.4 %collective-permute-start.10 = (bf16[256,1024]{1,0:T(8,128)(2,1)S(1)}, bf16[256,1024]{1,0:T(8,128)(2,1)S(1)}, u32[]{:S(2)}, u32[]{:S(2)}) collective-permute-start(bf16[256,1024]{1,0:T(8,128)(2,1)S(1)} %get-tuple-element.98), channel_id=1, source_target_pairs={{0,2},{1,3},{2,0},{3,1},{4,6},{5,7},{6,4},{7,5},{8,10},{9,11},{10,... | collective-permute-start | bytes 1572872 | tf_op jit(solution)/shard_map/ppermute | solution.py:358
  65.8 1.5 %collective-permute-start.13 = (bf16[192,512]{1,0:T(8,128)(2,1)S(1)}, bf16[192,512]{1,0:T(8,128)(2,1)S(1)}, u32[]{:S(2)}, u32[]{:S(2)}) collective-permute-start(bf16[192,512]{1,0:T(8,128)(2,1)S(1)} %get-tuple-element.101), channel_id=1, source_target_pairs={{0,16},{8,24},{16,0},{24,8},{1,17},{9,25},{17,1},{25,9},{2,18},{10... | collective-permute-start | bytes 589832 | tf_op jit(solution)/shard_map/ppermute | solution.py:361
  68.5 9.0 %collective-permute-done.10.refs_1_ = bf16[256,1024]{1,0:T(8,128)(2,1)S(1)} collective-permute-done((bf16[256,1024]{1,0:T(8,128)(2,1)S(1)}, bf16[256,1024]{1,0:T(8,128)(2,1)S(1)}, u32[]{:S(2)}, u32[]{:S(2)}) %collective-permute-start.10) | collective-permute-done | bytes 524320 | tf_op jit(solution)/shard_map/ppermute | solution.py:358
  77.6 3.2 %collective-permute-start.11 = (bf16[128,1024]{1,0:T(8,128)(2,1)S(1)}, bf16[128,1024]{1,0:T(8,128)(2,1)S(1)}, u32[]{:S(2)}, u32[]{:S(2)}) collective-permute-start(bf16[128,1024]{1,0:T(8,128)(2,1)S(1)} %fusion.2), channel_id=1, source_target_pairs={{0,4},{1,5},{2,6},{3,7},{4,0},{5,1},{6,2},{7,3},{8,12},{9,13},{10,... | collective-permute-start | bytes 786440 | tf_op jit(solution)/shard_map/ppermute | solution.py:358
  82.2 1.8 %collective-permute-start.16 = (bf16[256,1024]{1,0:T(8,128)(2,1)S(1)}, bf16[256,1024]{1,0:T(8,128)(2,1)S(1)}, u32[]{:S(2)}, u32[]{:S(2)}) collective-permute-start(bf16[256,1024]{1,0:T(8,128)(2,1)S(1)} %get-tuple-element.105), channel_id=1, source_target_pairs={{0,2},{1,3},{2,0},{3,1},{4,6},{5,7},{6,4},{7,5},{8,10},{9,11},{10,... | collective-permute-start | bytes 1572872 | tf_op jit(solution)/shard_map/ppermute | solution.py:358
  85.7 1.8 %collective-permute-start.20 = (bf16[208,256]{1,0:T(8,128)(2,1)S(1)}, bf16[208,256]{1,0:T(8,128)(2,1)S(1)}, u32[]{:S(2)}, u32[]{:S(2)}) collective-permute-start(bf16[208,256]{1,0:T(8,128)(2,1)S(1)} %get-tuple-element.106.refs_8_.refs_9_), channel_id=1, source_target_pairs={{0,24},{8,16},{16,8},{24,0},{1,25},{9,17},{17,9},{25,1},{2,26},{10... | collective-permute-start | bytes 319496 | tf_op jit(solution)/shard_map/ppermute | solution.py:361
  87.4 1.5 %collective-permute-done.18.refs_9_.refs_10_ = bf16[208,256]{1,0:T(8,128)(2,1)S(1)} collective-permute-done((bf16[208,256]{1,0:T(8,128)(2,1)S(1)}, bf16[208,256]{1,0:T(8,128)(2,1)S(1)}, u32[]{:S(2)}, u32[]{:S(2)}) %collective-permute-start.18) | collective-permute-done | bytes 106528 | tf_op jit(solution)/shard_map/ppermute | solution.py:361
  89.9 1.4 %collective-permute-done.20.refs_11_.refs_12_ = bf16[208,256]{1,0:T(8,128)(2,1)S(1)} collective-permute-done((bf16[208,256]{1,0:T(8,128)(2,1)S(1)}, bf16[208,256]{1,0:T(8,128)(2,1)S(1)}, u32[]{:S(2)}, u32[]{:S(2)}) %collective-permute-start.20) | collective-permute-done | bytes 106528 | tf_op jit(solution)/shard_map/ppermute | solution.py:361
  93.4 6.5 %collective-permute-done.16.refs_4_ = bf16[256,1024]{1,0:T(8,128)(2,1)S(1)} collective-permute-done((bf16[256,1024]{1,0:T(8,128)(2,1)S(1)}, bf16[256,1024]{1,0:T(8,128)(2,1)S(1)}, u32[]{:S(2)}, u32[]{:S(2)}) %collective-permute-start.16) | collective-permute-done | bytes 524320 | tf_op jit(solution)/shard_map/ppermute | solution.py:358
  100.9 2.5 %collective-permute-start.17 = (bf16[128,1024]{1,0:T(8,128)(2,1)S(1)}, bf16[128,1024]{1,0:T(8,128)(2,1)S(1)}, u32[]{:S(2)}, u32[]{:S(2)}) collective-permute-start(bf16[128,1024]{1,0:T(8,128)(2,1)S(1)} %fusion.3), channel_id=1, source_target_pairs={{0,4},{1,5},{2,6},{3,7},{4,0},{5,1},{6,2},{7,3},{8,12},{9,13},{10,... | collective-permute-start | bytes 786440 | tf_op jit(solution)/shard_map/ppermute | solution.py:358
  103.4 8.9 %collective-permute-done.22.refs_7_ = bf16[512,256]{1,0:T(8,128)(2,1)S(1)} collective-permute-done((bf16[512,256]{1,0:T(8,128)(2,1)S(1)}, bf16[512,256]{1,0:T(8,128)(2,1)S(1)}, u32[]{:S(2)}, u32[]{:S(2)}) %collective-permute-start.22) | collective-permute-done | bytes 262176 | tf_op jit(solution)/shard_map/ppermute | solution.py:358
  112.4 1.6 %collective-permute-done.17.refs_5_ = bf16[128,1024]{1,0:T(8,128)(2,1)S(1)} collective-permute-done((bf16[128,1024]{1,0:T(8,128)(2,1)S(1)}, bf16[128,1024]{1,0:T(8,128)(2,1)S(1)}, u32[]{:S(2)}, u32[]{:S(2)}) %collective-permute-start.17) | collective-permute-done | bytes 262176 | tf_op jit(solution)/shard_map/ppermute | solution.py:358
  114.0 5.7 %collective-permute-done.23.refs_8_ = bf16[256,256]{1,0:T(8,128)(2,1)S(1)} collective-permute-done((bf16[256,256]{1,0:T(8,128)(2,1)S(1)}, bf16[256,256]{1,0:T(8,128)(2,1)S(1)}, u32[]{:S(2)}, u32[]{:S(2)}) %collective-permute-start.23) | collective-permute-done | bytes 131104 | tf_op jit(solution)/shard_map/ppermute | solution.py:358
  (51 shorter events, 18.4 us)
Async XLA Ops:
  6.1 31.7 %collective-permute-start = (bf16[192,1536]{1,0:T(8,128)(2,1)}, bf16[192,1536]{1,0:T(8,128)(2,1)S(1)}, u32[]{:S(2)}, u32[]{:S(2)}) collective-permute-start(bf16[192,1536]{1,0:T(8,128)(2,1)} %get-tuple-element.69), channel_id=1, source_target_pairs={{0,8},{8,0},{16,24},{24,16},{1,9},{9,1},{17,25},{25,17},{2,10},{10... | collective-permute-start | bytes 1769480 | tf_op jit(solution)/shard_map/ppermute | solution.py:361
  9.1 28.7 %collective-permute-start.1 = (bf16[192,1536]{1,0:T(8,128)(2,1)}, bf16[192,1536]{1,0:T(8,128)(2,1)S(1)}, u32[]{:S(2)}, u32[]{:S(2)}) collective-permute-start(bf16[192,1536]{1,0:T(8,128)(2,1)} %get-tuple-element.70), channel_id=1, source_target_pairs={{0,16},{8,24},{16,0},{24,8},{1,17},{9,25},{17,1},{25,9},{2,18},{10... | collective-permute-start | bytes 1769480 | tf_op jit(solution)/shard_map/ppermute | solution.py:361
  10.6 27.2 %collective-permute-start.2 = (bf16[192,1536]{1,0:T(8,128)(2,1)}, bf16[192,1536]{1,0:T(8,128)(2,1)S(1)}, u32[]{:S(2)}, u32[]{:S(2)}) collective-permute-start(bf16[192,1536]{1,0:T(8,128)(2,1)} %get-tuple-element.71), channel_id=1, source_target_pairs={{0,24},{8,16},{16,8},{24,0},{1,25},{9,17},{17,9},{25,1},{2,26},{10... | collective-permute-start | bytes 1769480 | tf_op jit(solution)/shard_map/ppermute | solution.py:361
  37.8 3.6 %collective-permute-start.3 = (bf16[4,208,256]{2,1,0:T(8,128)(2,1)}, bf16[4,208,256]{2,1,0:T(8,128)(2,1)S(1)}, u32[]{:S(2)}, u32[]{:S(2)}) collective-permute-start(bf16[4,208,256]{2,1,0:T(8,128)(2,1)} %get-tuple-element.74), channel_id=1, source_target_pairs={{0,1},{1,0},{2,3},{3,2},{4,5},{5,4},{6,7},{7,6},{8,9},{9,8},{10,11... | collective-permute-start | bytes 1277960 | tf_op jit(solution)/shard_map/ppermute | solution.py:358
  37.9 16.1 %collective-permute-start.6 = (bf16[192,1024]{1,0:T(8,128)(2,1)}, bf16[192,1024]{1,0:T(8,128)(2,1)S(1)}, u32[]{:S(2)}, u32[]{:S(2)}) collective-permute-start(bf16[192,1024]{1,0:T(8,128)(2,1)} %get-tuple-element.84.refs_4_.gq_ref), channel_id=1, source_target_pairs={{0,8},{8,0},{16,24},{24,16},{1,9},{9,1},{17,25},{25,17},{2,10},{10... | collective-permute-start | bytes 1179656 | tf_op jit(solution)/shard_map/ppermute | solution.py:361
  38.3 19.8 %collective-permute-start.7 = (bf16[192,1024]{1,0:T(8,128)(2,1)}, bf16[192,1024]{1,0:T(8,128)(2,1)S(1)}, u32[]{:S(2)}, u32[]{:S(2)}) collective-permute-start(bf16[192,1024]{1,0:T(8,128)(2,1)} %get-tuple-element.84.refs_4_.gq_ref), channel_id=1, source_target_pairs={{0,16},{8,24},{16,0},{24,8},{1,17},{9,25},{17,1},{25,9},{2,18},{10... | collective-permute-start | bytes 1179656 | tf_op jit(solution)/shard_map/ppermute | solution.py:361
  40.1 18.0 %collective-permute-start.8 = (bf16[192,1024]{1,0:T(8,128)(2,1)}, bf16[192,1024]{1,0:T(8,128)(2,1)S(1)}, u32[]{:S(2)}, u32[]{:S(2)}) collective-permute-start(bf16[192,1024]{1,0:T(8,128)(2,1)} %get-tuple-element.84.refs_4_.gq_ref), channel_id=1, source_target_pairs={{0,24},{8,16},{16,8},{24,0},{1,25},{9,17},{17,9},{25,1},{2,26},{10... | collective-permute-start | bytes 1179656 | tf_op jit(solution)/shard_map/ppermute | solution.py:361
  42.7 6.8 %collective-permute-start.4 = (bf16[2,208,256]{2,1,0:T(8,128)(2,1)S(1)}, bf16[2,208,256]{2,1,0:T(8,128)(2,1)S(1)}, u32[]{:S(2)}, u32[]{:S(2)}) collective-permute-start(bf16[2,208,256]{2,1,0:T(8,128)(2,1)S(1)} %get-tuple-element.76), channel_id=1, source_target_pairs={{0,2},{1,3},{2,0},{3,1},{4,6},{5,7},{6,4},{7,5},{8,10},{9,11},{10,... | collective-permute-start | bytes 638984 | tf_op jit(solution)/shard_map/ppermute | solution.py:358
  49.6 8.5 %collective-permute-start.5 = (bf16[1,208,256]{2,1,0:T(8,128)(2,1)S(1)}, bf16[1,208,256]{2,1,0:T(8,128)(2,1)S(1)}, u32[]{:S(2)}, u32[]{:S(2)}) collective-permute-start(bf16[1,208,256]{2,1,0:T(8,128)(2,1)S(1)} %get-tuple-element.78), channel_id=1, source_target_pairs={{0,4},{1,5},{2,6},{3,7},{4,0},{5,1},{6,2},{7,3},{8,12},{9,13},{10,... | collective-permute-start | bytes 319496 | tf_op jit(solution)/shard_map/ppermute | solution.py:358
  59.5 2.8 %collective-permute-start.9 = (bf16[512,1024]{1,0:T(8,128)(2,1)S(1)}, bf16[512,1024]{1,0:T(8,128)(2,1)S(1)}, u32[]{:S(2)}, u32[]{:S(2)}) collective-permute-start(bf16[512,1024]{1,0:T(8,128)(2,1)S(1)} %weights_other_core.3), channel_id=1, source_target_pairs={{0,1},{1,0},{2,3},{3,2},{4,5},{5,4},{6,7},{7,6},{8,9},{9,8},{10,11... | collective-permute-start | bytes 3145736 | tf_op jit(solution)/shard_map/ppermute | solution.py:358
  60.9 20.0 %collective-permute-start.15 = (bf16[512,1024]{1,0:T(8,128)(2,1)S(1)}, bf16[512,1024]{1,0:T(8,128)(2,1)S(1)}, u32[]{:S(2)}, u32[]{:S(2)}) collective-permute-start(bf16[512,1024]{1,0:T(8,128)(2,1)S(1)} %weights_other_core.4), channel_id=1, source_target_pairs={{0,1},{1,0},{2,3},{3,2},{4,5},{5,4},{6,7},{7,6},{8,9},{9,8},{10,11... | collective-permute-start | bytes 3145736 | tf_op jit(solution)/shard_map/ppermute | solution.py:358
  63.6 13.9 %collective-permute-start.10 = (bf16[256,1024]{1,0:T(8,128)(2,1)S(1)}, bf16[256,1024]{1,0:T(8,128)(2,1)S(1)}, u32[]{:S(2)}, u32[]{:S(2)}) collective-permute-start(bf16[256,1024]{1,0:T(8,128)(2,1)S(1)} %get-tuple-element.98), channel_id=1, source_target_pairs={{0,2},{1,3},{2,0},{3,1},{4,6},{5,7},{6,4},{7,5},{8,10},{9,11},{10,... | collective-permute-start | bytes 1572872 | tf_op jit(solution)/shard_map/ppermute | solution.py:358
  65.0 15.8 %collective-permute-start.12 = (bf16[192,512]{1,0:T(8,128)(2,1)S(1)}, bf16[192,512]{1,0:T(8,128)(2,1)S(1)}, u32[]{:S(2)}, u32[]{:S(2)}) collective-permute-start(bf16[192,512]{1,0:T(8,128)(2,1)S(1)} %get-tuple-element.100), channel_id=1, source_target_pairs={{0,8},{8,0},{16,24},{24,16},{1,9},{9,1},{17,25},{25,17},{2,10},{10... | collective-permute-start | bytes 589832 | tf_op jit(solution)/shard_map/ppermute | solution.py:361
  65.8 15.0 %collective-permute-start.13 = (bf16[192,512]{1,0:T(8,128)(2,1)S(1)}, bf16[192,512]{1,0:T(8,128)(2,1)S(1)}, u32[]{:S(2)}, u32[]{:S(2)}) collective-permute-start(bf16[192,512]{1,0:T(8,128)(2,1)S(1)} %get-tuple-element.101), channel_id=1, source_target_pairs={{0,16},{8,24},{16,0},{24,8},{1,17},{9,25},{17,1},{25,9},{2,18},{10... | collective-permute-start | bytes 589832 | tf_op jit(solution)/shard_map/ppermute | solution.py:361
  67.3 13.5 %collective-permute-start.14 = (bf16[192,512]{1,0:T(8,128)(2,1)S(1)}, bf16[192,512]{1,0:T(8,128)(2,1)S(1)}, u32[]{:S(2)}, u32[]{:S(2)}) collective-permute-start(bf16[192,512]{1,0:T(8,128)(2,1)S(1)} %get-tuple-element.102), channel_id=1, source_target_pairs={{0,24},{8,16},{16,8},{24,0},{1,25},{9,17},{17,9},{25,1},{2,26},{10... | collective-permute-start | bytes 589832 | tf_op jit(solution)/shard_map/ppermute | solution.py:361
  77.6 14.9 %collective-permute-start.11 = (bf16[128,1024]{1,0:T(8,128)(2,1)S(1)}, bf16[128,1024]{1,0:T(8,128)(2,1)S(1)}, u32[]{:S(2)}, u32[]{:S(2)}) collective-permute-start(bf16[128,1024]{1,0:T(8,128)(2,1)S(1)} %fusion.2), channel_id=1, source_target_pairs={{0,4},{1,5},{2,6},{3,7},{4,0},{5,1},{6,2},{7,3},{8,12},{9,13},{10,... | collective-permute-start | bytes 786440 | tf_op jit(solution)/shard_map/ppermute | solution.py:358
  82.2 17.8 %collective-permute-start.16 = (bf16[256,1024]{1,0:T(8,128)(2,1)S(1)}, bf16[256,1024]{1,0:T(8,128)(2,1)S(1)}, u32[]{:S(2)}, u32[]{:S(2)}) collective-permute-start(bf16[256,1024]{1,0:T(8,128)(2,1)S(1)} %get-tuple-element.105), channel_id=1, source_target_pairs={{0,2},{1,3},{2,0},{3,1},{4,6},{5,7},{6,4},{7,5},{8,10},{9,11},{10,... | collective-permute-start | bytes 1572872 | tf_op jit(solution)/shard_map/ppermute | solution.py:358
  84.0 5.0 %collective-permute-start.18 = (bf16[208,256]{1,0:T(8,128)(2,1)S(1)}, bf16[208,256]{1,0:T(8,128)(2,1)S(1)}, u32[]{:S(2)}, u32[]{:S(2)}) collective-permute-start(bf16[208,256]{1,0:T(8,128)(2,1)S(1)} %get-tuple-element.106.refs_8_.refs_9_), channel_id=1, source_target_pairs={{0,8},{8,0},{16,24},{24,16},{1,9},{9,1},{17,25},{25,17},{2,10},{10... | collective-permute-start | bytes 319496 | tf_op jit(solution)/shard_map/ppermute | solution.py:361
  84.5 5.3 %collective-permute-start.19 = (bf16[208,256]{1,0:T(8,128)(2,1)S(1)}, bf16[208,256]{1,0:T(8,128)(2,1)S(1)}, u32[]{:S(2)}, u32[]{:S(2)}) collective-permute-start(bf16[208,256]{1,0:T(8,128)(2,1)S(1)} %get-tuple-element.106.refs_8_.refs_9_), channel_id=1, source_target_pairs={{0,16},{8,24},{16,0},{24,8},{1,17},{9,25},{17,1},{25,9},{2,18},{10... | collective-permute-start | bytes 319496 | tf_op jit(solution)/shard_map/ppermute | solution.py:361
  85.7 5.6 %collective-permute-start.20 = (bf16[208,256]{1,0:T(8,128)(2,1)S(1)}, bf16[208,256]{1,0:T(8,128)(2,1)S(1)}, u32[]{:S(2)}, u32[]{:S(2)}) collective-permute-start(bf16[208,256]{1,0:T(8,128)(2,1)S(1)} %get-tuple-element.106.refs_8_.refs_9_), channel_id=1, source_target_pairs={{0,24},{8,16},{16,8},{24,0},{1,25},{9,17},{17,9},{25,1},{2,26},{10... | collective-permute-start | bytes 319496 | tf_op jit(solution)/shard_map/ppermute | solution.py:361
  93.3 6.7 %collective-permute-start.21 = (bf16[1024,256]{1,0:T(8,128)(2,1)S(1)}, bf16[1024,256]{1,0:T(8,128)(2,1)S(1)}, u32[]{:S(2)}, u32[]{:S(2)}) collective-permute-start(bf16[1024,256]{1,0:T(8,128)(2,1)S(1)} %weights_other_core.5), channel_id=1, source_target_pairs={{0,1},{1,0},{2,3},{3,2},{4,5},{5,4},{6,7},{7,6},{8,9},{9,8},{10,11... | collective-permute-start | bytes 1572872 | tf_op jit(solution)/shard_map/ppermute | solution.py:358
  100.8 11.5 %collective-permute-start.22 = (bf16[512,256]{1,0:T(8,128)(2,1)S(1)}, bf16[512,256]{1,0:T(8,128)(2,1)S(1)}, u32[]{:S(2)}, u32[]{:S(2)}) collective-permute-start(bf16[512,256]{1,0:T(8,128)(2,1)S(1)} %get-tuple-element.112), channel_id=1, source_target_pairs={{0,2},{1,3},{2,0},{3,1},{4,6},{5,7},{6,4},{7,5},{8,10},{9,11},{10,... | collective-permute-start | bytes 786440 | tf_op jit(solution)/shard_map/ppermute | solution.py:358
  100.9 13.1 %collective-permute-start.17 = (bf16[128,1024]{1,0:T(8,128)(2,1)S(1)}, bf16[128,1024]{1,0:T(8,128)(2,1)S(1)}, u32[]{:S(2)}, u32[]{:S(2)}) collective-permute-start(bf16[128,1024]{1,0:T(8,128)(2,1)S(1)} %fusion.3), channel_id=1, source_target_pairs={{0,4},{1,5},{2,6},{3,7},{4,0},{5,1},{6,2},{7,3},{8,12},{9,13},{10,... | collective-permute-start | bytes 786440 | tf_op jit(solution)/shard_map/ppermute | solution.py:358
  112.3 7.4 %collective-permute-start.23 = (bf16[256,256]{1,0:T(8,128)(2,1)S(1)}, bf16[256,256]{1,0:T(8,128)(2,1)S(1)}, u32[]{:S(2)}, u32[]{:S(2)}) collective-permute-start(bf16[256,256]{1,0:T(8,128)(2,1)S(1)} %fusion.5), channel_id=1, source_target_pairs={{0,4},{1,5},{2,6},{3,7},{4,0},{5,1},{6,2},{7,3},{8,12},{9,13},{10,... | collective-permute-start | bytes 393224 | tf_op jit(solution)/shard_map/ppermute | solution.py:358
  (5 other events, 18.1 us)

commit v6 on v5

--- a/solution.py
+++ b/solution.py
@@ -418,7 +418,7 @@
         functools.partial(attend_kernel, shards, heads),
         out_shape=[
             struct((tok_dev, width)),
-            struct((shards // 2, tok_dev + EXTRA, 2 * head_dim), F32),
+            struct((shards // 2, tok_dev + EXTRA, 2 * head_dim)),
             struct((shards // 2, tok_dev + EXTRA, 2 * head_dim)),
         ],
         in_specs=[SMEM] + [VMEM] * 6,

time: 121 us -> 122 us (level)
  starting transfers between devices: 27.4 us -> 32.2 us
  waiting for transfers between devices: 47.3 us -> 45.2 us
  Pallas kernels: 24.6 us -> 23.3 us
    ppermute x12, starting transfers between devices: 12.4 us -> 17.2 us  [context_move(): return lax.ppermute(x, 'context', [(i, i ^ step) for i in range(shards)])]
    ppermute x12, waiting for transfers between devices: 39.4 us -> 37.6 us  [context_move(): return lax.ppermute(x, 'context', [(i, i ^ step) for i in range(shards)])]
    pallas_call x1, Pallas kernels: 9.68 us -> 8.34 us  [local(): pl.pallas_call(functools.partial(attend_kernel, shards, heads), out_shape...]
  transfers between devices with their start and end apart: 24 -> 24, of which waited for: 11 -> 13; matrix products, arithmetic and copies ran while one was open for 0% -> 0% of each run, Pallas kernels for 13% -> 12%
where the time goes in v6:
time: 122 us
  waiting for transfers between devices  45.2 us (37%)
  starting transfers between devices  32.2 us (26%)
  Pallas kernels  23.3 us (19%)
  blocking collectives  17.5 us (14%)
  local copies, waits for them, and re-layouts  2.91 us (2%)
    ppermute x12, waiting for transfers between devices, context_move(): return lax.ppermute(x, 'context', [(i, i ^ step) for i in range(shards)])  37.6 us
    all_gather x1, blocking collectives, local(): kv_all = lax.all_gather(own_kv, 'context', axis=0, tiled=True)  17.5 us
    ppermute x12, starting transfers between devices, context_move(): return lax.ppermute(x, 'context', [(i, i ^ step) for i in range(shards)])  17.2 us
    ppermute x12, starting transfers between devices, dp_move(): return lax.ppermute(x, 'dp', [(i, i ^ step) for i in range(replicas)])  15 us
    pallas_call x1, Pallas kernels, local(): pl.pallas_call(functools.partial(attend_kernel, shards, heads), out_shape...  8.34 us
    ppermute x12, waiting for transfers between devices, dp_move(): return lax.ppermute(x, 'dp', [(i, i ^ step) for i in range(replicas)])  7.57 us
    pallas_call x6, Pallas kernels, partial_weights(): pl.pallas_call(functools.partial(partial_kernel, replicas, len(groups), h...  6.8 us
    pallas_call x1, Pallas kernels, local(): pl.pallas_call(functools.partial(prepare_kernel, replicas, shards, order)...  5.43 us
  transfers between devices with their start and end apart: 24, of which 13 were waited for; matrix products, arithmetic and copies ran while one was open for 0% of the time, Pallas kernels for 12%

profile of v6, /device:TPU:0, one launch (start us, length us, event | category | flops | bytes accessed | tf_op | source)
XLA Modules:
  0.0 122.0 jit_solution(5801564750645072986)
XLA Ops:
  0.6 5.4 %prepare.1 = (bf16[192,1536]{1,0:T(8,128)(2,1)}, bf16[192,1536]{1,0:T(8,128)(2,1)}, bf16[192,1536]{1,0:T(8,128)(2,1)}, bf16[192,1536]{1,0:T(8,128)(2,1)}, s32[2,...) custom-call(s32[8]{0:T(128)} %pair_ref.1, ...), custom_call_target="tpu_custom_call" | custom-call | flops 4000000 | tf_op jit(solution)/shard_map/prepare/pallas_call | solution.py:377
  6.1 3.0 %collective-permute-start = (bf16[192,1536]{1,0:T(8,128)(2,1)}, bf16[192,1536]{1,0:T(8,128)(2,1)S(1)}, u32[]{:S(2)}, u32[]{:S(2)}) collective-permute-start(bf16[192,1536]{1,0:T(8,128)(2,1)} %get-tuple-element.69), channel_id=1, source_target_pairs={{0,8},{8,0},{16,24},{24,16},{1,9},{9,1},{17,25},{25,17},{2,10},{10... | collective-permute-start | bytes 1769480 | tf_op jit(solution)/shard_map/ppermute | solution.py:361
  9.1 1.5 %collective-permute-start.1 = (bf16[192,1536]{1,0:T(8,128)(2,1)}, bf16[192,1536]{1,0:T(8,128)(2,1)S(1)}, u32[]{:S(2)}, u32[]{:S(2)}) collective-permute-start(bf16[192,1536]{1,0:T(8,128)(2,1)} %get-tuple-element.70), channel_id=1, source_target_pairs={{0,16},{8,24},{16,0},{24,8},{1,17},{9,25},{17,1},{25,9},{2,18},{10... | collective-permute-start | bytes 1769480 | tf_op jit(solution)/shard_map/ppermute | solution.py:361
  10.6 17.5 %all_gather.3.kv_ref = bf16[1536,256]{1,0:T(8,128)(2,1)} all-gather(bf16[192,256]{1,0:T(8,128)(2,1)} %get-tuple-element.65), channel_id=1, replica_groups=mesh['dp'=4,'context'=8] {'context'}, dimensions={0}, use_global_device_ids=true | all-gather | bytes 884736 | tf_op jit(solution)/shard_map/all_gather | solution.py:413
  28.1 8.3 %attend.1 = (bf16[192,1024]{1,0:T(8,128)(2,1)}, bf16[4,208,256]{2,1,0:T(8,128)(2,1)}, bf16[4,208,256]{2,1,0:T(8,128)(2,1)}) custom-call(s32[2,3,19]{2,1,0:T(4,128)} %get-tuple-element.60.order, f32[2,96,256]{2,1,0:T(8,128)} %get-tuple-element.59.rope, s32[2,2,768]{2,1,0:T(2,128)} %get-tuple-element.61.bounds, f32[8,128]{1,0:T(8,128)} %get-tuple-element.62.out_top, ...), custom_call_target="tpu_custom_call" | custom-call | flops 12000000 | tf_op jit(solution)/shard_map/attend/pallas_call | solution.py:417
  38.8 1.6 %collective-permute-start.8 = (bf16[192,1024]{1,0:T(8,128)(2,1)}, bf16[192,1024]{1,0:T(8,128)(2,1)S(1)}, u32[]{:S(2)}, u32[]{:S(2)}) collective-permute-start(bf16[192,1024]{1,0:T(8,128)(2,1)} %get-tuple-element.84.refs_4_.gq_ref), channel_id=1, source_target_pairs={{0,24},{8,16},{16,8},{24,0},{1,25},{9,17},{17,9},{25,1},{2,26},{10... | collective-permute-start | bytes 1179656 | tf_op jit(solution)/shard_map/ppermute | solution.py:361
  41.5 1.5 %collective-permute-start.4 = (bf16[2,208,256]{2,1,0:T(8,128)(2,1)S(1)}, bf16[2,208,256]{2,1,0:T(8,128)(2,1)S(1)}, u32[]{:S(2)}, u32[]{:S(2)}) collective-permute-start(bf16[2,208,256]{2,1,0:T(8,128)(2,1)S(1)} %get-tuple-element.76), channel_id=1, source_target_pairs={{0,2},{1,3},{2,0},{3,1},{4,6},{5,7},{6,4},{7,5},{8,10},{9,11},{10,... | collective-permute-start | bytes 638984 | tf_op jit(solution)/shard_map/ppermute | solution.py:358
  43.0 5.2 %collective-permute-done.4.got_ref = bf16[2,208,256]{2,1,0:T(8,128)(2,1)S(1)} collective-permute-done((bf16[2,208,256]{2,1,0:T(8,128)(2,1)S(1)}, bf16[2,208,256]{2,1,0:T(8,128)(2,1)S(1)}, u32[]{:S(2)}, u32[]{:S(2)}) %collective-permute-start.4) | collective-permute-done | bytes 213024 | tf_op jit(solution)/shard_map/ppermute | solution.py:358
  48.3 4.1 %collective-permute-start.5 = (bf16[1,208,256]{2,1,0:T(8,128)(2,1)S(1)}, bf16[1,208,256]{2,1,0:T(8,128)(2,1)S(1)}, u32[]{:S(2)}, u32[]{:S(2)}) collective-permute-start(bf16[1,208,256]{2,1,0:T(8,128)(2,1)S(1)} %get-tuple-element.78), channel_id=1, source_target_pairs={{0,4},{1,5},{2,6},{3,7},{4,0},{5,1},{6,2},{7,3},{8,12},{9,13},{10,... | collective-permute-start | bytes 319496 | tf_op jit(solution)/shard_map/ppermute | solution.py:358
  52.4 1.9 %copy-done.1 = bf16[1,192,8192]{2,1,0:T(8,128)(2,1)S(1)} copy-done((bf16[1,192,8192]{2,1,0:T(8,128)(2,1)S(1)}, bf16[1,192,8192]{2,1,0:T(8,128)(2,1)}, u32[]{:S(2)}) %copy-start.1) | copy-done | bytes 3145752
  54.7 1.6 %collective-permute-done.7.refs_6_ = bf16[192,1024]{1,0:T(8,128)(2,1)S(1)} collective-permute-done((bf16[192,1024]{1,0:T(8,128)(2,1)}, bf16[192,1024]{1,0:T(8,128)(2,1)S(1)}, u32[]{:S(2)}, u32[]{:S(2)}) %collective-permute-start.7) | collective-permute-done | bytes 393248 | tf_op jit(solution)/shard_map/ppermute | solution.py:361
  56.3 1.5 %collective-permute-done.8.refs_7_ = bf16[192,1024]{1,0:T(8,128)(2,1)S(1)} collective-permute-done((bf16[192,1024]{1,0:T(8,128)(2,1)}, bf16[192,1024]{1,0:T(8,128)(2,1)S(1)}, u32[]{:S(2)}, u32[]{:S(2)}) %collective-permute-start.8) | collective-permute-done | bytes 393248 | tf_op jit(solution)/shard_map/ppermute | solution.py:361
  63.4 1.6 %collective-permute-start.10 = (bf16[256,1024]{1,0:T(8,128)(2,1)S(1)}, bf16[256,1024]{1,0:T(8,128)(2,1)S(1)}, u32[]{:S(2)}, u32[]{:S(2)}) collective-permute-start(bf16[256,1024]{1,0:T(8,128)(2,1)S(1)} %get-tuple-element.98), channel_id=1, source_target_pairs={{0,2},{1,3},{2,0},{3,1},{4,6},{5,7},{6,4},{7,5},{8,10},{9,11},{10,... | collective-permute-start | bytes 1572872 | tf_op jit(solution)/shard_map/ppermute | solution.py:358
  68.5 8.8 %collective-permute-done.10.refs_1_ = bf16[256,1024]{1,0:T(8,128)(2,1)S(1)} collective-permute-done((bf16[256,1024]{1,0:T(8,128)(2,1)S(1)}, bf16[256,1024]{1,0:T(8,128)(2,1)S(1)}, u32[]{:S(2)}, u32[]{:S(2)}) %collective-permute-start.10) | collective-permute-done | bytes 524320 | tf_op jit(solution)/shard_map/ppermute | solution.py:358
  77.3 4.6 %collective-permute-start.11 = (bf16[128,1024]{1,0:T(8,128)(2,1)S(1)}, bf16[128,1024]{1,0:T(8,128)(2,1)S(1)}, u32[]{:S(2)}, u32[]{:S(2)}) collective-permute-start(bf16[128,1024]{1,0:T(8,128)(2,1)S(1)} %fusion.2), channel_id=1, source_target_pairs={{0,4},{1,5},{2,6},{3,7},{4,0},{5,1},{6,2},{7,3},{8,12},{9,13},{10,... | collective-permute-start | bytes 786440 | tf_op jit(solution)/shard_map/ppermute | solution.py:358
  83.2 1.8 %collective-permute-start.16 = (bf16[256,1024]{1,0:T(8,128)(2,1)S(1)}, bf16[256,1024]{1,0:T(8,128)(2,1)S(1)}, u32[]{:S(2)}, u32[]{:S(2)}) collective-permute-start(bf16[256,1024]{1,0:T(8,128)(2,1)S(1)} %get-tuple-element.105), channel_id=1, source_target_pairs={{0,2},{1,3},{2,0},{3,1},{4,6},{5,7},{6,4},{7,5},{8,10},{9,11},{10,... | collective-permute-start | bytes 1572872 | tf_op jit(solution)/shard_map/ppermute | solution.py:358
  85.4 1.7 %collective-permute-start.19 = (bf16[208,256]{1,0:T(8,128)(2,1)S(1)}, bf16[208,256]{1,0:T(8,128)(2,1)S(1)}, u32[]{:S(2)}, u32[]{:S(2)}) collective-permute-start(bf16[208,256]{1,0:T(8,128)(2,1)S(1)} %get-tuple-element.106.refs_8_.refs_9_), channel_id=1, source_target_pairs={{0,16},{8,24},{16,0},{24,8},{1,17},{9,25},{17,1},{25,9},{2,18},{10... | collective-permute-start | bytes 319496 | tf_op jit(solution)/shard_map/ppermute | solution.py:361
  87.1 1.4 %collective-permute-start.20 = (bf16[208,256]{1,0:T(8,128)(2,1)S(1)}, bf16[208,256]{1,0:T(8,128)(2,1)S(1)}, u32[]{:S(2)}, u32[]{:S(2)}) collective-permute-start(bf16[208,256]{1,0:T(8,128)(2,1)S(1)} %get-tuple-element.106.refs_8_.refs_9_), channel_id=1, source_target_pairs={{0,24},{8,16},{16,8},{24,0},{1,25},{9,17},{17,9},{25,1},{2,26},{10... | collective-permute-start | bytes 319496 | tf_op jit(solution)/shard_map/ppermute | solution.py:361
  91.1 1.6 %collective-permute-done.20.refs_11_.refs_12_ = bf16[208,256]{1,0:T(8,128)(2,1)S(1)} collective-permute-done((bf16[208,256]{1,0:T(8,128)(2,1)S(1)}, bf16[208,256]{1,0:T(8,128)(2,1)S(1)}, u32[]{:S(2)}, u32[]{:S(2)}) %collective-permute-start.20) | collective-permute-done | bytes 106528 | tf_op jit(solution)/shard_map/ppermute | solution.py:361
  94.5 6.5 %collective-permute-done.16.refs_4_ = bf16[256,1024]{1,0:T(8,128)(2,1)S(1)} collective-permute-done((bf16[256,1024]{1,0:T(8,128)(2,1)S(1)}, bf16[256,1024]{1,0:T(8,128)(2,1)S(1)}, u32[]{:S(2)}, u32[]{:S(2)}) %collective-permute-start.16) | collective-permute-done | bytes 524320 | tf_op jit(solution)/shard_map/ppermute | solution.py:358
  101.9 2.5 %collective-permute-start.17 = (bf16[128,1024]{1,0:T(8,128)(2,1)S(1)}, bf16[128,1024]{1,0:T(8,128)(2,1)S(1)}, u32[]{:S(2)}, u32[]{:S(2)}) collective-permute-start(bf16[128,1024]{1,0:T(8,128)(2,1)S(1)} %fusion.3), channel_id=1, source_target_pairs={{0,4},{1,5},{2,6},{3,7},{4,0},{5,1},{6,2},{7,3},{8,12},{9,13},{10,... | collective-permute-start | bytes 786440 | tf_op jit(solution)/shard_map/ppermute | solution.py:358
  104.5 8.9 %collective-permute-done.22.refs_7_ = bf16[512,256]{1,0:T(8,128)(2,1)S(1)} collective-permute-done((bf16[512,256]{1,0:T(8,128)(2,1)S(1)}, bf16[512,256]{1,0:T(8,128)(2,1)S(1)}, u32[]{:S(2)}, u32[]{:S(2)}) %collective-permute-start.22) | collective-permute-done | bytes 262176 | tf_op jit(solution)/shard_map/ppermute | solution.py:358
  113.4 1.6 %collective-permute-done.17.refs_5_ = bf16[128,1024]{1,0:T(8,128)(2,1)S(1)} collective-permute-done((bf16[128,1024]{1,0:T(8,128)(2,1)S(1)}, bf16[128,1024]{1,0:T(8,128)(2,1)S(1)}, u32[]{:S(2)}, u32[]{:S(2)}) %collective-permute-start.17) | collective-permute-done | bytes 262176 | tf_op jit(solution)/shard_map/ppermute | solution.py:358
  115.1 5.7 %collective-permute-done.23.refs_8_ = bf16[256,256]{1,0:T(8,128)(2,1)S(1)} collective-permute-done((bf16[256,256]{1,0:T(8,128)(2,1)S(1)}, bf16[256,256]{1,0:T(8,128)(2,1)S(1)}, u32[]{:S(2)}, u32[]{:S(2)}) %collective-permute-start.23) | collective-permute-done | bytes 131104 | tf_op jit(solution)/shard_map/ppermute | solution.py:358
  (51 shorter events, 21.2 us)
Async XLA Ops:
  6.1 30.4 %collective-permute-start = (bf16[192,1536]{1,0:T(8,128)(2,1)}, bf16[192,1536]{1,0:T(8,128)(2,1)S(1)}, u32[]{:S(2)}, u32[]{:S(2)}) collective-permute-start(bf16[192,1536]{1,0:T(8,128)(2,1)} %get-tuple-element.69), channel_id=1, source_target_pairs={{0,8},{8,0},{16,24},{24,16},{1,9},{9,1},{17,25},{25,17},{2,10},{10... | collective-permute-start | bytes 1769480 | tf_op jit(solution)/shard_map/ppermute | solution.py:361
  9.1 27.6 %collective-permute-start.1 = (bf16[192,1536]{1,0:T(8,128)(2,1)}, bf16[192,1536]{1,0:T(8,128)(2,1)S(1)}, u32[]{:S(2)}, u32[]{:S(2)}) collective-permute-start(bf16[192,1536]{1,0:T(8,128)(2,1)} %get-tuple-element.70), channel_id=1, source_target_pairs={{0,16},{8,24},{16,0},{24,8},{1,17},{9,25},{17,1},{25,9},{2,18},{10... | collective-permute-start | bytes 1769480 | tf_op jit(solution)/shard_map/ppermute | solution.py:361
  10.6 26.1 %collective-permute-start.2 = (bf16[192,1536]{1,0:T(8,128)(2,1)}, bf16[192,1536]{1,0:T(8,128)(2,1)S(1)}, u32[]{:S(2)}, u32[]{:S(2)}) collective-permute-start(bf16[192,1536]{1,0:T(8,128)(2,1)} %get-tuple-element.71), channel_id=1, source_target_pairs={{0,24},{8,16},{16,8},{24,0},{1,25},{9,17},{17,9},{25,1},{2,26},{10... | collective-permute-start | bytes 1769480 | tf_op jit(solution)/shard_map/ppermute | solution.py:361
  36.7 3.7 %collective-permute-start.3 = (bf16[4,208,256]{2,1,0:T(8,128)(2,1)}, bf16[4,208,256]{2,1,0:T(8,128)(2,1)S(1)}, u32[]{:S(2)}, u32[]{:S(2)}) collective-permute-start(bf16[4,208,256]{2,1,0:T(8,128)(2,1)} %get-tuple-element.74), channel_id=1, source_target_pairs={{0,1},{1,0},{2,3},{3,2},{4,5},{5,4},{6,7},{7,6},{8,9},{9,8},{10,11... | collective-permute-start | bytes 1277960 | tf_op jit(solution)/shard_map/ppermute | solution.py:358
  36.9 17.9 %collective-permute-start.6 = (bf16[192,1024]{1,0:T(8,128)(2,1)}, bf16[192,1024]{1,0:T(8,128)(2,1)S(1)}, u32[]{:S(2)}, u32[]{:S(2)}) collective-permute-start(bf16[192,1024]{1,0:T(8,128)(2,1)} %get-tuple-element.84.refs_4_.gq_ref), channel_id=1, source_target_pairs={{0,8},{8,0},{16,24},{24,16},{1,9},{9,1},{17,25},{25,17},{2,10},{10... | collective-permute-start | bytes 1179656 | tf_op jit(solution)/shard_map/ppermute | solution.py:361
  38.0 18.4 %collective-permute-start.7 = (bf16[192,1024]{1,0:T(8,128)(2,1)}, bf16[192,1024]{1,0:T(8,128)(2,1)S(1)}, u32[]{:S(2)}, u32[]{:S(2)}) collective-permute-start(bf16[192,1024]{1,0:T(8,128)(2,1)} %get-tuple-element.84.refs_4_.gq_ref), channel_id=1, source_target_pairs={{0,16},{8,24},{16,0},{24,8},{1,17},{9,25},{17,1},{25,9},{2,18},{10... | collective-permute-start | bytes 1179656 | tf_op jit(solution)/shard_map/ppermute | solution.py:361
  38.8 19.1 %collective-permute-start.8 = (bf16[192,1024]{1,0:T(8,128)(2,1)}, bf16[192,1024]{1,0:T(8,128)(2,1)S(1)}, u32[]{:S(2)}, u32[]{:S(2)}) collective-permute-start(bf16[192,1024]{1,0:T(8,128)(2,1)} %get-tuple-element.84.refs_4_.gq_ref), channel_id=1, source_target_pairs={{0,24},{8,16},{16,8},{24,0},{1,25},{9,17},{17,9},{25,1},{2,26},{10... | collective-permute-start | bytes 1179656 | tf_op jit(solution)/shard_map/ppermute | solution.py:361
  41.5 6.7 %collective-permute-start.4 = (bf16[2,208,256]{2,1,0:T(8,128)(2,1)S(1)}, bf16[2,208,256]{2,1,0:T(8,128)(2,1)S(1)}, u32[]{:S(2)}, u32[]{:S(2)}) collective-permute-start(bf16[2,208,256]{2,1,0:T(8,128)(2,1)S(1)} %get-tuple-element.76), channel_id=1, source_target_pairs={{0,2},{1,3},{2,0},{3,1},{4,6},{5,7},{6,4},{7,5},{8,10},{9,11},{10,... | collective-permute-start | bytes 638984 | tf_op jit(solution)/shard_map/ppermute | solution.py:358
  48.3 9.6 %collective-permute-start.5 = (bf16[1,208,256]{2,1,0:T(8,128)(2,1)S(1)}, bf16[1,208,256]{2,1,0:T(8,128)(2,1)S(1)}, u32[]{:S(2)}, u32[]{:S(2)}) collective-permute-start(bf16[1,208,256]{2,1,0:T(8,128)(2,1)S(1)} %get-tuple-element.78), channel_id=1, source_target_pairs={{0,4},{1,5},{2,6},{3,7},{4,0},{5,1},{6,2},{7,3},{8,12},{9,13},{10,... | collective-permute-start | bytes 319496 | tf_op jit(solution)/shard_map/ppermute | solution.py:358
  59.2 2.8 %collective-permute-start.9 = (bf16[512,1024]{1,0:T(8,128)(2,1)S(1)}, bf16[512,1024]{1,0:T(8,128)(2,1)S(1)}, u32[]{:S(2)}, u32[]{:S(2)}) collective-permute-start(bf16[512,1024]{1,0:T(8,128)(2,1)S(1)} %weights_other_core.3), channel_id=1, source_target_pairs={{0,1},{1,0},{2,3},{3,2},{4,5},{5,4},{6,7},{7,6},{8,9},{9,8},{10,11... | collective-permute-start | bytes 3145736 | tf_op jit(solution)/shard_map/ppermute | solution.py:358
  60.6 21.3 %collective-permute-start.15 = (bf16[512,1024]{1,0:T(8,128)(2,1)S(1)}, bf16[512,1024]{1,0:T(8,128)(2,1)S(1)}, u32[]{:S(2)}, u32[]{:S(2)}) collective-permute-start(bf16[512,1024]{1,0:T(8,128)(2,1)S(1)} %weights_other_core.4), channel_id=1, source_target_pairs={{0,1},{1,0},{2,3},{3,2},{4,5},{5,4},{6,7},{7,6},{8,9},{9,8},{10,11... | collective-permute-start | bytes 3145736 | tf_op jit(solution)/shard_map/ppermute | solution.py:358
  63.4 13.9 %collective-permute-start.10 = (bf16[256,1024]{1,0:T(8,128)(2,1)S(1)}, bf16[256,1024]{1,0:T(8,128)(2,1)S(1)}, u32[]{:S(2)}, u32[]{:S(2)}) collective-permute-start(bf16[256,1024]{1,0:T(8,128)(2,1)S(1)} %get-tuple-element.98), channel_id=1, source_target_pairs={{0,2},{1,3},{2,0},{3,1},{4,6},{5,7},{6,4},{7,5},{8,10},{9,11},{10,... | collective-permute-start | bytes 1572872 | tf_op jit(solution)/shard_map/ppermute | solution.py:358
  65.0 16.9 %collective-permute-start.12 = (bf16[192,512]{1,0:T(8,128)(2,1)S(1)}, bf16[192,512]{1,0:T(8,128)(2,1)S(1)}, u32[]{:S(2)}, u32[]{:S(2)}) collective-permute-start(bf16[192,512]{1,0:T(8,128)(2,1)S(1)} %get-tuple-element.100), channel_id=1, source_target_pairs={{0,8},{8,0},{16,24},{24,16},{1,9},{9,1},{17,25},{25,17},{2,10},{10... | collective-permute-start | bytes 589832 | tf_op jit(solution)/shard_map/ppermute | solution.py:361
  66.0 15.9 %collective-permute-start.13 = (bf16[192,512]{1,0:T(8,128)(2,1)S(1)}, bf16[192,512]{1,0:T(8,128)(2,1)S(1)}, u32[]{:S(2)}, u32[]{:S(2)}) collective-permute-start(bf16[192,512]{1,0:T(8,128)(2,1)S(1)} %get-tuple-element.101), channel_id=1, source_target_pairs={{0,16},{8,24},{16,0},{24,8},{1,17},{9,25},{17,1},{25,9},{2,18},{10... | collective-permute-start | bytes 589832 | tf_op jit(solution)/shard_map/ppermute | solution.py:361
  67.3 14.6 %collective-permute-start.14 = (bf16[192,512]{1,0:T(8,128)(2,1)S(1)}, bf16[192,512]{1,0:T(8,128)(2,1)S(1)}, u32[]{:S(2)}, u32[]{:S(2)}) collective-permute-start(bf16[192,512]{1,0:T(8,128)(2,1)S(1)} %get-tuple-element.102), channel_id=1, source_target_pairs={{0,24},{8,16},{16,8},{24,0},{1,25},{9,17},{17,9},{25,1},{2,26},{10... | collective-permute-start | bytes 589832 | tf_op jit(solution)/shard_map/ppermute | solution.py:361
  77.3 16.3 %collective-permute-start.11 = (bf16[128,1024]{1,0:T(8,128)(2,1)S(1)}, bf16[128,1024]{1,0:T(8,128)(2,1)S(1)}, u32[]{:S(2)}, u32[]{:S(2)}) collective-permute-start(bf16[128,1024]{1,0:T(8,128)(2,1)S(1)} %fusion.2), channel_id=1, source_target_pairs={{0,4},{1,5},{2,6},{3,7},{4,0},{5,1},{6,2},{7,3},{8,12},{9,13},{10,... | collective-permute-start | bytes 786440 | tf_op jit(solution)/shard_map/ppermute | solution.py:358
  83.2 17.8 %collective-permute-start.16 = (bf16[256,1024]{1,0:T(8,128)(2,1)S(1)}, bf16[256,1024]{1,0:T(8,128)(2,1)S(1)}, u32[]{:S(2)}, u32[]{:S(2)}) collective-permute-start(bf16[256,1024]{1,0:T(8,128)(2,1)S(1)} %get-tuple-element.105), channel_id=1, source_target_pairs={{0,2},{1,3},{2,0},{3,1},{4,6},{5,7},{6,4},{7,5},{8,10},{9,11},{10,... | collective-permute-start | bytes 1572872 | tf_op jit(solution)/shard_map/ppermute | solution.py:358
  85.0 4.8 %collective-permute-start.18 = (bf16[208,256]{1,0:T(8,128)(2,1)S(1)}, bf16[208,256]{1,0:T(8,128)(2,1)S(1)}, u32[]{:S(2)}, u32[]{:S(2)}) collective-permute-start(bf16[208,256]{1,0:T(8,128)(2,1)S(1)} %get-tuple-element.106.refs_8_.refs_9_), channel_id=1, source_target_pairs={{0,8},{8,0},{16,24},{24,16},{1,9},{9,1},{17,25},{25,17},{2,10},{10... | collective-permute-start | bytes 319496 | tf_op jit(solution)/shard_map/ppermute | solution.py:361
  85.4 5.7 %collective-permute-start.19 = (bf16[208,256]{1,0:T(8,128)(2,1)S(1)}, bf16[208,256]{1,0:T(8,128)(2,1)S(1)}, u32[]{:S(2)}, u32[]{:S(2)}) collective-permute-start(bf16[208,256]{1,0:T(8,128)(2,1)S(1)} %get-tuple-element.106.refs_8_.refs_9_), channel_id=1, source_target_pairs={{0,16},{8,24},{16,0},{24,8},{1,17},{9,25},{17,1},{25,9},{2,18},{10... | collective-permute-start | bytes 319496 | tf_op jit(solution)/shard_map/ppermute | solution.py:361
  87.1 5.6 %collective-permute-start.20 = (bf16[208,256]{1,0:T(8,128)(2,1)S(1)}, bf16[208,256]{1,0:T(8,128)(2,1)S(1)}, u32[]{:S(2)}, u32[]{:S(2)}) collective-permute-start(bf16[208,256]{1,0:T(8,128)(2,1)S(1)} %get-tuple-element.106.refs_8_.refs_9_), channel_id=1, source_target_pairs={{0,24},{8,16},{16,8},{24,0},{1,25},{9,17},{17,9},{25,1},{2,26},{10... | collective-permute-start | bytes 319496 | tf_op jit(solution)/shard_map/ppermute | solution.py:361
  94.4 6.7 %collective-permute-start.21 = (bf16[1024,256]{1,0:T(8,128)(2,1)S(1)}, bf16[1024,256]{1,0:T(8,128)(2,1)S(1)}, u32[]{:S(2)}, u32[]{:S(2)}) collective-permute-start(bf16[1024,256]{1,0:T(8,128)(2,1)S(1)} %weights_other_core.5), channel_id=1, source_target_pairs={{0,1},{1,0},{2,3},{3,2},{4,5},{5,4},{6,7},{7,6},{8,9},{9,8},{10,11... | collective-permute-start | bytes 1572872 | tf_op jit(solution)/shard_map/ppermute | solution.py:358
  101.9 11.5 %collective-permute-start.22 = (bf16[512,256]{1,0:T(8,128)(2,1)S(1)}, bf16[512,256]{1,0:T(8,128)(2,1)S(1)}, u32[]{:S(2)}, u32[]{:S(2)}) collective-permute-start(bf16[512,256]{1,0:T(8,128)(2,1)S(1)} %get-tuple-element.112), channel_id=1, source_target_pairs={{0,2},{1,3},{2,0},{3,1},{4,6},{5,7},{6,4},{7,5},{8,10},{9,11},{10,... | collective-permute-start | bytes 786440 | tf_op jit(solution)/shard_map/ppermute | solution.py:358
  101.9 13.1 %collective-permute-start.17 = (bf16[128,1024]{1,0:T(8,128)(2,1)S(1)}, bf16[128,1024]{1,0:T(8,128)(2,1)S(1)}, u32[]{:S(2)}, u32[]{:S(2)}) collective-permute-start(bf16[128,1024]{1,0:T(8,128)(2,1)S(1)} %fusion.3), channel_id=1, source_target_pairs={{0,4},{1,5},{2,6},{3,7},{4,0},{5,1},{6,2},{7,3},{8,12},{9,13},{10,... | collective-permute-start | bytes 786440 | tf_op jit(solution)/shard_map/ppermute | solution.py:358
  113.4 7.4 %collective-permute-start.23 = (bf16[256,256]{1,0:T(8,128)(2,1)S(1)}, bf16[256,256]{1,0:T(8,128)(2,1)S(1)}, u32[]{:S(2)}, u32[]{:S(2)}) collective-permute-start(bf16[256,256]{1,0:T(8,128)(2,1)S(1)} %fusion.5), channel_id=1, source_target_pairs={{0,4},{1,5},{2,6},{3,7},{4,0},{5,1},{6,2},{7,3},{8,12},{9,13},{10,... | collective-permute-start | bytes 393224 | tf_op jit(solution)/shard_map/ppermute | solution.py:358
  (5 other events, 18.0 us)
